TPU v7x, 128 devices: a whole 4x4x4 slice. The times are simulated.
128 devices in a mesh: rep: 32 (over z_hi, x, y), fsdp: 4 (over z_lo, core).
Axes of the slice: x: 4, y: 4, z: 4 (z_hi: 2, z_lo: 2; z = z_hi * 2 + z_lo), core: 2. Of those that a mesh axis runs over, the one named last changes fastest.
Arguments:
- grads: bfloat16 [32, 4, 256, 2, 8192], P('rep', 'fsdp'), may hold values from -6 to 6
- momentum: float32 [32, 256, 2, 8192], P('rep', 'fsdp'), may hold values from -6 to 6
Outputs:
- new_momentum: float32 [32, 256, 2, 8192], P('rep', 'fsdp')
- update: float32 [256, 2, 8192], P('fsdp')
All inputs are finite; a program needn't handle non-finite values.
Results may differ from a plain program's by a relative error of at most 0.0003.
Values sent between devices are 32-bit elements; how exact they have to be, the bound alone decides.
No kernel may reach another device: no remote copies, remote signals or barrier semaphores. Data moves between devices by JAX's collectives and lax.ppermute only.
A program may use at most 128 MiB of HBM per device.

v0:
```python
import math

import jax
import jax.numpy as jnp
from jax import lax
from jax.sharding import PartitionSpec as P

SPAN = 64
BAND = 16


momentum_decay = 0.9


def cosine_basis():
    frequency = jnp.arange(BAND, dtype=jnp.int32)
    positions = jnp.arange(SPAN, dtype=jnp.int32)
    angles = (frequency[:, None] * (2 * positions[None, :] + 1)).astype(jnp.float32) * (
        math.pi / (2 * SPAN)
    )
    factors = jnp.where(frequency == 0, math.sqrt(1.0 / SPAN), math.sqrt(2.0 / SPAN)).astype(
        jnp.float32
    )
    return factors[:, None] * jnp.cos(angles)


def forward_band(field, basis):
    block_count = field.shape[0] // SPAN
    mat_count = field.shape[1]
    column_blocks = field.shape[2] // SPAN
    blocked = field.reshape(block_count, SPAN, mat_count, field.shape[2])
    low_rows = jnp.einsum("pn,anmd->apmd", basis, blocked, precision=lax.Precision.HIGHEST)
    pieces = low_rows.reshape(block_count, BAND, mat_count, column_blocks, SPAN)
    return jnp.einsum("apmjc,qc->apmqj", pieces, basis, precision=lax.Precision.HIGHEST)


def inverse_band(band, basis):
    block_count = band.shape[0]
    mat_count = band.shape[2]
    column_blocks = band.shape[4]
    wide = jnp.einsum("apmqj,qc->apmjc", band, basis, precision=lax.Precision.HIGHEST)
    merged = wide.reshape(block_count, BAND, mat_count, column_blocks * SPAN)
    full = jnp.einsum("pn,apmd->anmd", basis, merged, precision=lax.Precision.HIGHEST)
    return full.reshape(block_count * SPAN, mat_count, column_blocks * SPAN)


def advance(part_grads, part_moment, basis):
    rep_count = lax.axis_size("rep")
    summed = lax.psum_scatter(
        part_grads.astype(jnp.float32), "fsdp", scatter_dimension=0, tiled=True
    )
    moment = momentum_decay * part_moment + summed
    own_band = forward_band(moment, basis)
    band_total = lax.psum(own_band, "rep")
    mean_band = band_total / rep_count
    return (moment - inverse_band(own_band, basis), inverse_band(mean_band, basis))


def per_device(grads, momentum):
    basis = cosine_basis()
    local_grads = grads[0, 0]
    local_moment = momentum[0]
    mat_count = local_moment.shape[1]
    results = [
        advance(local_grads[:, matrix : matrix + 1], local_moment[:, matrix : matrix + 1], basis)
        for matrix in range(mat_count)
    ]
    new_moment = jnp.concatenate([result[0] for result in results], axis=1)
    update = jnp.concatenate([result[1] for result in results], axis=1)
    return (new_moment[None], update)


def solution(mesh):
    in_specs = (P("rep", "fsdp", None, None, None), P("rep", "fsdp", None, None))
    out_specs = (P("rep", "fsdp", None, None), P("fsdp", None, None))
    return jax.shard_map(
        per_device, mesh=mesh, in_specs=in_specs, out_specs=out_specs, check_vma=False
    )
```

profile of v0, /device:TPU:0, one launch (start us, length us, event | category | flops | bytes accessed | tf_op | source)
XLA Modules:
  0.0 579.0 jit_solution(8103895965288953746)
XLA Ops:
  7.2 12.5 %copy.28 = bf16[1,1,256,2,8192]{4,2,3,1,0:T(8,128)(2,1)} copy(bf16[1,1,256,2,8192]{4,3,2,1,0:T(2,128)(2,1)} %param.2) | data formatting | bytes 16777216 | tf_op args[0]
  19.7 11.4 %slice_convert_fusion.1 = (f32[256,1,8192]{2,0,1:T(8,128)}, f32[256,1,8192]{2,0,1:T(8,128)}) fusion(bf16[256,2,8192]{2,0,1:T(8,128)(2,1)} %bitcast.101), kind=kLoop, calls=%fused_computation.10 | loop fusion | flops 4194304 | bytes 25165824 | tf_op jit(solution)/shard_map/convert_element_type | solution.py:50
  31.2 0.5 reduce-scatter.3.cloned.1.call-start
  31.9 6.6 %copy.29 = f32[1,64,2,8192]{3,1,2,0:T(8,128)} copy(f32[1,64,2,8192]{3,2,1,0:T(2,128)} %param.3) | data formatting | bytes 8388608 | tf_op args[1]
  38.6 74.3 %reduce-scatter.5.cloned.1.call-done = f32[64,1,8192]{2,0,1:T(8,128)} async-done(((f32[256,1,8192]{2,0,1:T(8,128)}), f32[64,1,8192]{2,0,1:T(8,128)}) %reduce-scatter.5.cloned.1.call-update) | async-done | bytes 2097168 | tf_op jit(solution)/shard_map/reduce_scatter | solution.py:49
  112.9 3.6 convolution_bitcast_fusion.4
  116.9 1.0 fusion.23
  117.9 1.8 fusion.8
  119.7 1.2 reshape.104
  120.9 74.6 %reduce-scatter.3.cloned.1.call-done = f32[64,1,8192]{2,0,1:T(8,128)} async-done(((f32[256,1,8192]{2,0,1:T(8,128)}), f32[64,1,8192]{2,0,1:T(8,128)}) %reduce-scatter.3.cloned.1.call-update) | async-done | bytes 2097168 | tf_op jit(solution)/shard_map/reduce_scatter | solution.py:49
  195.5 3.6 convolution_bitcast_fusion.5
  199.5 1.0 fusion.26
  200.5 1.8 fusion.10
  202.5 1.2 reshape.99
  203.8 4.1 fusion.1
  207.9 2.2 fusion
  210.5 5.2 copy.18
  215.8 339.7 %all-reduce.3.cloned.1.call-done = (f32[1,16,1,16,128]{4,3,1,2,0:T(8,128)}, f32[1,16,1,16,128]{4,3,1,2,0:T(8,128)}) async-done(((f32[1,16,1,16,128]{4,3,1,2,0:T(8,128)}, f32[1,16,1,16,128]{4,3,1,2,0:T(8,128)}), (f32[1,16,1,16,128]{4,3,1,2,0:T(8,128)}, f32[1,16,1,16,128]{4,3,1,2,0:T(8,128)})) %all-reduce.3.cloned.1.call-update) | async-done | bytes 262160 | tf_op jit(solution)/shard_map/psum | solution.py:54
  555.4 2.7 fusion.12
  558.5 1.9 convolution_bitcast_fusion
  560.5 2.0 fusion.14
  562.5 1.2 reshape.107
  563.6 2.9 convolution_bitcast_fusion.1
  567.0 5.2 copy.19
  (26 shorter events, 2.5 us)
Async XLA Ops:
  7.2 105.7 %reduce-scatter.5.cloned.1.call-start = ((), (), s32[]{:S(2)}) async-start(), calls=%async_computation.3 | async-start | bytes 10485760 | tf_op jit(solution)/shard_map/reduce_scatter | solution.py:49
  31.2 164.3 %reduce-scatter.3.cloned.1.call-start = ((), (), s32[]{:S(2)}) async-start(), calls=%async_computation.2 | async-start | bytes 10485760 | tf_op jit(solution)/shard_map/reduce_scatter | solution.py:49
  117.9 81.2 %copy-start.4 = (f32[16,16,128]{2,0,1:T(8,128)}, f32[16,16,128]{2,0,1:T(8,128)S(1)}, u32[]{:S(2)}) copy-start(f32[16,16,128]{2,0,1:T(8,128)S(1)} %fusion.23) | copy-start | bytes 393220
  199.5 4.3 copy-start.1
  200.5 3.2 copy-start.5
  202.3 353.1 %all-reduce.3.cloned.1.call-start = ((), (), s32[]{:S(2)}) async-start(), calls=%async_computation.4 | async-start | bytes 524288 | tf_op jit(solution)/shard_map/psum | solution.py:54
  203.7 4.1 copy-start
  203.8 4.1 copy-start.2
  203.8 4.1 copy-start.3
  558.2 2.3 copy-start.6
Sparse Core Ops, SparseCore 0:
  31.3 81.5 reduce-scatter.4
  115.3 80.0 reduce-scatter.2
  205.7 349.7 all-reduce.2
where the time goes:
time: 585 us; the launch traced here: 579 us
  waiting for transfers between devices  489 us (84%)
  local copies, waits for them, and re-layouts  34.3 us (6%)
  matrix products  28.7 us (5%)
  between operations  14.2 us (2%)
  other arithmetic  12.2 us (2%)
    psum x1, waiting for transfers between devices, advance(): band_total = lax.psum(own_band, 'rep')  340 us
    reduce_scatter x2, waiting for transfers between devices, advance(): lax.psum_scatter(part_grads.astype(jnp.float32), 'fsdp', scatter_dimensio...  149 us
    unnamed x18, local copies, waits for them, and re-layouts  29.7 us
  transfers between devices with their start and end apart: 3, of which 3 were waited for; matrix products, arithmetic and copies ran while one was open for 5% of the time, Pallas kernels for 0%

commit v1 on v0

v1 whole, which is shorter than its diff:
```python
import functools
import math

import jax
import jax.numpy as jnp
import ml_dtypes
import numpy as np
from jax import lax
from jax.experimental import pallas as pl
from jax.experimental.pallas import tpu as pltpu
from jax.sharding import PartitionSpec as P

SPAN = 64
BAND = 16
LANES = 128
GROUP = 8
QUANTUM = 2 * GROUP
DECAY = 0.9
HIGH = (SPAN - BAND) * GROUP
LOW = BAND * GROUP
QUARTER = LOW // 4
PAYLOAD = 2 * HIGH + 3 * 2 * QUARTER
VMEM = 40 * 1024 * 1024


def dct(order):
    q = np.arange(order)[:, None]
    n = np.arange(order)[None, :]
    scale = np.where(q == 0, math.sqrt(1.0 / order), math.sqrt(2.0 / order))
    return scale * np.cos(math.pi * (2 * n + 1) * q / (2 * order))


def split_constant(a):
    high = a.astype(ml_dtypes.bfloat16)
    return high, (a - high.astype(np.float64)).astype(ml_dtypes.bfloat16)


def constants():
    t = dct(SPAN)
    rows = np.kron(t, np.eye(GROUP))
    lanes = np.kron(np.eye(8), t.T)
    coef = np.arange(512) % SPAN
    order = np.concatenate([np.flatnonzero(coef >= BAND), np.flatnonzero(coef < BAND)])
    mats = split_constant(rows) + split_constant(lanes[:, order])
    return [jnp.asarray(a) for a in mats]


def split(x):
    high = x.astype(jnp.bfloat16)
    return high, (x - high.astype(jnp.float32)).astype(jnp.bfloat16)


def dot3(a, b, dims):
    def one(u, v):
        return lax.dot_general(u, v, ((dims[:1], dims[1:]), ((), ())), preferred_element_type=jnp.float32)
    return one(a[0], b[0]) + (one(a[0], b[1]) + one(a[1], b[0]))


def to_wide(x):
    parts = [x[:, g * GROUP : (g + 1) * GROUP, :].reshape(SPAN * GROUP, LANES) for g in range(2)]
    return jnp.concatenate(parts, axis=1)


def store_wide(ref, x, base=None):
    for g in range(2):
        part = x[:, g * LANES : (g + 1) * LANES].reshape(SPAN, GROUP, LANES)
        at = (slice(None), slice(g * GROUP, (g + 1) * GROUP), slice(None))
        ref[at] = part if base is None else base[at] + part


def quarters(x):
    groups = []
    for g in range(2):
        lane = slice(g * LANES, (g + 1) * LANES)
        groups.append(jnp.concatenate([x[i * QUARTER : (i + 1) * QUARTER, lane] for i in range(4)], axis=1))
    return jnp.concatenate(groups, axis=0)


def unquarters(x):
    groups = []
    for g in range(2):
        row = slice(g * QUARTER, (g + 1) * QUARTER)
        groups.append(jnp.concatenate([x[row, i * LANES : (i + 1) * LANES] for i in range(4)], axis=0))
    return jnp.concatenate(groups, axis=1)


def cast_kernel(place, g_ref, out_ref):
    out_ref[...] = g_ref[...].astype(jnp.float32)


def encode(g_ref, r_ref, th, tl, wh, wl, pay_ref, band_ref):
    x = to_wide(g_ref[...].astype(jnp.float32) + r_ref[...])
    c = dot3((th[...], tl[...]), split(x), (1, 0))
    w = dot3(split(quarters(c[:LOW])), (wh[...], wl[...]), (1, 0))
    pay_ref[0:HIGH, :] = c[LOW:, :LANES]
    pay_ref[HIGH : 2 * HIGH, :] = c[LOW:, LANES:]
    for i in range(3):
        at = 2 * HIGH + i * 2 * QUARTER
        pay_ref[at : at + 2 * QUARTER, :] = w[:, i * LANES : (i + 1) * LANES]
    band_ref[...] = w[:, 3 * LANES :].reshape(band_ref.shape)


def encode_kernel(n, place, g_ref, r_ref, th, tl, wh, wl, *outs):
    step = pl.program_id(0)
    for k in range(n):
        @pl.when(step == k)
        def _(k=k):
            encode(g_ref, r_ref, th, tl, wh, wl, outs[k], outs[n])


def project(band, th, tl, wh, wl):
    low = dot3(split(band), (wh[:, 3 * LANES :], wl[:, 3 * LANES :]), (1, 1))
    return dot3((th[:LOW], tl[:LOW]), split(unquarters(low)), (0, 0))


def base_kernel(place, m_ref, g_ref, r_ref, th, tl, wh, wl, out_ref, band_ref):
    x = to_wide(DECAY * m_ref[...] + (g_ref[...].astype(jnp.float32) + r_ref[...]))
    c = dot3((th[:LOW], tl[:LOW]), split(x), (1, 0))
    band = dot3(split(quarters(c)), (wh[:, 3 * LANES :], wl[:, 3 * LANES :]), (1, 0))
    band_ref[...] = band.reshape(band_ref.shape)
    store_wide(out_ref, x - project(band, th, tl, wh, wl))


def decode_kernel(pay_ref, th, tl, wh, wl, base_ref, out_ref):
    at = 2 * HIGH
    w = jnp.concatenate([pay_ref[at + i * 2 * QUARTER : at + (i + 1) * 2 * QUARTER, :] for i in range(3)], axis=1)
    low = dot3(split(w), (wh[:, : 3 * LANES], wl[:, : 3 * LANES]), (1, 1))
    high = jnp.concatenate([pay_ref[:HIGH, :], pay_ref[HIGH : 2 * HIGH, :]], axis=1)
    x = jnp.concatenate([unquarters(low), high], axis=0)
    store_wide(out_ref, dot3((th[...], tl[...]), split(x), (0, 0)), base_ref)


def update_kernel(scale, band_ref, th, tl, wh, wl, out_ref):
    band = band_ref[...].reshape(2 * QUARTER, LANES) * scale
    store_wide(out_ref, project(band, th, tl, wh, wl))


def params():
    return pltpu.CompilerParams(vmem_limit_bytes=VMEM)


def whole(shape):
    return pl.BlockSpec(shape, lambda *_: (0,) * len(shape))


MATRICES = [whole((512, 512))] * 4


def cast(place, g, first, count, slot):
    return pl.pallas_call(
        cast_kernel,
        grid_spec=pltpu.PrefetchScalarGridSpec(
            num_scalar_prefetch=1,
            grid=(count,),
            in_specs=[pl.BlockSpec((SPAN, QUANTUM, LANES), lambda i, p: (p[slot], first + i, 0))],
            out_specs=pl.BlockSpec((SPAN, QUANTUM, LANES), lambda i, p: (0, i, 0)),
        ),
        out_shape=jax.ShapeDtypeStruct((SPAN, count * QUANTUM, LANES), jnp.float32),
        compiler_params=params(),
    )(place, g)


def encoded(place, g, received, first, count, slot, mats):
    out = pl.pallas_call(
        functools.partial(encode_kernel, count),
        grid_spec=pltpu.PrefetchScalarGridSpec(
            num_scalar_prefetch=1,
            grid=(count,),
            in_specs=[
                pl.BlockSpec((SPAN, QUANTUM, LANES), lambda i, p: (p[slot], first + i, 0)),
                pl.BlockSpec((SPAN, QUANTUM, LANES), lambda i, p: (0, i, 0)),
            ]
            + MATRICES,
            out_specs=[whole((PAYLOAD, LANES))] * count
            + [pl.BlockSpec((2, QUARTER, LANES), lambda i, p: (i, 0, 0))],
        ),
        out_shape=[jax.ShapeDtypeStruct((PAYLOAD, LANES), jnp.float32)] * count
        + [jax.ShapeDtypeStruct((2 * count, QUARTER, LANES), jnp.float32)],
        compiler_params=params(),
    )(place, g, received, *mats)
    return out[:count], out[count]


def based(place, m, g, received, slot, mats):
    count = m.shape[1] // QUANTUM
    block = (SPAN, QUANTUM, LANES)
    return pl.pallas_call(
        base_kernel,
        grid_spec=pltpu.PrefetchScalarGridSpec(
            num_scalar_prefetch=1,
            grid=(count,),
            in_specs=[
                pl.BlockSpec(block, lambda i, p: (0, i, 0)),
                pl.BlockSpec(block, lambda i, p: (p[slot], i, 0)),
                pl.BlockSpec(block, lambda i, p: (0, i, 0)),
            ]
            + MATRICES,
            out_specs=[
                pl.BlockSpec(block, lambda i, p: (0, i, 0)),
                pl.BlockSpec((2, QUARTER, LANES), lambda i, p: (i, 0, 0)),
            ],
        ),
        out_shape=[
            jax.ShapeDtypeStruct(m.shape, jnp.float32),
            jax.ShapeDtypeStruct((2 * count, QUARTER, LANES), jnp.float32),
        ],
        compiler_params=params(),
    )(place, m, g, received, *mats)


def decoded(payload, base, at, mats):
    block = pl.BlockSpec((SPAN, QUANTUM, LANES), lambda i: (0, at, 0))
    return pl.pallas_call(
        decode_kernel,
        grid=(1,),
        in_specs=[whole((PAYLOAD, LANES))] + MATRICES + [block],
        out_specs=block,
        out_shape=jax.ShapeDtypeStruct(base.shape, jnp.float32),
        input_output_aliases={5: 0},
        compiler_params=params(),
    )(payload, *mats, base)


def updated(band, scale, shape, mats):
    count = shape[1] // QUANTUM
    return pl.pallas_call(
        functools.partial(update_kernel, scale),
        grid=(count,),
        in_specs=[pl.BlockSpec((2, QUARTER, LANES), lambda i: (i, 0, 0))] + MATRICES,
        out_specs=pl.BlockSpec((SPAN, QUANTUM, LANES), lambda i: (0, i, 0)),
        out_shape=jax.ShapeDtypeStruct(shape, jnp.float32),
        compiler_params=params(),
    )(band, *mats)


def tiles(x):
    rows, mats, width = x.shape
    x = x.reshape(rows, mats, width // LANES, LANES).transpose(0, 2, 1, 3)
    return x.reshape(rows, mats * width // LANES, LANES)


def untiles(x, mats):
    rows, places, _ = x.shape
    x = x.reshape(rows, places // mats, mats, LANES).transpose(0, 2, 1, 3)
    return x.reshape(rows, mats, places // mats * LANES)


def tie(*arrays):
    return lax.optimization_barrier(arrays)


def per_device(grads, momentum):
    rep_count = lax.axis_size("rep")
    mat_count = grads.shape[3]
    mats = constants()
    g = tiles(grads[0, 0])
    m = tiles(momentum[0])
    count = m.shape[1] // QUANTUM
    member = lax.axis_index("fsdp")
    place = jnp.stack([member, member ^ 1, member ^ 2, member ^ 3]).astype(jnp.int32)
    over_core = [(f, f ^ 1) for f in range(4)]
    over_z = [(f, f ^ 2) for f in range(4)]

    def core(x):
        return lax.ppermute(x, "fsdp", over_core)

    def link(x):
        return lax.ppermute(x, "fsdp", over_z)

    cells, later = tie(cast(place, g, 0, 1, 3), place)
    first = core(cells)
    cells, later = tie(cast(later, g, 1, count - 1, 3), later)
    rest = core(cells)
    mine = core(cast(later, g, 0, count, 1))
    pay0, band0 = encoded(place, g, first, 0, 1, 2, mats)
    pays, bands = encoded(place, g, rest, 1, count - 1, 2, mats)
    payloads = list(pay0) + list(pays)
    base, own_band = based(place, m, g, mine, 0, mats)
    other_band = jnp.concatenate([band0, bands], axis=0)

    groups = [[h * 16 + i for i in range(16)] for h in range(rep_count // 16)]
    both = jnp.stack([own_band, other_band], axis=1)
    met = lax.all_to_all(both, "rep", 0, 0, axis_index_groups=groups, tiled=True)
    part = jnp.sum(met, axis=0)
    names = ("rep", "fsdp")
    everyone = range(rep_count * 4)
    from_z = lax.ppermute(part[1], names, [(d, d ^ 2) for d in everyone])
    from_far = lax.ppermute(part[0], names, [(d, d ^ 64) for d in everyone])
    from_wrap = lax.ppermute(part[1], names, [(d, d ^ 66) for d in everyone])
    total = (part[0] + from_z) + (from_far + from_wrap)
    spread = jnp.broadcast_to(total[None], (16,) + total.shape)
    band_total = lax.all_to_all(spread, "rep", 0, 0, axis_index_groups=groups, tiled=True)
    update = updated(band_total, 1.0 / rep_count, m.shape, mats)

    arrived = []
    for k in range(count):
        if k >= 2:
            payloads[k], arrived[k - 2] = tie(payloads[k], arrived[k - 2])
        arrived.append(link(payloads[k]))
    out = base
    for k in range(count):
        out = decoded(arrived[k], out, k, mats)
    return (untiles(out, mat_count)[None], untiles(update, mat_count))


def solution(mesh):
    in_specs = (P("rep", "fsdp", None, None, None), P("rep", "fsdp", None, None))
    out_specs = (P("rep", "fsdp", None, None), P("fsdp", None, None))
    return jax.shard_map(
        per_device, mesh=mesh, in_specs=in_specs, out_specs=out_specs, check_vma=False
    )
```

time: 585 us -> 153 us (0.26)
  waiting for transfers between devices: 489 us -> 55 us
  Pallas kernels: 0 us -> 62.6 us
  local copies, waits for them, and re-layouts: 34.3 us -> 4.99 us
  matrix products: 28.7 us -> 0 us
  starting transfers between devices: 0.76 us -> 27 us
  between operations: 14.2 us -> 0.77 us
  other arithmetic: 12.2 us -> 1.22 us
    psum x1 -> x0, waiting for transfers between devices: 340 us -> none  [advance(): band_total = lax.psum(own_band, 'rep')]
    reduce_scatter x2 -> x0, waiting for transfers between devices: 149 us -> none  [advance(): lax.psum_scatter(part_grads.astype(jnp.float32), 'fsdp', scatter_dimensio...]
    pallas_call x0 -> x15, Pallas kernels: none -> 62.6 us  [the longest x8 24 us: decoded(): pl.pallas_call(decode_kernel, grid=(1,), in_specs=[whole((PAYLOAD, LANES)...]
    ppermute x0 -> x14, waiting for transfers between devices: none -> 46.9 us  [the longest x8 25.6 us: link(): return lax.ppermute(x, 'fsdp', over_z)]
    dot_general x12 -> x0, matrix products: 28.7 us -> none  [the longest x4 11.1 us: inverse_band(): jnp.einsum('pn,apmd->anmd', basis, merged, precision=lax.Precision.HIGHEST)]
    unnamed x18 -> x22, local copies, waits for them, and re-layouts: 29.7 us -> 3.42 us
    all_to_all x0 -> x2, starting transfers between devices: none -> 14.1 us  [the longest x1 7.22 us: per_device(): lax.all_to_all(both, 'rep', 0, 0, axis_index_groups=groups, tiled=True)]
    ppermute x0 -> x14, starting transfers between devices: none -> 12.9 us  [the longest x8 8.53 us: link(): return lax.ppermute(x, 'fsdp', over_z)]
  transfers between devices with their start and end apart: 3 -> 16, of which waited for: 3 -> 6; matrix products, arithmetic and copies ran while one was open for 5% -> 2% of each run, Pallas kernels for 0% -> 36%
where the time goes in v1:
time: 153 us; the launch traced here: 152 us
  Pallas kernels  62.6 us (41%)
  waiting for transfers between devices  55 us (36%)
  starting transfers between devices  27 us (18%)
  local copies, waits for them, and re-layouts  4.99 us (3%)
    ppermute x8, waiting for transfers between devices, link(): return lax.ppermute(x, 'fsdp', over_z)  25.6 us
    pallas_call x8, Pallas kernels, decoded(): pl.pallas_call(decode_kernel, grid=(1,), in_specs=[whole((PAYLOAD, LANES)...  24 us
    ppermute x1, waiting for transfers between devices, per_device(): from_far = lax.ppermute(part[0], names, [(d, d ^ 64) for d in everyone])  15.7 us
    pallas_call x2, Pallas kernels, encoded(): pl.pallas_call(functools.partial(encode_kernel, count), grid_spec=pltpu.P...  13 us
    pallas_call x1, Pallas kernels, based(): pl.pallas_call(base_kernel, grid_spec=pltpu.PrefetchScalarGridSpec(num_sc...  13 us
    ppermute x8, starting transfers between devices, link(): return lax.ppermute(x, 'fsdp', over_z)  8.53 us
    all_to_all x1, waiting for transfers between devices, per_device(): lax.all_to_all(both, 'rep', 0, 0, axis_index_groups=groups, tiled=True)  8.03 us
    all_to_all x1, starting transfers between devices, per_device(): lax.all_to_all(both, 'rep', 0, 0, axis_index_groups=groups, tiled=True)  7.22 us
  transfers between devices with their start and end apart: 16, of which 6 were waited for; matrix products, arithmetic and copies ran while one was open for 2% of the time, Pallas kernels for 36%

profile of v1, /device:TPU:0, one launch (start us, length us, event | category | flops | bytes accessed | tf_op | source)
XLA Modules:
  0.0 151.5 jit_solution(2306013820605737013)
XLA Ops:
  0.7 3.4 %copy-done = bf16[1,1,256,2,8192]{4,3,2,1,0:T(2,128)(2,1)S(1)} copy-done((bf16[1,1,256,2,8192]{4,3,2,1,0:T(2,128)(2,1)S(1)}, bf16[1,1,256,2,8192]{4,3,2,1,0:T(2,128)(2,1)}, u32[]{:S(2)}) %copy-start) | copy-done | bytes 8388632
  4.7 4.0 %shard_map.78 = f32[64,112,128]{2,1,0:T(8,128)} custom-call(s32[4]{0:T(128)S(1)} %pad_add_fusion.place, bf16[256,128,128]{2,1,0:T(8,128)(2,1)S(1)} %bitcast.36), custom_call_target="tpu_custom_call" | custom-call | tf_op jit(solution)/shard_map/pallas_call | solution.py:150
  11.1 5.7 %collective-permute-done.5.r_ref = f32[64,16,128]{2,1,0:T(8,128)S(1)} collective-permute-done((f32[64,16,128]{2,1,0:T(8,128)S(1)}, f32[64,16,128]{2,1,0:T(8,128)S(1)}, u32[]{:S(2)}, u32[]{:S(2)}) %collective-permute-start.5) | collective-permute-done | bytes 524320 | tf_op jit(solution)/shard_map/ppermute | solution.py:265
  16.8 1.7 %shard_map.80 = (f32[960,128]{1,0:T(8,128)S(1)}, f32[2,32,128]{2,1,0:T(8,128)S(1)}) custom-call(s32[4]{0:T(128)S(1)} %pad_add_fusion.place, bf16[256,128,128]{2,1,0:T(8,128)(2,1)S(1)} %bitcast.38, f32[64,16,128]{2,1,0:T(8,128)S(1)} %collective-permute-done.5.r_ref, bf16[512,512]{1,0:T(8,128)(2,1)S(1)} %copy-done.4, bf16[512,512]{1,0:T(8,128)(2,1)S(1)} %copy-done.3, ...), custom_call_target="tpu_custom_call" | custom-call | tf_op jit(solution)/shard_map/pallas_call | solution.py:164
  18.5 2.1 %collective-permute-start.6 = (f32[960,128]{1,0:T(8,128)S(1)}, f32[960,128]{1,0:T(8,128)S(1)}, u32[]{:S(2)}, u32[]{:S(2)}) collective-permute-start(f32[960,128]{1,0:T(8,128)S(1)} %get-tuple-element.43), channel_id=1, source_target_pairs={{0,2},{1,3},{2,0},{3,1},{4,6},{5,7},{6,4},{7,5},{8,10},{9,11},{10,... | collective-permute-start | bytes 1474568 | tf_op jit(solution)/shard_map/ppermute | solution.py:268
  20.6 11.3 %shard_map.79 = (f32[960,128]{1,0:T(8,128)S(1)}, f32[960,128]{1,0:T(8,128)S(1)}, f32[960,128]{1,0:T(8,128)}, f32[960,128]{1,0:T(8,128)}, f32[960,128]{1,0:T(8,12...) custom-call(s32[4]{0:T(128)S(1)} %pad_add_fusion.place, ...), custom_call_target="tpu_custom_call" | custom-call | tf_op jit(solution)/shard_map/pallas_call | solution.py:164
  34.0 12.1 %collective-permute-done.1.pay_ref = f32[960,128]{1,0:T(8,128)S(1)} collective-permute-done((f32[960,128]{1,0:T(8,128)S(1)}, f32[960,128]{1,0:T(8,128)S(1)}, u32[]{:S(2)}, u32[]{:S(2)}) %collective-permute-start.1) | collective-permute-done | bytes 491552 | tf_op jit(solution)/shard_map/ppermute | solution.py:268
  46.5 10.2 %collective-permute-done.7.pay_ref = f32[960,128]{1,0:T(8,128)S(1)} collective-permute-done((f32[960,128]{1,0:T(8,128)S(1)}, f32[960,128]{1,0:T(8,128)S(1)}, u32[]{:S(2)}, u32[]{:S(2)}) %collective-permute-start.7) | collective-permute-done | bytes 491552 | tf_op jit(solution)/shard_map/ppermute | solution.py:268
  57.0 13.0 %shard_map.82 = (f32[64,128,128]{2,1,0:T(8,128)}, f32[16,32,128]{2,1,0:T(8,128)S(1)}) custom-call(s32[4]{0:T(128)S(1)} %pad_add_fusion.place, f32[64,128,128]{2,1,0:T(8,128)S(1)} %bitcast.39, bf16[256,128,128]{2,1,0:T(8,128)(2,1)} %bitcast.34, f32[64,128,128]{2,1,0:T(8,128)} %collective-permute-done.10.r_ref, bf16[512,512]{1,0:T(8,128)(2,1)S(1)} %copy-done.4, ...), custom_call_target="tpu_custom_call" | custom-call | tf_op jit(solution)/shard_map/pallas_call | solution.py:187
  70.9 7.2 %all-to-all-start = ((f32[16,2,32,128]{3,2,1,0:T(8,128)}), f32[16,2,32,128]{3,2,1,0:T(8,128)}, u32[]{:S(2)}, u32[]{:S(2)}) async-start(f32[16,2,32,128]{3,2,1,0:T(8,128)} %copy.23), calls=%async_computation | async-start | bytes 1048576 | tf_op jit(solution)/shard_map/all_to_all | solution.py:283
  80.3 8.0 %all-to-all-done = f32[16,2,32,128]{3,2,1,0:T(8,128)} async-done(((f32[16,2,32,128]{3,2,1,0:T(8,128)}), f32[16,2,32,128]{3,2,1,0:T(8,128)}, u32[]{:S(2)}, u32[]{:S(2)}) %all-to-all-start) | async-done | bytes 524320 | tf_op jit(solution)/shard_map/all_to_all | solution.py:283
  89.4 3.3 %collective-permute-done.3.pay_ref = f32[960,128]{1,0:T(8,128)} collective-permute-done((f32[960,128]{1,0:T(8,128)}, f32[960,128]{1,0:T(8,128)}, u32[]{:S(2)}, u32[]{:S(2)}) %collective-permute-start.3) | collective-permute-done | bytes 491552 | tf_op jit(solution)/shard_map/ppermute | solution.py:268
  94.3 3.6 %collective-permute-start.12 = (f32[32,128]{1,0:T(8,128)S(1)}, f32[32,128]{1,0:T(8,128)S(1)}, u32[]{:S(2)}, u32[]{:S(2)}) collective-permute-start(f32[32,128]{1,0:T(8,128)S(1)} %get-tuple-element.59), channel_id=1, source_target_pairs={{0,64},{1,65},{2,66},{3,67},{4,68},{5,69},{6,70},{7,71},{8,72},{9,... | collective-permute-start | bytes 49160 | tf_op jit(solution)/shard_map/ppermute | solution.py:288
  97.9 15.7 %collective-permute-done.12 = f32[32,128]{1,0:T(8,128)S(1)} collective-permute-done((f32[32,128]{1,0:T(8,128)S(1)}, f32[32,128]{1,0:T(8,128)S(1)}, u32[]{:S(2)}, u32[]{:S(2)}) %collective-permute-start.12) | collective-permute-done | bytes 16416 | tf_op jit(solution)/shard_map/ppermute | solution.py:288
  114.3 6.9 %all-to-all-start.1 = ((f32[16,32,128]{2,1,0:T(8,128)}), f32[16,32,128]{2,1,0:T(8,128)S(1)}, u32[]{:S(2)}, u32[]{:S(2)}) async-start(f32[16,32,128]{2,1,0:T(8,128)} %broadcast_in_dim.2), calls=%async_computation.1 | async-start | bytes 524288 | tf_op jit(solution)/shard_map/all_to_all | solution.py:292
  121.2 2.9 %shard_map.83.base_ref = f32[64,128,128]{2,1,0:T(8,128)} custom-call(f32[960,128]{1,0:T(8,128)S(1)} %collective-permute-done.6.pay_ref, bf16[512,512]{1,0:T(8,128)(2,1)S(1)} %copy-done.4, bf16[512,512]{1,0:T(8,128)(2,1)S(1)} %copy-done.3, bf16[512,512]{1,0:T(8,128)(2,1)S(1)} %copy-done.2, ...), custom_call_target="tpu_custom_call", output_to_operand_aliasing={{}: (5, {})} | custom-call | tf_op jit(solution)/shard_map/pallas_call | solution.py:213
  124.1 3.0 %shard_map.84.base_ref = f32[64,128,128]{2,1,0:T(8,128)} custom-call(f32[960,128]{1,0:T(8,128)S(1)} %collective-permute-done.1.pay_ref, bf16[512,512]{1,0:T(8,128)(2,1)S(1)} %copy-done.4, bf16[512,512]{1,0:T(8,128)(2,1)S(1)} %copy-done.3, bf16[512,512]{1,0:T(8,128)(2,1)S(1)} %copy-done.2, ...), custom_call_target="tpu_custom_call", output_to_operand_aliasing={{}: (5, {})} | custom-call | tf_op jit(solution)/shard_map/pallas_call | solution.py:213
  127.1 2.9 %shard_map.85.base_ref = f32[64,128,128]{2,1,0:T(8,128)} custom-call(f32[960,128]{1,0:T(8,128)S(1)} %copy-done.7, bf16[512,512]{1,0:T(8,128)(2,1)S(1)} %copy-done.4, bf16[512,512]{1,0:T(8,128)(2,1)S(1)} %copy-done.3, bf16[512,512]{1,0:T(8,128)(2,1)S(1)} %copy-done.2, bf16[512,512]{1,0:T(8,128)(2,1)S(1)} %copy-done.1, ...), custom_call_target="tpu_custom_call", output_to_operand_aliasing={{}: (5, {})} | custom-call | tf_op jit(solution)/shard_map/pallas_call | solution.py:213
  130.0 3.0 %shard_map.86.base_ref = f32[64,128,128]{2,1,0:T(8,128)} custom-call(f32[960,128]{1,0:T(8,128)} %collective-permute-done.2.pay_ref, bf16[512,512]{1,0:T(8,128)(2,1)S(1)} %copy-done.4, bf16[512,512]{1,0:T(8,128)(2,1)S(1)} %copy-done.3, bf16[512,512]{1,0:T(8,128)(2,1)S(1)} %copy-done.2, ...), custom_call_target="tpu_custom_call", output_to_operand_aliasing={{}: (5, {})} | custom-call | tf_op jit(solution)/shard_map/pallas_call | solution.py:213
  133.0 3.0 %shard_map.87.base_ref = f32[64,128,128]{2,1,0:T(8,128)} custom-call(f32[960,128]{1,0:T(8,128)} %collective-permute-done.8.pay_ref, bf16[512,512]{1,0:T(8,128)(2,1)S(1)} %copy-done.4, bf16[512,512]{1,0:T(8,128)(2,1)S(1)} %copy-done.3, bf16[512,512]{1,0:T(8,128)(2,1)S(1)} %copy-done.2, ...), custom_call_target="tpu_custom_call", output_to_operand_aliasing={{}: (5, {})} | custom-call | tf_op jit(solution)/shard_map/pallas_call | solution.py:213
  136.1 6.3 %shard_map.91 = f32[64,128,128]{2,1,0:T(8,128)} custom-call(f32[16,32,128]{2,1,0:T(8,128)S(1)} %all-to-all-done.1.band_ref, bf16[512,512]{1,0:T(8,128)(2,1)S(1)} %copy-done.4, bf16[512,512]{1,0:T(8,128)(2,1)S(1)} %copy-done.3, bf16[512,512]{1,0:T(8,128)(2,1)S(1)} %copy-done.2, bf16[512,512]{1,0:T(8,128)(2,1)S(1)} %copy-done.1), custom_call_target="tpu_custom_call" | custom-call | tf_op jit(solution)/shard_map/pallas_call | solution.py:226
  142.4 3.0 %shard_map.88.base_ref = f32[64,128,128]{2,1,0:T(8,128)} custom-call(f32[960,128]{1,0:T(8,128)} %collective-permute-done.3.pay_ref, bf16[512,512]{1,0:T(8,128)(2,1)S(1)} %copy-done.4, bf16[512,512]{1,0:T(8,128)(2,1)S(1)} %copy-done.3, bf16[512,512]{1,0:T(8,128)(2,1)S(1)} %copy-done.2, ...), custom_call_target="tpu_custom_call", output_to_operand_aliasing={{}: (5, {})} | custom-call | tf_op jit(solution)/shard_map/pallas_call | solution.py:213
  145.4 3.1 %shard_map.89.base_ref = f32[64,128,128]{2,1,0:T(8,128)} custom-call(f32[960,128]{1,0:T(8,128)} %collective-permute-done.9.pay_ref, bf16[512,512]{1,0:T(8,128)(2,1)S(1)} %copy-done.4, bf16[512,512]{1,0:T(8,128)(2,1)S(1)} %copy-done.3, bf16[512,512]{1,0:T(8,128)(2,1)S(1)} %copy-done.2, ...), custom_call_target="tpu_custom_call", output_to_operand_aliasing={{}: (5, {})} | custom-call | tf_op jit(solution)/shard_map/pallas_call | solution.py:213
  148.5 3.0 %shard_map.90 = f32[64,128,128]{2,1,0:T(8,128)} custom-call(f32[960,128]{1,0:T(8,128)} %collective-permute-done.4.pay_ref, bf16[512,512]{1,0:T(8,128)(2,1)S(1)} %copy-done.4, bf16[512,512]{1,0:T(8,128)(2,1)S(1)} %copy-done.3, bf16[512,512]{1,0:T(8,128)(2,1)S(1)} %copy-done.2, bf16[512,512]{1,0:T(8,128)(2,1)S(1)} %copy-done.1, ...), custom_call_target="tpu_custom_call", output_to_operand_aliasing={{}: (5, {})} | custom-call | tf_op jit(solution)/shard_map/pallas_call | solution.py:213
  (53 shorter events, 12.2 us)
Async XLA Ops:
  8.8 8.0 %copy-start.2 = (bf16[512,512]{1,0:T(8,128)(2,1)S(1)}, bf16[512,512]{1,0:T(8,128)(2,1)}, u32[]{:S(2)}) copy-start(bf16[512,512]{1,0:T(8,128)(2,1)} %constant.22.clone.wh) | copy-start | bytes 1572868
  8.8 8.0 %copy-start.3 = (bf16[512,512]{1,0:T(8,128)(2,1)S(1)}, bf16[512,512]{1,0:T(8,128)(2,1)}, u32[]{:S(2)}) copy-start(bf16[512,512]{1,0:T(8,128)(2,1)} %constant.21.clone.tl) | copy-start | bytes 1572868
  8.8 8.0 %copy-start.4 = (bf16[512,512]{1,0:T(8,128)(2,1)S(1)}, bf16[512,512]{1,0:T(8,128)(2,1)}, u32[]{:S(2)}) copy-start(bf16[512,512]{1,0:T(8,128)(2,1)} %constant.20.clone.th) | copy-start | bytes 1572868
  8.8 11.8 %collective-permute-start = (f32[64,112,128]{2,1,0:T(8,128)}, f32[64,112,128]{2,1,0:T(8,128)}, u32[]{:S(2)}, u32[]{:S(2)}) collective-permute-start(f32[64,112,128]{2,1,0:T(8,128)} %shard_map.78), channel_id=1, source_target_pairs={{0,1},{1,0},{2,3},{3,2},{4,5},{5,4},{6,7},{7,6},{8,9},{9,8},{10,11... | collective-permute-start | bytes 11010056 | tf_op jit(solution)/shard_map/ppermute | solution.py:265
  10.4 46.6 %collective-permute-start.10 = (f32[64,128,128]{2,1,0:T(8,128)S(1)}, f32[64,128,128]{2,1,0:T(8,128)}, u32[]{:S(2)}, u32[]{:S(2)}) collective-permute-start(f32[64,128,128]{2,1,0:T(8,128)S(1)} %shard_map.81), channel_id=1, source_target_pairs={{0,1},{1,0},{2,3},{3,2},{4,5},{5,4},{6,7},{7,6},{8,9},{9,8},{10,11... | collective-permute-start | bytes 12582920 | tf_op jit(solution)/shard_map/ppermute | solution.py:265
  11.0 5.7 %collective-permute-start.5 = (f32[64,16,128]{2,1,0:T(8,128)S(1)}, f32[64,16,128]{2,1,0:T(8,128)S(1)}, u32[]{:S(2)}, u32[]{:S(2)}) collective-permute-start(f32[64,16,128]{2,1,0:T(8,128)S(1)} %shard_map.77), channel_id=1, source_target_pairs={{0,1},{1,0},{2,3},{3,2},{4,5},{5,4},{6,7},{7,6},{8,9},{9,8},{10,11... | collective-permute-start | bytes 1572872 | tf_op jit(solution)/shard_map/ppermute | solution.py:265
  18.5 38.5 %copy-start.5 = (f32[1,64,2,8192]{3,2,1,0:T(2,128)S(1)}, f32[1,64,2,8192]{3,2,1,0:T(2,128)}, u32[]{:S(2)}) copy-start(f32[1,64,2,8192]{3,2,1,0:T(2,128)} %param.7) | copy-start | bytes 12582916
  18.5 13.8 %collective-permute-start.6 = (f32[960,128]{1,0:T(8,128)S(1)}, f32[960,128]{1,0:T(8,128)S(1)}, u32[]{:S(2)}, u32[]{:S(2)}) collective-permute-start(f32[960,128]{1,0:T(8,128)S(1)} %get-tuple-element.43), channel_id=1, source_target_pairs={{0,2},{1,3},{2,0},{3,1},{4,6},{5,7},{6,4},{7,5},{8,10},{9,11},{10,... | collective-permute-start | bytes 1474568 | tf_op jit(solution)/shard_map/ppermute | solution.py:268
  31.9 38.1 %copy-start.8 = (f32[960,128]{1,0:T(8,128)}, f32[960,128]{1,0:T(8,128)S(1)}, u32[]{:S(2)}) copy-start(f32[960,128]{1,0:T(8,128)S(1)} %get-tuple-element.38) | copy-start | bytes 1474564
  31.9 38.1 %copy-start.9 = (f32[960,128]{1,0:T(8,128)}, f32[960,128]{1,0:T(8,128)S(1)}, u32[]{:S(2)}) copy-start(f32[960,128]{1,0:T(8,128)S(1)} %get-tuple-element.46) | copy-start | bytes 1474564
  31.9 38.1 %copy-start.10 = (f32[960,128]{1,0:T(8,128)}, f32[960,128]{1,0:T(8,128)S(1)}, u32[]{:S(2)}) copy-start(f32[960,128]{1,0:T(8,128)S(1)} %get-tuple-element.37) | copy-start | bytes 1474564
  31.9 14.2 %collective-permute-start.1 = (f32[960,128]{1,0:T(8,128)S(1)}, f32[960,128]{1,0:T(8,128)S(1)}, u32[]{:S(2)}, u32[]{:S(2)}) collective-permute-start(f32[960,128]{1,0:T(8,128)S(1)} %get-tuple-element.35), channel_id=1, source_target_pairs={{0,2},{1,3},{2,0},{3,1},{4,6},{5,7},{6,4},{7,5},{8,10},{9,11},{10,... | collective-permute-start | bytes 1474568 | tf_op jit(solution)/shard_map/ppermute | solution.py:268
  32.4 24.3 %collective-permute-start.7 = (f32[960,128]{1,0:T(8,128)S(1)}, f32[960,128]{1,0:T(8,128)S(1)}, u32[]{:S(2)}, u32[]{:S(2)}) collective-permute-start(f32[960,128]{1,0:T(8,128)S(1)} %get-tuple-element.44), channel_id=1, source_target_pairs={{0,2},{1,3},{2,0},{3,1},{4,6},{5,7},{6,4},{7,5},{8,10},{9,11},{10,... | collective-permute-start | bytes 1474568 | tf_op jit(solution)/shard_map/ppermute | solution.py:268
  46.1 32.0 %collective-permute-start.2 = (f32[960,128]{1,0:T(8,128)}, f32[960,128]{1,0:T(8,128)}, u32[]{:S(2)}, u32[]{:S(2)}) collective-permute-start(f32[960,128]{1,0:T(8,128)} %get-tuple-element.36), channel_id=1, source_target_pairs={{0,2},{1,3},{2,0},{3,1},{4,6},{5,7},{6,4},{7,5},{8,10},{9,11},{10,... | collective-permute-start | bytes 1474568 | tf_op jit(solution)/shard_map/ppermute | solution.py:268
  56.7 13.4 %copy-start.6 = (f32[960,128]{1,0:T(8,128)}, f32[960,128]{1,0:T(8,128)S(1)}, u32[]{:S(2)}) copy-start(f32[960,128]{1,0:T(8,128)S(1)} %collective-permute-done.7.pay_ref) | copy-start | bytes 1474564
  56.7 23.2 %collective-permute-start.8 = (f32[960,128]{1,0:T(8,128)}, f32[960,128]{1,0:T(8,128)}, u32[]{:S(2)}, u32[]{:S(2)}) collective-permute-start(f32[960,128]{1,0:T(8,128)} %get-tuple-element.45), channel_id=1, source_target_pairs={{0,2},{1,3},{2,0},{3,1},{4,6},{5,7},{6,4},{7,5},{8,10},{9,11},{10,... | collective-permute-start | bytes 1474568 | tf_op jit(solution)/shard_map/ppermute | solution.py:268
  70.9 17.4 %all-to-all-start = ((f32[16,2,32,128]{3,2,1,0:T(8,128)}), f32[16,2,32,128]{3,2,1,0:T(8,128)}, u32[]{:S(2)}, u32[]{:S(2)}) async-start(f32[16,2,32,128]{3,2,1,0:T(8,128)} %copy.23), calls=%async_computation | async-start | bytes 1048576 | tf_op jit(solution)/shard_map/all_to_all | solution.py:283
  78.2 14.6 %collective-permute-start.3 = (f32[960,128]{1,0:T(8,128)}, f32[960,128]{1,0:T(8,128)}, u32[]{:S(2)}, u32[]{:S(2)}) collective-permute-start(f32[960,128]{1,0:T(8,128)} %copy-done.10), channel_id=1, source_target_pairs={{0,2},{1,3},{2,0},{3,1},{4,6},{5,7},{6,4},{7,5},{8,10},{9,11},{10,... | collective-permute-start | bytes 1474568 | tf_op jit(solution)/shard_map/ppermute | solution.py:268
  79.8 65.6 %collective-permute-start.9 = (f32[960,128]{1,0:T(8,128)}, f32[960,128]{1,0:T(8,128)}, u32[]{:S(2)}, u32[]{:S(2)}) collective-permute-start(f32[960,128]{1,0:T(8,128)} %copy-done.9), channel_id=1, source_target_pairs={{0,2},{1,3},{2,0},{3,1},{4,6},{5,7},{6,4},{7,5},{8,10},{9,11},{10,... | collective-permute-start | bytes 1474568 | tf_op jit(solution)/shard_map/ppermute | solution.py:268
  92.7 55.8 %collective-permute-start.4 = (f32[960,128]{1,0:T(8,128)}, f32[960,128]{1,0:T(8,128)}, u32[]{:S(2)}, u32[]{:S(2)}) collective-permute-start(f32[960,128]{1,0:T(8,128)} %copy-done.8), channel_id=1, source_target_pairs={{0,2},{1,3},{2,0},{3,1},{4,6},{5,7},{6,4},{7,5},{8,10},{9,11},{10,... | collective-permute-start | bytes 1474568 | tf_op jit(solution)/shard_map/ppermute | solution.py:268
  94.3 19.3 %collective-permute-start.12 = (f32[32,128]{1,0:T(8,128)S(1)}, f32[32,128]{1,0:T(8,128)S(1)}, u32[]{:S(2)}, u32[]{:S(2)}) collective-permute-start(f32[32,128]{1,0:T(8,128)S(1)} %get-tuple-element.59), channel_id=1, source_target_pairs={{0,64},{1,65},{2,66},{3,67},{4,68},{5,69},{6,70},{7,71},{8,72},{9,... | collective-permute-start | bytes 49160 | tf_op jit(solution)/shard_map/ppermute | solution.py:288
  97.9 15.7 %collective-permute-start.13 = (f32[32,128]{1,0:T(8,128)S(1)}, f32[32,128]{1,0:T(8,128)S(1)}, u32[]{:S(2)}, u32[]{:S(2)}) collective-permute-start(f32[32,128]{1,0:T(8,128)S(1)} %get-tuple-element.58), channel_id=1, source_target_pairs={{0,66},{1,67},{2,64},{3,65},{4,70},{5,71},{6,68},{7,69},{8,74},{9,... | collective-permute-start | bytes 49160 | tf_op jit(solution)/shard_map/ppermute | solution.py:289
  97.9 15.7 %collective-permute-start.11 = (f32[32,128]{1,0:T(8,128)S(1)}, f32[32,128]{1,0:T(8,128)S(1)}, u32[]{:S(2)}, u32[]{:S(2)}) collective-permute-start(f32[32,128]{1,0:T(8,128)S(1)} %get-tuple-element.58), channel_id=1, source_target_pairs={{0,2},{1,3},{2,0},{3,1},{4,6},{5,7},{6,4},{7,5},{8,10},{9,11},{10,... | collective-permute-start | bytes 49160 | tf_op jit(solution)/shard_map/ppermute | solution.py:287
  114.3 21.8 %all-to-all-start.1 = ((f32[16,32,128]{2,1,0:T(8,128)}), f32[16,32,128]{2,1,0:T(8,128)S(1)}, u32[]{:S(2)}, u32[]{:S(2)}) async-start(f32[16,32,128]{2,1,0:T(8,128)} %broadcast_in_dim.2), calls=%async_computation.1 | async-start | bytes 524288 | tf_op jit(solution)/shard_map/all_to_all | solution.py:292
  (3 other events, 14.3 us)

commit v2 on v0

v2 whole, which is shorter than its diff:
```python
import functools
import math

import jax
import jax.numpy as jnp
import ml_dtypes
import numpy as np
from jax import lax
from jax.experimental import pallas as pl
from jax.experimental.pallas import tpu as pltpu
from jax.sharding import PartitionSpec as P

SPAN = 64
BAND = 16
LANES = 128
GROUP = 8
QUANTUM = 2 * GROUP
DECAY = 0.9
HIGH = SPAN - BAND
QUARTER = GROUP // 4 * BAND
PAYLOAD = QUANTUM * HIGH + 3 * SPAN
PLANE = 16
VMEM = 46 * 1024 * 1024


def dct(order):
    q = np.arange(order)[:, None]
    n = np.arange(order)[None, :]
    scale = np.where(q == 0, math.sqrt(1.0 / order), math.sqrt(2.0 / order))
    return scale * np.cos(math.pi * (2 * n + 1) * q / (2 * order))


def halves(a):
    high = a.astype(ml_dtypes.bfloat16)
    return high, (a - high.astype(np.float64)).astype(ml_dtypes.bfloat16)


def left(a):
    high, low = halves(a)
    return np.concatenate([high, low, high], axis=1)


def right(a):
    high, low = halves(a)
    return np.concatenate([high, low, high], axis=0)


def constants():
    t = dct(SPAN)
    lanes = np.kron(np.eye(8), t.T)
    coef = np.arange(512) % SPAN
    order = np.concatenate([np.flatnonzero(coef >= BAND), np.flatnonzero(coef < BAND)])
    lanes = lanes[:, order]
    kept, band = lanes[:, : 3 * LANES], lanes[:, 3 * LANES :]
    mats = dict(
        rows=left(t), rows_back=left(t.T), low=left(t[:BAND]), low_back=left(t[:BAND].T),
        lanes=right(lanes), kept_back=right(kept.T), band=right(band), band_back=right(band.T),
    )
    return {name: jnp.asarray(a) for name, a in mats.items()}


def split(x):
    high = x.astype(jnp.bfloat16)
    return high, (x - high.astype(jnp.float32)).astype(jnp.bfloat16)


def tall(x):
    high, low = split(x)
    return jnp.concatenate([high, high, low], axis=0)


def long(x):
    high, low = split(x)
    return jnp.concatenate([high, high, low], axis=1)


def dot(a, b):
    return jnp.dot(a, b, preferred_element_type=jnp.float32)


def beside(x):
    x = jnp.swapaxes(x, 0, 1)
    return [jnp.concatenate([x[4 * s + j] for j in range(4)], axis=1) for s in range(4)]


def apart(parts):
    x = jnp.stack([p[:, j * LANES : (j + 1) * LANES] for p in parts for j in range(4)], axis=0)
    return jnp.swapaxes(x, 0, 1)


def forward(x, rows):
    return [dot(rows, tall(part)) for part in beside(x)]


def back(parts, rows):
    return apart([dot(rows, tall(p)) for p in parts])


def bands_of(c):
    return [c[s * BAND : (s + 1) * BAND] for s in range(4)]


def rows_of(place, slot):
    return pl.ds(pl.multiple_of(place[slot] * SPAN, SPAN), SPAN)


def quantum(k):
    return pl.ds(k * QUANTUM, QUANTUM)


def load(constants, buffers, sems):
    copies = [pltpu.make_async_copy(c, b, sems.at[i]) for i, (c, b) in enumerate(zip(constants, buffers))]
    for copy in copies:
        copy.start()
    return copies


def cast_kernel(first, counts, slot, place, g_ref, *refs):
    outs, (held, cells, sems) = refs[: len(counts)], refs[len(counts) :]
    into, out = [], []
    for o, n in zip(outs, counts):
        for j in range(n):
            k = len(into)
            source = g_ref.at[rows_of(place, slot), quantum(first + k), :]
            into.append(pltpu.make_async_copy(source, held.at[k], sems.at[0, k]))
            out.append(pltpu.make_async_copy(cells.at[k], o.at[:, quantum(j), :], sems.at[1, k]))
            into[-1].start()
    for k in range(len(into)):
        into[k].wait()
        cells[k] = held[k].astype(jnp.float32)
        out[k].start()
    for copy in out:
        copy.wait()


def encode_kernel(first, count, skip, slot, place, g_ref, r_ref, rows, lanes, *refs):
    pay_ref, band_ref, g_buf, r_buf, pay_buf, band_buf, low_buf, rows_buf, lanes_buf, sems, const_sems = refs[-11:]
    high = QUANTUM * HIGH

    def into(k):
        yield pltpu.make_async_copy(g_ref.at[rows_of(place, slot), quantum(first + k), :], g_buf.at[k], sems.at[0, k])
        yield pltpu.make_async_copy(r_ref.at[:, quantum(skip + k), :], r_buf.at[k], sems.at[1, k])

    def out_high(k):
        at = pl.ds(0, high)
        return pltpu.make_async_copy(pay_buf.at[k, at], pay_ref.at[k, at], sems.at[2, k])

    def out_low(k):
        at = pl.ds(high, 3 * SPAN)
        yield pltpu.make_async_copy(pay_buf.at[k, at], pay_ref.at[k, at], sems.at[3, k])
        to = band_ref.at[pl.ds((first + k + PLANE // 2 - 2) % (PLANE // 2) * 2, 2), 1]
        yield pltpu.make_async_copy(band_buf.at[k], to, sems.at[4, k])

    for copy in into(0):
        copy.start()
    consts = load((rows, lanes), (rows_buf, lanes_buf), const_sems)
    for k in range(1, count):
        for copy in into(k):
            copy.start()
    consts[0].wait()

    def body(k, _):
        for copy in into(k):
            copy.wait()
        for s, c in enumerate(forward(g_buf[k].astype(jnp.float32) + r_buf[k], rows_buf[...])):
            low_buf[k, s * BAND : (s + 1) * BAND, :] = c[:BAND]
            for j in range(4):
                at = (4 * s + j) * HIGH
                pay_buf[k, at : at + HIGH, :] = c[BAND:, j * LANES : (j + 1) * LANES]
        out_high(k).start()
        return 0

    lax.fori_loop(0, count, body, 0)
    consts[1].wait()
    w = dot(long(low_buf[...].reshape(count * SPAN, 4 * LANES)), lanes_buf[...])
    for k in range(count):
        part = w[k * SPAN : (k + 1) * SPAN]
        for i in range(3):
            at = high + i * SPAN
            pay_buf[k, at : at + SPAN, :] = part[:, i * LANES : (i + 1) * LANES]
        band_buf[k] = part[:, 3 * LANES :].reshape(2, QUARTER, LANES)
        for copy in out_low(k):
            copy.start()
    for k in range(count):
        out_high(k).wait()
        for copy in out_low(k):
            copy.wait()


def base_kernel(counts, slot, place, m_ref, g_ref, *refs):
    received, refs = refs[: len(counts)], refs[len(counts) :]
    constants, refs = refs[:4], refs[5:]
    out_ref, band_ref, m_buf, g_buf, r_buf, out_buf, band_buf, low_buf = refs[:8]
    buffers, (sems, const_sems) = refs[8:12], refs[12:]
    total = sum(counts)
    where = [(r, j) for r, n in zip(received, counts) for j in range(n)]

    def into(k, r=None, j=0):
        yield pltpu.make_async_copy(m_ref.at[:, quantum(k), :], m_buf.at[k], sems.at[0, k])
        yield pltpu.make_async_copy(g_ref.at[rows_of(place, slot), quantum(k), :], g_buf.at[k], sems.at[1, k])
        r = received[0] if r is None else r
        yield pltpu.make_async_copy(r.at[:, quantum(j), :], r_buf.at[k], sems.at[2, k])

    def out(k):
        return pltpu.make_async_copy(out_buf.at[k], out_ref.at[:, quantum(k), :], sems.at[3, k])

    def out_band(k):
        return pltpu.make_async_copy(band_buf.at[k], band_ref.at[pl.ds(2 * k, 2), 0], sems.at[4, k])

    for copy in into(0, *where[0]):
        copy.start()
    consts = load(constants, buffers, const_sems)
    for k in range(1, total):
        for copy in into(k, *where[k]):
            copy.start()
    for copy in consts:
        copy.wait()
    low, low_back, band, band_back = buffers

    def body(k, _):
        for copy in into(k):
            copy.wait()
        cells = DECAY * m_buf[k] + (g_buf[k].astype(jnp.float32) + r_buf[k])
        m_buf[k] = cells
        for s, c in enumerate(forward(cells, low[...])):
            low_buf[k, s * BAND : (s + 1) * BAND, :] = c
        return 0

    lax.fori_loop(0, total, body, 0)
    b = dot(long(low_buf[...].reshape(total * SPAN, 4 * LANES)), band[...])
    band_buf[...] = b.reshape(total, 2, QUARTER, LANES)
    for k in range(total):
        out_band(k).start()
    low_buf[...] = dot(long(b), band_back[...]).reshape(total, SPAN, 4 * LANES)

    def body_back(k, _):
        out_buf[k] = m_buf[k] - back(bands_of(low_buf[k]), low_back[...])
        out(k).start()
        return 0

    lax.fori_loop(0, total, body_back, 0)
    for k in range(total):
        out(k).wait()
        out_band(k).wait()


def decode_kernel(first, count, pay_ref, rows_back, kept_back, base_ref, out_ref, *refs):
    pay_buf, base_buf, low_buf, rows_buf, kept_buf, sems, const_sems = refs
    at = QUANTUM * HIGH

    def into(k):
        yield pltpu.make_async_copy(pay_ref.at[k], pay_buf.at[k], sems.at[0, k])
        yield pltpu.make_async_copy(base_ref.at[:, quantum(first + k), :], base_buf.at[k], sems.at[1, k])

    def out(k):
        return pltpu.make_async_copy(base_buf.at[k], out_ref.at[:, quantum(first + k), :], sems.at[2, k])

    for k in range(count):
        for copy in into(k):
            copy.start()
    for copy in load((rows_back, kept_back), (rows_buf, kept_buf), const_sems):
        copy.wait()
    for k in range(count):
        for copy in into(k):
            copy.wait()
    kept = [
        jnp.concatenate([pay_buf[k, at + i * SPAN : at + (i + 1) * SPAN, :] for i in range(3)], axis=1)
        for k in range(count)
    ]
    low_buf[...] = dot(long(jnp.concatenate(kept, axis=0)), kept_buf[...]).reshape(count, SPAN, 4 * LANES)

    def body(k, _):
        parts = []
        for s, low in enumerate(bands_of(low_buf[k])):
            high = [pay_buf[k, (4 * s + j) * HIGH : (4 * s + j + 1) * HIGH, :] for j in range(4)]
            parts.append(jnp.concatenate([low, jnp.concatenate(high, axis=1)], axis=0))
        base_buf[k] = base_buf[k] + back(parts, rows_buf[...])
        out(k).start()
        return 0

    lax.fori_loop(0, count, body, 0)
    for k in range(count):
        out(k).wait()


def update_kernel(scale, count, band_ref, low_back, band_back, out_ref, band_buf, low_rows, back_buf, out_buf, low_buf, sems, const_sems):
    for copy in load((band_ref, low_back, band_back), (band_buf, low_rows, back_buf), const_sems):
        copy.wait()
    b = band_buf[...].reshape(count * SPAN, LANES) * scale
    low_buf[...] = dot(long(b), back_buf[...]).reshape(count, SPAN, 4 * LANES)

    def out(k):
        return pltpu.make_async_copy(out_buf.at[k], out_ref.at[:, quantum(k), :], sems.at[k])

    def body(k, _):
        out_buf[k] = back(bands_of(low_buf[k]), low_rows[...])
        out(k).start()
        return 0

    lax.fori_loop(0, count, body, 0)
    for k in range(count):
        out(k).wait()


ANY = pl.BlockSpec(memory_space=pl.ANY)
BANDS = jax.ShapeDtypeStruct((PLANE, 2, QUARTER, LANES), jnp.float32)


def call(kernel, place, operands, outs, scratch, aliases):
    scalars = [] if place is None else [place]
    return pl.pallas_call(
        kernel,
        grid_spec=pltpu.PrefetchScalarGridSpec(
            num_scalar_prefetch=len(scalars),
            grid=(),
            in_specs=[ANY] * len(operands),
            out_specs=[ANY] * len(outs),
            scratch_shapes=scratch,
        ),
        out_shape=outs,
        input_output_aliases=aliases,
        cost_estimate=pl.CostEstimate(flops=0, bytes_accessed=0, transcendentals=0),
        compiler_params=pltpu.CompilerParams(vmem_limit_bytes=VMEM),
    )(*scalars, *operands)


def floats(*shape):
    return jax.ShapeDtypeStruct(shape, jnp.float32)


def held(count, *dtypes):
    return [pltpu.VMEM((count, SPAN, QUANTUM, LANES), dtype) for dtype in dtypes]


def lows(count):
    return [pltpu.VMEM((count, SPAN, 4 * LANES), jnp.float32)]


def same(arrays):
    return [pltpu.VMEM(a.shape, a.dtype) for a in arrays]


def sems(*shape):
    return pltpu.SemaphoreType.DMA(shape)


def cast(place, g, first, counts, slot):
    n = sum(counts)
    return call(
        functools.partial(cast_kernel, first, counts, slot),
        place,
        [g],
        [floats(SPAN, c * QUANTUM, LANES) for c in counts],
        held(n, jnp.bfloat16, jnp.float32) + [sems(2, n)],
        {},
    )


def encoded(place, g, received, skip, first, count, slot, mats, bands=None):
    values = [mats["rows"], mats["lanes"]]
    more = [] if bands is None else [bands]
    return call(
        functools.partial(encode_kernel, first, count, skip, slot),
        place,
        [g, received, *values, *more],
        [floats(count, PAYLOAD, LANES), BANDS],
        held(count, jnp.bfloat16, jnp.float32)
        + [pltpu.VMEM((count, PAYLOAD, LANES), jnp.float32), pltpu.VMEM((count, 2, QUARTER, LANES), jnp.float32)]
        + lows(count)
        + same(values)
        + [sems(5, count), sems(2)],
        {5: 1} if more else {},
    )


def based(place, m, g, received, slot, mats, bands):
    values = [mats[name] for name in ("low", "low_back", "band", "band_back")]
    counts = [r.shape[1] // QUANTUM for r in received]
    n = sum(counts)
    return call(
        functools.partial(base_kernel, counts, slot),
        place,
        [m, g, *received, *values, bands],
        [floats(*m.shape), BANDS],
        held(n, jnp.float32, jnp.bfloat16, jnp.float32, jnp.float32)
        + [pltpu.VMEM((n, 2, QUARTER, LANES), jnp.float32)]
        + lows(n)
        + same(values)
        + [sems(5, n), sems(4)],
        {3 + len(received) + 4: 1},
    )


def decoded(payload, base, first, mats):
    values = [mats["rows_back"], mats["kept_back"]]
    count = payload.shape[0]
    return call(
        functools.partial(decode_kernel, first, count),
        None,
        [payload, *values, base],
        [floats(*base.shape)],
        [pltpu.VMEM((count, PAYLOAD, LANES), jnp.float32)]
        + held(count, jnp.float32)
        + lows(count)
        + same(values)
        + [sems(3, count), sems(2)],
        {3: 0},
    )[0]


def updated(band, scale, shape, mats):
    values = [mats["low_back"], mats["band_back"]]
    count = shape[1] // QUANTUM
    return call(
        functools.partial(update_kernel, scale, count),
        None,
        [band, *values],
        [floats(*shape)],
        same([band, *values]) + held(count, jnp.float32) + lows(count) + [sems(count), sems(3)],
        {},
    )[0]


def tiles(x):
    rows, mats, width = x.shape
    x = x.reshape(rows, mats, width // LANES, LANES).transpose(0, 2, 1, 3)
    return x.reshape(rows, mats * width // LANES, LANES)


def untiles(x, mats):
    rows, places, _ = x.shape
    x = x.reshape(rows, places // mats, mats, LANES).transpose(0, 2, 1, 3)
    return x.reshape(rows, mats, places // mats * LANES)


def tie(*arrays):
    return lax.optimization_barrier(arrays)


def per_device(grads, momentum):
    rep_count = lax.axis_size("rep")
    mat_count = grads.shape[3]
    mats = constants()
    g = tiles(grads[0, 0])
    m = tiles(momentum[0])
    count = m.shape[1] // QUANTUM
    member = lax.axis_index("fsdp")
    place = jnp.stack([member, member ^ 1, member ^ 2, member ^ 3]).astype(jnp.int32)
    over_core = [(f, f ^ 1) for f in range(4)]
    over_z = [(f, f ^ 2) for f in range(4)]

    def core(x):
        return lax.ppermute(x, "fsdp", over_core)

    def link(x):
        return lax.ppermute(x, "fsdp", over_z)

    (cells,) = cast(place, g, 0, (1,), 3)
    place1, cells = tie(place, cells)
    more, last = cast(place1, g, 1, (6, 1), 3)
    got, more = tie(core(cells), more)
    pay0, bands = encoded(place, g, got, 0, 0, 1, 2, mats)
    there0 = link(pay0)
    pay1, bands = encoded(place, g, core(more), 0, 1, 6, 2, mats, bands)
    place2, pay1 = tie(place1, pay1)
    mine = cast(place2, g, 0, (2, 2, 2, 2), 1)
    pay1, there0, *mine = tie(pay1, there0, *mine)
    there1 = link(pay1)
    pay2, bands = encoded(place, g, core(last), 0, 7, 1, 2, mats, bands)
    there2 = link(pay2)
    base, bands = based(place, m, g, [core(c) for c in mine], 0, mats, bands)

    groups = [[h * PLANE + i for i in range(PLANE)] for h in range(rep_count // PLANE)]
    met = lax.all_to_all(bands, "rep", 0, 0, axis_index_groups=groups, tiled=True)
    part = jnp.sum(met, axis=0)
    names = ("rep", "fsdp")
    own = part[0] + lax.ppermute(part[1], names, steps(rep_count, 1, 4, 2))
    other = part[1] + lax.ppermute(part[0], names, steps(rep_count, 1, -4, 2))
    total = own + lax.ppermute(other, names, steps(rep_count, 0, 4, 2))
    spread = jnp.broadcast_to(total[None], (PLANE,) + total.shape)
    band_total = lax.all_to_all(spread, "rep", 0, 0, axis_index_groups=groups, tiled=True)
    update = updated(band_total, 1.0 / rep_count, m.shape, mats)

    out = decoded(there0, base, 0, mats)
    there1, update = tie(there1, update)
    out = decoded(there1, out, 1, mats)
    there2, out = tie(there2, out)
    out = decoded(there2, out, 7, mats)
    return (untiles(out, mat_count)[None], untiles(update, mat_count))


def steps(rep_count, z_hi, plane, member):
    pairs = []
    for rep in range(rep_count):
        high, low = divmod(rep, PLANE)
        to = (high ^ z_hi) * PLANE + (low + plane) % PLANE
        pairs += [(rep * 4 + f, to * 4 + (f ^ member)) for f in range(4)]
    return pairs


def solution(mesh):
    in_specs = (P("rep", "fsdp", None, None, None), P("rep", "fsdp", None, None))
    out_specs = (P("rep", "fsdp", None, None), P("fsdp", None, None))
    return jax.shard_map(
        per_device, mesh=mesh, in_specs=in_specs, out_specs=out_specs, check_vma=False
    )
```

time: 585 us -> 101 us (0.17)
  waiting for transfers between devices: 489 us -> 25.2 us
  Pallas kernels: 0 us -> 41.8 us
  local copies, waits for them, and re-layouts: 34.3 us -> 0.78 us
  matrix products: 28.7 us -> 0 us
  blocking collectives: 0 us -> 18.6 us
  between operations: 14.2 us -> 0.83 us
  starting transfers between devices: 0.76 us -> 13.3 us
  other arithmetic: 12.2 us -> 0.12 us
    psum x1 -> x0, waiting for transfers between devices: 340 us -> none  [advance(): band_total = lax.psum(own_band, 'rep')]
    reduce_scatter x2 -> x0, waiting for transfers between devices: 149 us -> none  [advance(): lax.psum_scatter(part_grads.astype(jnp.float32), 'fsdp', scatter_dimensio...]
    pallas_call x0 -> x11, Pallas kernels: none -> 41.8 us  [call(): pl.pallas_call(kernel, grid_spec=pltpu.PrefetchScalarGridSpec(num_scalar_...]
    unnamed x18 -> x16, local copies, waits for them, and re-layouts: 29.7 us -> 0.04 us
    dot_general x12 -> x0, matrix products: 28.7 us -> none  [the longest x4 11.1 us: inverse_band(): jnp.einsum('pn,apmd->anmd', basis, merged, precision=lax.Precision.HIGHEST)]
    ppermute x0 -> x13, waiting for transfers between devices: none -> 19.5 us  [the longest x3 7.86 us: link(): return lax.ppermute(x, 'fsdp', over_z)]
    all_to_all x0 -> x1, blocking collectives: none -> 18.6 us  [per_device(): lax.all_to_all(bands, 'rep', 0, 0, axis_index_groups=groups, tiled=True)]
    convert_element_type x1 -> x0, other arithmetic: 11.4 us -> none  [advance(): part_grads.astype(jnp.float32)]
  transfers between devices with their start and end apart: 3 -> 14, of which waited for: 3 -> 11; matrix products, arithmetic and copies ran while one was open for 5% -> 1% of each run, Pallas kernels for 0% -> 37%
where the time goes in v2:
time: 101 us
  Pallas kernels  41.8 us (41%)
  waiting for transfers between devices  25.2 us (25%)
  blocking collectives  18.6 us (18%)
  starting transfers between devices  13.3 us (13%)
    pallas_call x11, Pallas kernels, call(): pl.pallas_call(kernel, grid_spec=pltpu.PrefetchScalarGridSpec(num_scalar_...  41.8 us
    all_to_all x1, blocking collectives, per_device(): lax.all_to_all(bands, 'rep', 0, 0, axis_index_groups=groups, tiled=True)  18.6 us
    ppermute x3, waiting for transfers between devices, link(): return lax.ppermute(x, 'fsdp', over_z)  7.86 us
    all_to_all x1, waiting for transfers between devices, per_device(): lax.all_to_all(spread, 'rep', 0, 0, axis_index_groups=groups, tiled=True)  5.61 us
    ppermute x1, waiting for transfers between devices, per_device(): own = part[0] + lax.ppermute(part[1], names, steps(rep_count, 1, 4, 2))  5.26 us
    ppermute x3, starting transfers between devices, link(): return lax.ppermute(x, 'fsdp', over_z)  4.84 us
    ppermute x7, waiting for transfers between devices, core(): return lax.ppermute(x, 'fsdp', over_core)  4.06 us
    all_to_all x1, starting transfers between devices, per_device(): lax.all_to_all(spread, 'rep', 0, 0, axis_index_groups=groups, tiled=True)  3.53 us
  transfers between devices with their start and end apart: 14, of which 11 were waited for; matrix products, arithmetic and copies ran while one was open for 1% of the time, Pallas kernels for 37%

profile of v2, /device:TPU:0, one launch (start us, length us, event | category | flops | bytes accessed | tf_op | source)
XLA Modules:
  0.0 100.6 jit_solution(8381604889518169196)
XLA Ops:
  0.7 1.6 %shard_map.113 = f32[64,16,128]{2,1,0:T(8,128)S(1)} custom-call(s32[4]{0:T(128)S(1)} %pad_add_fusion.place, bf16[256,128,128]{2,1,0:T(8,128)(2,1)} %bitcast.32), custom_call_target="tpu_custom_call" | custom-call | tf_op jit(solution)/shard_map/pallas_call | solution.py:311
  2.4 2.3 %shard_map.114 = (f32[64,96,128]{2,1,0:T(8,128)S(1)}, f32[64,16,128]{2,1,0:T(8,128)S(1)}) custom-call(s32[4]{0:T(128)S(1)} %pad_add_fusion.place, bf16[256,128,128]{2,1,0:T(8,128)(2,1)} %bitcast.33), custom_call_target="tpu_custom_call" | custom-call | tf_op jit(solution)/shard_map/pallas_call | solution.py:311
  5.3 2.6 %shard_map.115 = (f32[1,960,128]{2,1,0:T(8,128)S(1)}, f32[16,2,32,128]{3,2,1,0:T(8,128)S(1)}) custom-call(s32[4]{0:T(128)S(1)} %pad_add_fusion.place, bf16[256,128,128]{2,1,0:T(8,128)(2,1)} %bitcast.34, f32[64,16,128]{2,1,0:T(8,128)S(1)} %collective-permute-done.1.r_ref, bf16[64,192]{1,0:T(8,128)(2,1)S(1)} %copy-done.5, bf16[1536,512]{1,0:T(8,128)(2,1)S(1)} %copy-done), custom_call_target="tpu_custom_call" | custom-call | tf_op jit(solution)/shard_map/pallas_call | solution.py:311
  8.0 2.1 %collective-permute-start.4 = (f32[1,960,128]{2,1,0:T(8,128)S(1)}, f32[1,960,128]{2,1,0:T(8,128)S(1)}, u32[]{:S(2)}, u32[]{:S(2)}) collective-permute-start(f32[1,960,128]{2,1,0:T(8,128)S(1)} %get-tuple-element.43), channel_id=1, source_target_pairs={{0,2},{1,3},{2,0},{3,1},{4,6},{5,7},{6,4},{7,5},{8,10},{9,11},{10,... | collective-permute-start | bytes 1474568 | tf_op jit(solution)/shard_map/ppermute | solution.py:456
  10.6 5.5 %shard_map.116 = (f32[6,960,128]{2,1,0:T(8,128)}, f32[16,2,32,128]{3,2,1,0:T(8,128)S(1)}) custom-call(s32[4]{0:T(128)S(1)} %pad_add_fusion.place, bf16[256,128,128]{2,1,0:T(8,128)(2,1)} %bitcast.35, f32[64,96,128]{2,1,0:T(8,128)S(1)} %collective-permute-done.2.r_ref, bf16[64,192]{1,0:T(8,128)(2,1)S(1)} %copy-done.5, ...), custom_call_target="tpu_custom_call", output_to_operand_aliasing={{1}: (5, {})} | custom-call | tf_op jit(solution)/shard_map/pallas_call | solution.py:311
  16.1 2.5 %shard_map.118 = (f32[64,32,128]{2,1,0:T(8,128)S(1)}, f32[64,32,128]{2,1,0:T(8,128)S(1)}, f32[64,32,128]{2,1,0:T(8,128)S(1)}, f32[64,32,128]{2,1,0:T(8,128)S(1)}) custom-call(s32[4]{0:T(128)S(1)} %pad_add_fusion.place, bf16[256,128,128]{2,1,0:T(8,128)(2,1)} %bitcast.36), custom_call_target="tpu_custom_call" | custom-call | tf_op jit(solution)/shard_map/pallas_call | solution.py:311
  18.6 2.8 %collective-permute-done.4.pay_ref = f32[1,960,128]{2,1,0:T(8,128)S(1)} collective-permute-done((f32[1,960,128]{2,1,0:T(8,128)S(1)}, f32[1,960,128]{2,1,0:T(8,128)S(1)}, u32[]{:S(2)}, u32[]{:S(2)}) %collective-permute-start.4) | collective-permute-done | bytes 491552 | tf_op jit(solution)/shard_map/ppermute | solution.py:456
  21.5 1.7 %collective-permute-start.5 = (f32[6,960,128]{2,1,0:T(8,128)}, f32[6,960,128]{2,1,0:T(8,128)}, u32[]{:S(2)}, u32[]{:S(2)}) collective-permute-start(f32[6,960,128]{2,1,0:T(8,128)} %get-tuple-element.49), channel_id=1, source_target_pairs={{0,2},{1,3},{2,0},{3,1},{4,6},{5,7},{6,4},{7,5},{8,10},{9,11},{10,... | collective-permute-start | bytes 8847368 | tf_op jit(solution)/shard_map/ppermute | solution.py:456
  24.2 2.6 %shard_map.117 = (f32[1,960,128]{2,1,0:T(8,128)S(1)}, f32[16,2,32,128]{3,2,1,0:T(8,128)S(1)}) custom-call(s32[4]{0:T(128)S(1)} %pad_add_fusion.place, bf16[256,128,128]{2,1,0:T(8,128)(2,1)} %bitcast.37, f32[64,16,128]{2,1,0:T(8,128)S(1)} %collective-permute-done.r_ref, bf16[64,192]{1,0:T(8,128)(2,1)S(1)} %copy-done.5, ...), custom_call_target="tpu_custom_call", output_to_operand_aliasing={{1}: (5, {})} | custom-call | tf_op jit(solution)/shard_map/pallas_call | solution.py:311
  27.4 1.5 %collective-permute-done.8.refs_2_ = f32[64,32,128]{2,1,0:T(8,128)S(1)} collective-permute-done((f32[64,32,128]{2,1,0:T(8,128)S(1)}, f32[64,32,128]{2,1,0:T(8,128)S(1)}, u32[]{:S(2)}, u32[]{:S(2)}) %collective-permute-start.8) | collective-permute-done | bytes 1048608 | tf_op jit(solution)/shard_map/ppermute | solution.py:453
  28.9 1.5 %collective-permute-done.9.refs_3_ = f32[64,32,128]{2,1,0:T(8,128)S(1)} collective-permute-done((f32[64,32,128]{2,1,0:T(8,128)S(1)}, f32[64,32,128]{2,1,0:T(8,128)S(1)}, u32[]{:S(2)}, u32[]{:S(2)}) %collective-permute-start.9) | collective-permute-done | bytes 1048608 | tf_op jit(solution)/shard_map/ppermute | solution.py:453
  30.4 9.5 %shard_map.119 = (f32[64,128,128]{2,1,0:T(8,128)}, f32[16,2,32,128]{3,2,1,0:T(8,128)S(1)}) custom-call(s32[4]{0:T(128)S(1)} %pad_add_fusion.place, f32[64,128,128]{2,1,0:T(8,128)} %bitcast.41, bf16[256,128,128]{2,1,0:T(8,128)(2,1)} %bitcast.38, f32[64,32,128]{2,1,0:T(8,128)S(1)} %collective-permute-done.6.refs_0_, ...), custom_call_target="tpu_custom_call", output_to_operand_aliasing={{1}: (11, {})} | custom-call | tf_op jit(solution)/shard_map/pallas_call | solution.py:311
  39.9 18.6 %all_to_all.10 = f32[16,2,32,128]{3,2,1,0:T(8,128)S(1)} all-to-all(f32[16,2,32,128]{3,2,1,0:T(8,128)S(1)} %get-tuple-element.55), channel_id=1, replica_groups={{0,4,8,12,16,20,24,28,32,36,40,44,48,52,56,60},{64,68,72,76,80,84,88,92..., dimensions={0} | all-to-all | bytes 1048576 | tf_op jit(solution)/shard_map/all_to_all | solution.py:474
  58.6 3.1 %collective-permute-start.11 = (f32[32,128]{1,0:T(8,128)S(1)}, f32[32,128]{1,0:T(8,128)S(1)}, u32[]{:S(2)}, u32[]{:S(2)}) collective-permute-start(f32[32,128]{1,0:T(8,128)S(1)} %get-tuple-element.63), channel_id=1, source_target_pairs={{0,114},{1,115},{2,112},{3,113},{4,118},{5,119},{6,116},{7,117},{8... | collective-permute-start | bytes 49160 | tf_op jit(solution)/shard_map/ppermute | solution.py:478
  62.8 1.7 %collective-permute-done.11 = f32[32,128]{1,0:T(8,128)S(1)} collective-permute-done((f32[32,128]{1,0:T(8,128)S(1)}, f32[32,128]{1,0:T(8,128)S(1)}, u32[]{:S(2)}, u32[]{:S(2)}) %collective-permute-start.11) | collective-permute-done | bytes 16416 | tf_op jit(solution)/shard_map/ppermute | solution.py:478
  64.6 5.3 %collective-permute-done.10 = f32[32,128]{1,0:T(8,128)S(1)} collective-permute-done((f32[32,128]{1,0:T(8,128)S(1)}, f32[32,128]{1,0:T(8,128)S(1)}, u32[]{:S(2)}, u32[]{:S(2)}) %collective-permute-start.10) | collective-permute-done | bytes 16416 | tf_op jit(solution)/shard_map/ppermute | solution.py:477
  71.2 3.5 %all-to-all-start.1 = ((f32[16,32,128]{2,1,0:T(8,128)}), f32[16,32,128]{2,1,0:T(8,128)S(1)}, u32[]{:S(2)}, u32[]{:S(2)}) async-start(f32[16,32,128]{2,1,0:T(8,128)} %broadcast_in_dim.2), calls=%async_computation.1 | async-start | bytes 524288 | tf_op jit(solution)/shard_map/all_to_all | solution.py:481
  74.8 2.8 %shard_map.121.base_ref = f32[64,128,128]{2,1,0:T(8,128)} custom-call(f32[1,960,128]{2,1,0:T(8,128)S(1)} %collective-permute-done.4.pay_ref, bf16[64,192]{1,0:T(8,128)(2,1)S(1)} %copy-done.4, bf16[1152,512]{1,0:T(8,128)(2,1)S(1)} %copy-done.1, f32[64,128,128]{2,1,0:T(8,128)} %get-tuple-element.58.base_ref), custom_call_target="tpu_custom_call", output_to_operand_aliasing={{}: (3, {})} | custom-call | tf_op jit(solution)/shard_map/pallas_call | solution.py:311
  77.6 5.6 %all-to-all-done.1.band_ref = f32[16,32,128]{2,1,0:T(8,128)S(1)} async-done(((f32[16,32,128]{2,1,0:T(8,128)}), f32[16,32,128]{2,1,0:T(8,128)S(1)}, u32[]{:S(2)}, u32[]{:S(2)}) %all-to-all-start.1) | async-done | bytes 262176 | tf_op jit(solution)/shard_map/all_to_all | solution.py:481
  83.2 3.4 %shard_map.120 = f32[64,128,128]{2,1,0:T(8,128)} custom-call(f32[16,32,128]{2,1,0:T(8,128)S(1)} %all-to-all-done.1.band_ref, bf16[64,48]{1,0:T(8,128)(2,1)S(1)} %copy-done.6, bf16[384,512]{1,0:T(8,128)(2,1)S(1)} %copy-done.2), custom_call_target="tpu_custom_call" | custom-call | tf_op jit(solution)/shard_map/pallas_call | solution.py:311
  86.7 2.3 %collective-permute-done.5.pay_ref = f32[6,960,128]{2,1,0:T(8,128)} collective-permute-done((f32[6,960,128]{2,1,0:T(8,128)}, f32[6,960,128]{2,1,0:T(8,128)}, u32[]{:S(2)}, u32[]{:S(2)}) %collective-permute-start.5) | collective-permute-done | bytes 2949152 | tf_op jit(solution)/shard_map/ppermute | solution.py:456
  89.0 6.1 %shard_map.122.base_ref = f32[64,128,128]{2,1,0:T(8,128)} custom-call(f32[6,960,128]{2,1,0:T(8,128)} %collective-permute-done.5.pay_ref, bf16[64,192]{1,0:T(8,128)(2,1)S(1)} %copy-done.4, bf16[1152,512]{1,0:T(8,128)(2,1)S(1)} %copy-done.1, f32[64,128,128]{2,1,0:T(8,128)} %shard_map.121.base_ref), custom_call_target="tpu_custom_call", output_to_operand_aliasing={{}: (3, {})} | custom-call | tf_op jit(solution)/shard_map/pallas_call | solution.py:311
  95.1 2.7 %collective-permute-done.3.pay_ref = f32[1,960,128]{2,1,0:T(8,128)S(1)} collective-permute-done((f32[1,960,128]{2,1,0:T(8,128)S(1)}, f32[1,960,128]{2,1,0:T(8,128)S(1)}, u32[]{:S(2)}, u32[]{:S(2)}) %collective-permute-start.3) | collective-permute-done | bytes 491552 | tf_op jit(solution)/shard_map/ppermute | solution.py:456
  97.8 2.8 %shard_map.123 = f32[64,128,128]{2,1,0:T(8,128)} custom-call(f32[1,960,128]{2,1,0:T(8,128)S(1)} %collective-permute-done.3.pay_ref, bf16[64,192]{1,0:T(8,128)(2,1)S(1)} %copy-done.4, bf16[1152,512]{1,0:T(8,128)(2,1)S(1)} %copy-done.1, f32[64,128,128]{2,1,0:T(8,128)} %shard_map.122.base_ref), custom_call_target="tpu_custom_call", output_to_operand_aliasing={{}: (3, {})} | custom-call | tf_op jit(solution)/shard_map/pallas_call | solution.py:311
  (38 shorter events, 5.4 us)
Async XLA Ops:
  2.3 3.0 %copy-start = (bf16[1536,512]{1,0:T(8,128)(2,1)S(1)}, bf16[1536,512]{1,0:T(8,128)(2,1)}, u32[]{:S(2)}) copy-start(bf16[1536,512]{1,0:T(8,128)(2,1)} %constant.32.clone.lanes) | copy-start | bytes 4718596
  2.3 3.0 %copy-start.5 = (bf16[64,192]{1,0:T(8,128)(2,1)S(1)}, bf16[64,192]{1,0:T(8,128)(2,1)}, u32[]{:S(2)}) copy-start(bf16[64,192]{1,0:T(8,128)(2,1)} %constant.28.clone.rows) | copy-start | bytes 73732
  2.3 2.4 %collective-permute-start.1 = (f32[64,16,128]{2,1,0:T(8,128)S(1)}, f32[64,16,128]{2,1,0:T(8,128)S(1)}, u32[]{:S(2)}, u32[]{:S(2)}) collective-permute-start(f32[64,16,128]{2,1,0:T(8,128)S(1)} %shard_map.113), channel_id=1, source_target_pairs={{0,1},{1,0},{2,3},{3,2},{4,5},{5,4},{6,7},{7,6},{8,9},{9,8},{10,11... | collective-permute-start | bytes 1572872 | tf_op jit(solution)/shard_map/ppermute | solution.py:453
  4.8 5.9 %collective-permute-start.2 = (f32[64,96,128]{2,1,0:T(8,128)S(1)}, f32[64,96,128]{2,1,0:T(8,128)S(1)}, u32[]{:S(2)}, u32[]{:S(2)}) collective-permute-start(f32[64,96,128]{2,1,0:T(8,128)S(1)} %get-tuple-element.36), channel_id=1, source_target_pairs={{0,1},{1,0},{2,3},{3,2},{4,5},{5,4},{6,7},{7,6},{8,9},{9,8},{10,11... | collective-permute-start | bytes 9437192 | tf_op jit(solution)/shard_map/ppermute | solution.py:453
  8.0 13.5 %collective-permute-start.4 = (f32[1,960,128]{2,1,0:T(8,128)S(1)}, f32[1,960,128]{2,1,0:T(8,128)S(1)}, u32[]{:S(2)}, u32[]{:S(2)}) collective-permute-start(f32[1,960,128]{2,1,0:T(8,128)S(1)} %get-tuple-element.43), channel_id=1, source_target_pairs={{0,2},{1,3},{2,0},{3,1},{4,6},{5,7},{6,4},{7,5},{8,10},{9,11},{10,... | collective-permute-start | bytes 1474568 | tf_op jit(solution)/shard_map/ppermute | solution.py:456
  10.0 13.7 %collective-permute-start = (f32[64,16,128]{2,1,0:T(8,128)S(1)}, f32[64,16,128]{2,1,0:T(8,128)S(1)}, u32[]{:S(2)}, u32[]{:S(2)}) collective-permute-start(f32[64,16,128]{2,1,0:T(8,128)S(1)} %get-tuple-element.33), channel_id=1, source_target_pairs={{0,1},{1,0},{2,3},{3,2},{4,5},{5,4},{6,7},{7,6},{8,9},{9,8},{10,11... | collective-permute-start | bytes 1572872 | tf_op jit(solution)/shard_map/ppermute | solution.py:453
  21.5 67.5 %collective-permute-start.5 = (f32[6,960,128]{2,1,0:T(8,128)}, f32[6,960,128]{2,1,0:T(8,128)}, u32[]{:S(2)}, u32[]{:S(2)}) collective-permute-start(f32[6,960,128]{2,1,0:T(8,128)} %get-tuple-element.49), channel_id=1, source_target_pairs={{0,2},{1,3},{2,0},{3,1},{4,6},{5,7},{6,4},{7,5},{8,10},{9,11},{10,... | collective-permute-start | bytes 8847368 | tf_op jit(solution)/shard_map/ppermute | solution.py:456
  23.2 3.7 %collective-permute-start.6 = (f32[64,32,128]{2,1,0:T(8,128)S(1)}, f32[64,32,128]{2,1,0:T(8,128)S(1)}, u32[]{:S(2)}, u32[]{:S(2)}) collective-permute-start(f32[64,32,128]{2,1,0:T(8,128)S(1)} %get-tuple-element.50), channel_id=1, source_target_pairs={{0,1},{1,0},{2,3},{3,2},{4,5},{5,4},{6,7},{7,6},{8,9},{9,8},{10,11... | collective-permute-start | bytes 3145736 | tf_op jit(solution)/shard_map/ppermute | solution.py:453
  23.2 4.2 %collective-permute-start.7 = (f32[64,32,128]{2,1,0:T(8,128)S(1)}, f32[64,32,128]{2,1,0:T(8,128)S(1)}, u32[]{:S(2)}, u32[]{:S(2)}) collective-permute-start(f32[64,32,128]{2,1,0:T(8,128)S(1)} %get-tuple-element.51), channel_id=1, source_target_pairs={{0,1},{1,0},{2,3},{3,2},{4,5},{5,4},{6,7},{7,6},{8,9},{9,8},{10,11... | collective-permute-start | bytes 3145736 | tf_op jit(solution)/shard_map/ppermute | solution.py:453
  23.7 5.1 %collective-permute-start.8 = (f32[64,32,128]{2,1,0:T(8,128)S(1)}, f32[64,32,128]{2,1,0:T(8,128)S(1)}, u32[]{:S(2)}, u32[]{:S(2)}) collective-permute-start(f32[64,32,128]{2,1,0:T(8,128)S(1)} %get-tuple-element.52), channel_id=1, source_target_pairs={{0,1},{1,0},{2,3},{3,2},{4,5},{5,4},{6,7},{7,6},{8,9},{9,8},{10,11... | collective-permute-start | bytes 3145736 | tf_op jit(solution)/shard_map/ppermute | solution.py:453
  23.7 6.6 %collective-permute-start.9 = (f32[64,32,128]{2,1,0:T(8,128)S(1)}, f32[64,32,128]{2,1,0:T(8,128)S(1)}, u32[]{:S(2)}, u32[]{:S(2)}) collective-permute-start(f32[64,32,128]{2,1,0:T(8,128)S(1)} %get-tuple-element.53), channel_id=1, source_target_pairs={{0,1},{1,0},{2,3},{3,2},{4,5},{5,4},{6,7},{7,6},{8,9},{9,8},{10,11... | collective-permute-start | bytes 3145736 | tf_op jit(solution)/shard_map/ppermute | solution.py:453
  24.2 6.1 %copy-start.2 = (bf16[384,512]{1,0:T(8,128)(2,1)S(1)}, bf16[384,512]{1,0:T(8,128)(2,1)}, u32[]{:S(2)}) copy-start(bf16[384,512]{1,0:T(8,128)(2,1)} %constant.35.clone.refs_7_.band_back) | copy-start | bytes 1179652
  24.2 6.1 %copy-start.3 = (bf16[1536,128]{1,0:T(8,128)(2,1)S(1)}, bf16[1536,128]{1,0:T(8,128)(2,1)}, u32[]{:S(2)}) copy-start(bf16[1536,128]{1,0:T(8,128)(2,1)} %constant.34.clone.refs_6_) | copy-start | bytes 1179652
  24.2 6.1 %copy-start.6 = (bf16[64,48]{1,0:T(8,128)(2,1)S(1)}, bf16[64,48]{1,0:T(8,128)(2,1)}, u32[]{:S(2)}) copy-start(bf16[64,48]{1,0:T(8,128)(2,1)} %constant.31.clone.refs_5_.low_back) | copy-start | bytes 18436
  24.2 6.1 %copy-start.7 = (bf16[16,192]{1,0:T(8,128)(2,1)S(1)}, bf16[16,192]{1,0:T(8,128)(2,1)}, u32[]{:S(2)}) copy-start(bf16[16,192]{1,0:T(8,128)(2,1)} %constant.30.clone.refs_4_) | copy-start | bytes 18436
  30.4 44.4 %copy-start.1 = (bf16[1152,512]{1,0:T(8,128)(2,1)S(1)}, bf16[1152,512]{1,0:T(8,128)(2,1)}, u32[]{:S(2)}) copy-start(bf16[1152,512]{1,0:T(8,128)(2,1)} %constant.33.clone.kept_back) | copy-start | bytes 3538948
  30.4 44.4 %copy-start.4 = (bf16[64,192]{1,0:T(8,128)(2,1)S(1)}, bf16[64,192]{1,0:T(8,128)(2,1)}, u32[]{:S(2)}) copy-start(bf16[64,192]{1,0:T(8,128)(2,1)} %constant.29.clone.rows_back) | copy-start | bytes 73732
  58.6 5.9 %collective-permute-start.11 = (f32[32,128]{1,0:T(8,128)S(1)}, f32[32,128]{1,0:T(8,128)S(1)}, u32[]{:S(2)}, u32[]{:S(2)}) collective-permute-start(f32[32,128]{1,0:T(8,128)S(1)} %get-tuple-element.63), channel_id=1, source_target_pairs={{0,114},{1,115},{2,112},{3,113},{4,118},{5,119},{6,116},{7,117},{8... | collective-permute-start | bytes 49160 | tf_op jit(solution)/shard_map/ppermute | solution.py:478
  61.8 36.1 %collective-permute-start.3 = (f32[1,960,128]{2,1,0:T(8,128)S(1)}, f32[1,960,128]{2,1,0:T(8,128)S(1)}, u32[]{:S(2)}, u32[]{:S(2)}) collective-permute-start(f32[1,960,128]{2,1,0:T(8,128)S(1)} %get-tuple-element.40), channel_id=1, source_target_pairs={{0,2},{1,3},{2,0},{3,1},{4,6},{5,7},{6,4},{7,5},{8,10},{9,11},{10,... | collective-permute-start | bytes 1474568 | tf_op jit(solution)/shard_map/ppermute | solution.py:456
  62.8 7.1 %collective-permute-start.10 = (f32[32,128]{1,0:T(8,128)S(1)}, f32[32,128]{1,0:T(8,128)S(1)}, u32[]{:S(2)}, u32[]{:S(2)}) collective-permute-start(f32[32,128]{1,0:T(8,128)S(1)} %get-tuple-element.62), channel_id=1, source_target_pairs={{0,82},{1,83},{2,80},{3,81},{4,86},{5,87},{6,84},{7,85},{8,90},{9,... | collective-permute-start | bytes 49160 | tf_op jit(solution)/shard_map/ppermute | solution.py:477
  64.5 6.0 %collective-permute-start.12 = (f32[32,128]{1,0:T(8,128)S(1)}, f32[32,128]{1,0:T(8,128)S(1)}, u32[]{:S(2)}, u32[]{:S(2)}) collective-permute-start(f32[32,128]{1,0:T(8,128)S(1)} %fusion), channel_id=1, source_target_pairs={{0,18},{1,19},{2,16},{3,17},{4,22},{5,23},{6,20},{7,21},{8,26},{9,... | collective-permute-start | bytes 49160 | tf_op jit(solution)/shard_map/ppermute | solution.py:479
  71.2 12.0 %all-to-all-start.1 = ((f32[16,32,128]{2,1,0:T(8,128)}), f32[16,32,128]{2,1,0:T(8,128)S(1)}, u32[]{:S(2)}, u32[]{:S(2)}) async-start(f32[16,32,128]{2,1,0:T(8,128)} %broadcast_in_dim.2), calls=%async_computation.1 | async-start | bytes 524288 | tf_op jit(solution)/shard_map/all_to_all | solution.py:481

commit v3 on v2

--- a/solution.py
+++ b/solution.py
@@ -19,8 +19,10 @@
 HIGH = SPAN - BAND
 QUARTER = GROUP // 4 * BAND
 PAYLOAD = QUANTUM * HIGH + 3 * SPAN
+SPLIT = 48
 PLANE = 16
-VMEM = 46 * 1024 * 1024
+TURN = 4
+MOST = 46
 
 
 def dct(order):
@@ -106,6 +108,10 @@
 
 def quantum(k):
     return pl.ds(k * QUANTUM, QUANTUM)
+
+
+def band_at(k, shift):
+    return pl.ds(lax.rem(2 * k + PLANE - shift, PLANE), 2)
 
 
 def load(constants, buffers, sems):
@@ -133,115 +139,172 @@
         copy.wait()
 
 
-def encode_kernel(first, count, skip, slot, place, g_ref, r_ref, rows, lanes, *refs):
-    pay_ref, band_ref, g_buf, r_buf, pay_buf, band_buf, low_buf, rows_buf, lanes_buf, sems, const_sems = refs[-11:]
+def encode_kernel(first, counts, slot, place, g_ref, r_ref, rows, lanes, *refs):
+    pays, refs = refs[: len(counts)], refs[len(counts) :]
+    band_ref, g_buf, r_buf, pay_buf, band_buf, low_buf, zero_buf, rows_buf, lanes_buf, sems, more_sems = refs
     high = QUANTUM * HIGH
+    sent = sum(counts)
+    count = sent + 1
+    where = [(ref, j) for ref, n in zip(pays, counts) for j in range(n)]
+    turn = place[5]
 
     def into(k):
         yield pltpu.make_async_copy(g_ref.at[rows_of(place, slot), quantum(first + k), :], g_buf.at[k], sems.at[0, k])
-        yield pltpu.make_async_copy(r_ref.at[:, quantum(skip + k), :], r_buf.at[k], sems.at[1, k])
-
-    def out_high(k):
+        yield pltpu.make_async_copy(r_ref.at[:, quantum(k), :], r_buf.at[k], sems.at[1, k])
+
+    def out_high(k, ref, j):
         at = pl.ds(0, high)
-        return pltpu.make_async_copy(pay_buf.at[k, at], pay_ref.at[k, at], sems.at[2, k])
-
-    def out_low(k):
+        return pltpu.make_async_copy(pay_buf.at[k, at], ref.at[j, at], sems.at[2, k])
+
+    def out_low(k, ref, j):
         at = pl.ds(high, 3 * SPAN)
-        yield pltpu.make_async_copy(pay_buf.at[k, at], pay_ref.at[k, at], sems.at[3, k])
-        to = band_ref.at[pl.ds((first + k + PLANE // 2 - 2) % (PLANE // 2) * 2, 2), 1]
-        yield pltpu.make_async_copy(band_buf.at[k], to, sems.at[4, k])
-
+        return pltpu.make_async_copy(pay_buf.at[k, at], ref.at[j, at], sems.at[3, k])
+
+    def out_band(k):
+        return pltpu.make_async_copy(band_buf.at[k], band_ref.at[band_at(first + k, turn)], sems.at[4, k])
+
+    blank = pltpu.make_async_copy(zero_buf, band_ref.at[band_at(0, turn)], more_sems.at[2])
     for copy in into(0):
         copy.start()
-    consts = load((rows, lanes), (rows_buf, lanes_buf), const_sems)
+    consts = load((rows, lanes), (rows_buf, lanes_buf), more_sems)
     for k in range(1, count):
         for copy in into(k):
             copy.start()
+    zero_buf[...] = jnp.zeros_like(zero_buf)
+    blank.start()
     consts[0].wait()
 
-    def body(k, _):
+    def low_of(k, c, s):
+        low_buf[k, s * BAND : (s + 1) * BAND, :] = c[:BAND]
+
+    def cells_of(k):
         for copy in into(k):
             copy.wait()
-        for s, c in enumerate(forward(g_buf[k].astype(jnp.float32) + r_buf[k], rows_buf[...])):
-            low_buf[k, s * BAND : (s + 1) * BAND, :] = c[:BAND]
+        return g_buf[k].astype(jnp.float32) + r_buf[k]
+
+    def body(k, _):
+        for s, c in enumerate(forward(cells_of(k), rows_buf[...])):
+            low_of(k, c, s)
             for j in range(4):
                 at = (4 * s + j) * HIGH
                 pay_buf[k, at : at + HIGH, :] = c[BAND:, j * LANES : (j + 1) * LANES]
-        out_high(k).start()
+        for i, ref in enumerate(pays):
+            start = sum(counts[:i])
+
+            @pl.when((k >= start) & (k < start + counts[i]))
+            def _():
+                out_high(k, ref, k - start).start()
+
         return 0
 
-    lax.fori_loop(0, count, body, 0)
+    lax.fori_loop(0, sent, body, 0)
+    for k in range(sent, count):
+        for s, c in enumerate(forward(cells_of(k), rows_buf[:BAND, :])):
+            low_of(k, c, s)
     consts[1].wait()
     w = dot(long(low_buf[...].reshape(count * SPAN, 4 * LANES)), lanes_buf[...])
     for k in range(count):
         part = w[k * SPAN : (k + 1) * SPAN]
-        for i in range(3):
-            at = high + i * SPAN
-            pay_buf[k, at : at + SPAN, :] = part[:, i * LANES : (i + 1) * LANES]
+        if k < sent:
+            for i in range(3):
+                at = high + i * SPAN
+                pay_buf[k, at : at + SPAN, :] = part[:, i * LANES : (i + 1) * LANES]
+            out_low(k, *where[k]).start()
         band_buf[k] = part[:, 3 * LANES :].reshape(2, QUARTER, LANES)
-        for copy in out_low(k):
-            copy.start()
+        out_band(k).start()
     for k in range(count):
-        out_high(k).wait()
-        for copy in out_low(k):
-            copy.wait()
-
-
-def base_kernel(counts, slot, place, m_ref, g_ref, *refs):
+        if k < sent:
+            out_high(k, *where[k]).wait()
+            out_low(k, *where[k]).wait()
+        out_band(k).wait()
+    blank.wait()
+
+
+def base_kernel(counts, mine, theirs, place, m_ref, g_ref, early_ref, theirs_ref, *refs):
     received, refs = refs[: len(counts)], refs[len(counts) :]
-    constants, refs = refs[:4], refs[5:]
-    out_ref, band_ref, m_buf, g_buf, r_buf, out_buf, band_buf, low_buf = refs[:8]
-    buffers, (sems, const_sems) = refs[8:12], refs[12:]
+    constants, refs = refs[:4], refs[4:]
+    out_ref, top_ref, bottom_ref, band_ref = refs[:4]
+    m_buf, g_buf, r_buf, out_buf, band_buf, low_buf, early_buf = refs[4:11]
+    buffers, (sems, const_sems, more_sems) = refs[11:15], refs[15:]
     total = sum(counts)
-    where = [(r, j) for r, n in zip(received, counts) for j in range(n)]
+    where = [(r, j) for r, n in zip(received, counts) for j in range(n)] + [(theirs_ref, theirs_ref.shape[1] // QUANTUM - 1)]
+    split = top_ref.shape[0]
 
     def into(k, r=None, j=0):
-        yield pltpu.make_async_copy(m_ref.at[:, quantum(k), :], m_buf.at[k], sems.at[0, k])
-        yield pltpu.make_async_copy(g_ref.at[rows_of(place, slot), quantum(k), :], g_buf.at[k], sems.at[1, k])
-        r = received[0] if r is None else r
-        yield pltpu.make_async_copy(r.at[:, quantum(j), :], r_buf.at[k], sems.at[2, k])
+        r, slot, at = (received[0], mine, k) if r is None else (r, theirs if r is theirs_ref else mine, min(k, total - 1))
+        yield pltpu.make_async_copy(g_ref.at[rows_of(place, slot), quantum(at), :], g_buf.at[k], sems.at[0, k])
+        yield pltpu.make_async_copy(r.at[:, quantum(j), :], r_buf.at[k], sems.at[1, k])
+
+    def moment(k):
+        return pltpu.make_async_copy(m_ref.at[:, quantum(k), :], m_buf.at[k], sems.at[2, k])
 
     def out(k):
         return pltpu.make_async_copy(out_buf.at[k], out_ref.at[:, quantum(k), :], sems.at[3, k])
 
     def out_band(k):
-        return pltpu.make_async_copy(band_buf.at[k], band_ref.at[pl.ds(2 * k, 2), 0], sems.at[4, k])
-
-    for copy in into(0, *where[0]):
+        return pltpu.make_async_copy(band_buf.at[k], band_ref.at[band_at(k, place[4])], sems.at[4, k])
+
+    def out_last():
+        yield pltpu.make_async_copy(out_buf.at[total, pl.ds(0, split)], top_ref, more_sems.at[0])
+        yield pltpu.make_async_copy(out_buf.at[total, pl.ds(split, SPAN - split)], bottom_ref, more_sems.at[1])
+
+    early = pltpu.make_async_copy(early_ref, early_buf, more_sems.at[2])
+    for copy in (*into(0, *where[0]), moment(0), early):
         copy.start()
     consts = load(constants, buffers, const_sems)
-    for k in range(1, total):
+    for k in range(1, total + 1):
         for copy in into(k, *where[k]):
             copy.start()
+        if k < total:
+            moment(k).start()
     for copy in consts:
         copy.wait()
     low, low_back, band, band_back = buffers
 
-    def body(k, _):
-        for copy in into(k):
+    def cells_of(k, add):
+        for copy in into(k, *(where[k] if isinstance(k, int) else ())):
             copy.wait()
-        cells = DECAY * m_buf[k] + (g_buf[k].astype(jnp.float32) + r_buf[k])
+        cells = add(g_buf[k].astype(jnp.float32) + r_buf[k])
         m_buf[k] = cells
         for s, c in enumerate(forward(cells, low[...])):
             low_buf[k, s * BAND : (s + 1) * BAND, :] = c
+
+    def own_cells(k, more=None):
+        moment(k).wait()
+        decayed = DECAY * m_buf[k]
+        cells_of(k, lambda x: decayed + (x if more is None else x + more))
+
+    def body(k, _):
+        own_cells(k)
         return 0
 
-    lax.fori_loop(0, total, body, 0)
-    b = dot(long(low_buf[...].reshape(total * SPAN, 4 * LANES)), band[...])
-    band_buf[...] = b.reshape(total, 2, QUARTER, LANES)
+    early.wait()
+    own_cells(0, early_buf[...])
+    lax.fori_loop(1, total, body, 0)
+    cells_of(total, lambda x: x)
+    b = dot(long(low_buf[...].reshape((total + 1) * SPAN, 4 * LANES)), band[...])
+    band_buf[...] = b.reshape(total + 1, 2, QUARTER, LANES)
     for k in range(total):
         out_band(k).start()
-    low_buf[...] = dot(long(b), band_back[...]).reshape(total, SPAN, 4 * LANES)
+    low_buf[...] = dot(long(b), band_back[...]).reshape(total + 1, SPAN, 4 * LANES)
+
+    def without_band(k):
+        out_buf[k] = m_buf[k] - back(bands_of(low_buf[k]), low_back[...])
 
     def body_back(k, _):
-        out_buf[k] = m_buf[k] - back(bands_of(low_buf[k]), low_back[...])
+        without_band(k)
         out(k).start()
         return 0
 
+    without_band(total)
+    for copy in out_last():
+        copy.start()
     lax.fori_loop(0, total, body_back, 0)
     for k in range(total):
         out(k).wait()
         out_band(k).wait()
+    for copy in out_last():
+        copy.wait()
 
 
 def decode_kernel(first, count, pay_ref, rows_back, kept_back, base_ref, out_ref, *refs):
@@ -283,7 +346,23 @@
         out(k).wait()
 
 
-def update_kernel(scale, count, band_ref, low_back, band_back, out_ref, band_buf, low_rows, back_buf, out_buf, low_buf, sems, const_sems):
+def add_kernel(first, row, there_ref, base_ref, out_ref, there_buf, base_buf, sems):
+    at = (pl.ds(row, there_ref.shape[0]), quantum(first))
+    into = [
+        pltpu.make_async_copy(there_ref, there_buf, sems.at[0]),
+        pltpu.make_async_copy(base_ref.at[at], base_buf, sems.at[1]),
+    ]
+    for copy in into:
+        copy.start()
+    for copy in into:
+        copy.wait()
+    base_buf[...] += there_buf[...]
+    out = pltpu.make_async_copy(base_buf, out_ref.at[at], sems.at[2])
+    out.start()
+    out.wait()
+
+
+def update_kernel(scale, count, place, band_ref, low_back, band_back, out_ref, band_buf, low_rows, back_buf, out_buf, low_buf, sems, const_sems):
     for copy in load((band_ref, low_back, band_back), (band_buf, low_rows, back_buf), const_sems):
         copy.wait()
     b = band_buf[...].reshape(count * SPAN, LANES) * scale
@@ -293,7 +372,8 @@
         return pltpu.make_async_copy(out_buf.at[k], out_ref.at[:, quantum(k), :], sems.at[k])
 
     def body(k, _):
-        out_buf[k] = back(bands_of(low_buf[k]), low_rows[...])
+        turned = lax.rem(k + count - lax.div(place[4], 2), count)
+        out_buf[k] = back(bands_of(low_buf[turned]), low_rows[...])
         out(k).start()
         return 0
 
@@ -303,10 +383,10 @@
 
 
 ANY = pl.BlockSpec(memory_space=pl.ANY)
-BANDS = jax.ShapeDtypeStruct((PLANE, 2, QUARTER, LANES), jnp.float32)
-
-
-def call(kernel, place, operands, outs, scratch, aliases):
+BANDS = jax.ShapeDtypeStruct((PLANE, QUARTER, LANES), jnp.float32)
+
+
+def call(kernel, place, operands, outs, scratch, aliases, vmem):
     scalars = [] if place is None else [place]
     return pl.pallas_call(
         kernel,
@@ -320,7 +400,7 @@
         out_shape=outs,
         input_output_aliases=aliases,
         cost_estimate=pl.CostEstimate(flops=0, bytes_accessed=0, transcendentals=0),
-        compiler_params=pltpu.CompilerParams(vmem_limit_bytes=VMEM),
+        compiler_params=pltpu.CompilerParams(vmem_limit_bytes=vmem * 1024 * 1024),
     )(*scalars, *operands)
 
 
@@ -353,42 +433,59 @@
         [floats(SPAN, c * QUANTUM, LANES) for c in counts],
         held(n, jnp.bfloat16, jnp.float32) + [sems(2, n)],
         {},
+        MOST,
     )
 
 
-def encoded(place, g, received, skip, first, count, slot, mats, bands=None):
+def encoded(place, g, received, first, counts, slot, mats):
     values = [mats["rows"], mats["lanes"]]
-    more = [] if bands is None else [bands]
+    sent = sum(counts)
     return call(
-        functools.partial(encode_kernel, first, count, skip, slot),
+        functools.partial(encode_kernel, first, counts, slot),
         place,
-        [g, received, *values, *more],
-        [floats(count, PAYLOAD, LANES), BANDS],
-        held(count, jnp.bfloat16, jnp.float32)
-        + [pltpu.VMEM((count, PAYLOAD, LANES), jnp.float32), pltpu.VMEM((count, 2, QUARTER, LANES), jnp.float32)]
-        + lows(count)
+        [g, received, *values],
+        [floats(n, PAYLOAD, LANES) for n in counts] + [BANDS],
+        held(sent + 1, jnp.bfloat16, jnp.float32)
+        + [pltpu.VMEM((sent, PAYLOAD, LANES), jnp.float32), pltpu.VMEM((sent + 1, 2, QUARTER, LANES), jnp.float32)]
+        + lows(sent + 1)
+        + [pltpu.VMEM((2, QUARTER, LANES), jnp.float32)]
         + same(values)
-        + [sems(5, count), sems(2)],
-        {5: 1} if more else {},
+        + [sems(5, sent + 1), sems(3)],
+        {},
+        MOST,
     )
 
 
-def based(place, m, g, received, slot, mats, bands):
+def based(place, m, g, early, other, received, mine, theirs, mats):
     values = [mats[name] for name in ("low", "low_back", "band", "band_back")]
     counts = [r.shape[1] // QUANTUM for r in received]
-    n = sum(counts)
+    n = sum(counts) + 1
     return call(
-        functools.partial(base_kernel, counts, slot),
+        functools.partial(base_kernel, counts, mine, theirs),
         place,
-        [m, g, *received, *values, bands],
-        [floats(*m.shape), BANDS],
+        [m, g, early, other, *received, *values],
+        [floats(*m.shape), floats(SPLIT, QUANTUM, LANES), floats(SPAN - SPLIT, QUANTUM, LANES), BANDS],
         held(n, jnp.float32, jnp.bfloat16, jnp.float32, jnp.float32)
         + [pltpu.VMEM((n, 2, QUARTER, LANES), jnp.float32)]
         + lows(n)
+        + [pltpu.VMEM((SPAN, QUANTUM, LANES), jnp.float32)]
         + same(values)
-        + [sems(5, n), sems(4)],
-        {3 + len(received) + 4: 1},
+        + [sems(5, n), sems(4), sems(3)],
+        {},
+        MOST,
     )
+
+
+def added(there, base, first, row, mats):
+    return call(
+        functools.partial(add_kernel, first, row),
+        None,
+        [there, base],
+        [floats(*base.shape)],
+        same([there, there]) + [sems(3)],
+        {1: 0},
+        MOST,
+    )[0]
 
 
 def decoded(payload, base, first, mats):
@@ -405,19 +502,21 @@
         + same(values)
         + [sems(3, count), sems(2)],
         {3: 0},
+        MOST,
     )[0]
 
 
-def updated(band, scale, shape, mats):
+def updated(place, band, scale, shape, mats):
     values = [mats["low_back"], mats["band_back"]]
     count = shape[1] // QUANTUM
     return call(
         functools.partial(update_kernel, scale, count),
-        None,
+        place,
         [band, *values],
         [floats(*shape)],
         same([band, *values]) + held(count, jnp.float32) + lows(count) + [sems(count), sems(3)],
         {},
+        MOST,
     )[0]
 
 
@@ -445,7 +544,8 @@
     m = tiles(momentum[0])
     count = m.shape[1] // QUANTUM
     member = lax.axis_index("fsdp")
-    place = jnp.stack([member, member ^ 1, member ^ 2, member ^ 3]).astype(jnp.int32)
+    turn = lax.axis_index("rep") // PLANE * TURN
+    place = jnp.stack([member, member ^ 1, member ^ 2, member ^ 3, turn, TURN - turn]).astype(jnp.int32)
     over_core = [(f, f ^ 1) for f in range(4)]
     over_z = [(f, f ^ 2) for f in range(4)]
 
@@ -455,45 +555,52 @@
     def link(x):
         return lax.ppermute(x, "fsdp", over_z)
 
-    (cells,) = cast(place, g, 0, (1,), 3)
-    place1, cells = tie(place, cells)
-    more, last = cast(place1, g, 1, (6, 1), 3)
+    def head(slot):
+        return lax.dynamic_slice(g, (place[slot] * SPAN, 0, 0), (SPAN, QUANTUM, LANES)).astype(jnp.float32)
+
+    place1, cells = tie(place, head(3))
+    (more,) = cast(place1, g, 1, (count - 1,), 3)
     got, more = tie(core(cells), more)
-    pay0, bands = encoded(place, g, got, 0, 0, 1, 2, mats)
-    there0 = link(pay0)
-    pay1, bands = encoded(place, g, core(more), 0, 1, 6, 2, mats, bands)
-    place2, pay1 = tie(place1, pay1)
-    mine = cast(place2, g, 0, (2, 2, 2, 2), 1)
-    pay1, there0, *mine = tie(pay1, there0, *mine)
-    there1 = link(pay1)
-    pay2, bands = encoded(place, g, core(last), 0, 7, 1, 2, mats, bands)
-    there2 = link(pay2)
-    base, bands = based(place, m, g, [core(c) for c in mine], 0, mats, bands)
+    cells = head(2) + got
+    early = link(cells)
+    place2, cells = tie(place1, cells)
+    mine = cast(place2, g, 0, (2, 2, 2), 1)
+    got, *mine = tie(core(more), *mine)
+    *pays, other_band = encoded(place, g, got, 1, (4, 2), 2, mats)
+    theres = [link(pay) for pay in pays]
+    names = ("rep", "fsdp")
+    wrapped = lax.ppermute(other_band, names, steps(rep_count, 0, 2))
+    place3, early, _ = tie(place2, early, pays[0])
+    mine = [core(c) for c in [*mine, *cast(place3, g, 6, (2,), 1)]]
+    base, top, bottom, own_band = based(place, m, g, early, got, mine, 0, 2, mats)
+    top, bottom = link(top), link(bottom)
 
     groups = [[h * PLANE + i for i in range(PLANE)] for h in range(rep_count // PLANE)]
-    met = lax.all_to_all(bands, "rep", 0, 0, axis_index_groups=groups, tiled=True)
-    part = jnp.sum(met, axis=0)
-    names = ("rep", "fsdp")
-    own = part[0] + lax.ppermute(part[1], names, steps(rep_count, 1, 4, 2))
-    other = part[1] + lax.ppermute(part[0], names, steps(rep_count, 1, -4, 2))
-    total = own + lax.ppermute(other, names, steps(rep_count, 0, 4, 2))
+    met = lax.all_to_all(own_band + wrapped, "rep", 0, 0, axis_index_groups=groups, tiled=True)
+    part = jnp.sum(met.reshape(PLANE, QUARTER, LANES), axis=0)
+    total = part + lax.ppermute(part, names, steps(rep_count, TURN, 0))
     spread = jnp.broadcast_to(total[None], (PLANE,) + total.shape)
     band_total = lax.all_to_all(spread, "rep", 0, 0, axis_index_groups=groups, tiled=True)
-    update = updated(band_total, 1.0 / rep_count, m.shape, mats)
-
-    out = decoded(there0, base, 0, mats)
-    there1, update = tie(there1, update)
-    out = decoded(there1, out, 1, mats)
-    there2, out = tie(there2, out)
-    out = decoded(there2, out, 7, mats)
+    update = updated(place, band_total, 1.0 / rep_count, m.shape, mats)
+
+    theres[1], update = tie(theres[1], update)
+    out, first = base, 1
+    for there in theres:
+        there, out = tie(there, out)
+        out = decoded(there, out, first, mats)
+        first += there.shape[0]
+    top, out = tie(top, out)
+    out = added(top, out, count - 1, 0, mats)
+    bottom, out = tie(bottom, out)
+    out = added(bottom, out, count - 1, SPLIT, mats)
     return (untiles(out, mat_count)[None], untiles(update, mat_count))
 
 
-def steps(rep_count, z_hi, plane, member):
+def steps(rep_count, turn, member):
     pairs = []
     for rep in range(rep_count):
         high, low = divmod(rep, PLANE)
-        to = (high ^ z_hi) * PLANE + (low + plane) % PLANE
+        to = (high ^ 1) * PLANE + (low + (turn if high else PLANE - turn)) % PLANE
         pairs += [(rep * 4 + f, to * 4 + (f ^ member)) for f in range(4)]
     return pairs
 

time: 101 us -> 99.9 us (0.989)
  blocking collectives: 18.6 us -> 0 us
  starting transfers between devices: 13.3 us -> 26.2 us
  other arithmetic: 0.12 us -> 5.05 us
  waiting for transfers between devices: 25.2 us -> 22.2 us
  local copies, waits for them, and re-layouts: 0.78 us -> 2.86 us
    all_to_all x1 -> x0, blocking collectives: 18.6 us -> none  [per_device(): lax.all_to_all(bands, 'rep', 0, 0, axis_index_groups=groups, tiled=True)]
    all_to_all x0 -> x1, waiting for transfers between devices: none -> 7.79 us  [per_device(): lax.all_to_all(own_band + wrapped, 'rep', 0, 0, axis_index_groups=groups,...]
    all_to_all x0 -> x1, starting transfers between devices: none -> 7.06 us  [per_device(): lax.all_to_all(own_band + wrapped, 'rep', 0, 0, axis_index_groups=groups,...]
    ppermute x3 -> x5, waiting for transfers between devices: 7.86 us -> 1.43 us  [link(): return lax.ppermute(x, 'fsdp', over_z)]
    ppermute x3 -> x2, waiting for transfers between devices: 7.63 us -> 4.31 us  [the longest x1 4.3 us: per_device(): total = part + lax.ppermute(part, names, steps(rep_count, TURN, 0))]
    ppermute x7 -> x6, waiting for transfers between devices: 4.06 us -> 0.97 us  [core(): return lax.ppermute(x, 'fsdp', over_core)]
    ppermute x3 -> x2, starting transfers between devices: 3.23 us -> 6.19 us  [the longest x1 3.37 us: per_device(): total = part + lax.ppermute(part, names, steps(rep_count, TURN, 0))]
    add x2 -> x3, other arithmetic: 0.01 us -> 2.47 us  [the longest x1 1.01 us: per_device(): cells = head(2) + got]
  transfers between devices with their start and end apart: 14 -> 15, of which waited for: 11 -> 7; matrix products, arithmetic and copies ran while one was open for 1% -> 5% of each run, Pallas kernels for 37% -> 40%
where the time goes in v3:
time: 99.9 us; the launch traced here: 98.7 us
  Pallas kernels  41.6 us (42%)
  starting transfers between devices  26.2 us (26%)
  waiting for transfers between devices  22.2 us (22%)
  other arithmetic  5.05 us (5%)
  local copies, waits for them, and re-layouts  2.86 us (3%)
    pallas_call x10, Pallas kernels, call(): pl.pallas_call(kernel, grid_spec=pltpu.PrefetchScalarGridSpec(num_scalar_...  41.6 us
    all_to_all x1, waiting for transfers between devices, per_device(): lax.all_to_all(own_band + wrapped, 'rep', 0, 0, axis_index_groups=groups,...  7.79 us
    all_to_all x1, waiting for transfers between devices, per_device(): lax.all_to_all(spread, 'rep', 0, 0, axis_index_groups=groups, tiled=True)  7.69 us
    ppermute x5, starting transfers between devices, link(): return lax.ppermute(x, 'fsdp', over_z)  7.16 us
    all_to_all x1, starting transfers between devices, per_device(): lax.all_to_all(own_band + wrapped, 'rep', 0, 0, axis_index_groups=groups,...  7.06 us
    ppermute x1, waiting for transfers between devices, per_device(): total = part + lax.ppermute(part, names, steps(rep_count, TURN, 0))  4.3 us
    all_to_all x1, starting transfers between devices, per_device(): lax.all_to_all(spread, 'rep', 0, 0, axis_index_groups=groups, tiled=True)  4.2 us
    ppermute x1, starting transfers between devices, per_device(): total = part + lax.ppermute(part, names, steps(rep_count, TURN, 0))  3.37 us
  transfers between devices with their start and end apart: 15, of which 7 were waited for; matrix products, arithmetic and copies ran while one was open for 5% of the time, Pallas kernels for 40%

profile of v3, /device:TPU:0, one launch (start us, length us, event | category | flops | bytes accessed | tf_op | source)
XLA Modules:
  0.0 98.7 jit_solution(10584296847718024518)
XLA Ops:
  0.7 1.0 %dynamic-slice_convert_fusion = f32[64,16,128]{2,1,0:T(8,128)S(1)} fusion(bf16[256,128,128]{2,1,0:T(8,128)(2,1)} %bitcast.26, s32[]{:T(128)S(6)} %select_n.12), kind=kLoop, calls=%fused_computation.1 | loop fusion | flops 131072 | bytes 786436 | tf_op jit(solution)/shard_map/convert_element_type | solution.py:559
  1.8 3.5 %shard_map.113 = f32[64,112,128]{2,1,0:T(8,128)} custom-call(s32[6]{0:T(128)S(1)} %stack.27.place, bf16[256,128,128]{2,1,0:T(8,128)(2,1)} %bitcast.27), custom_call_target="tpu_custom_call" | custom-call | tf_op jit(solution)/shard_map/pallas_call | solution.py:391
  5.9 1.0 %convert_add_fusion = f32[64,16,128]{2,1,0:T(8,128)S(1)} fusion(f32[64,16,128]{2,1,0:T(8,128)S(1)} %collective-permute-done, bf16[256,128,128]{2,1,0:T(8,128)(2,1)} %bitcast.28, s32[]{:T(128)S(6)} %select_n.13), kind=kLoop, calls=%fused_computation | loop fusion | flops 262144 | bytes 1310724 | tf_op jit(solution)/shard_map/add | solution.py:564
  6.9 2.1 %collective-permute-start.1 = (f32[64,16,128]{2,1,0:T(8,128)S(1)}, f32[64,16,128]{2,1,0:T(8,128)S(1)}, u32[]{:S(2)}, u32[]{:S(2)}) collective-permute-start(f32[64,16,128]{2,1,0:T(8,128)S(1)} %convert_add_fusion), channel_id=1, source_target_pairs={{0,2},{1,3},{2,0},{3,1},{4,6},{5,7},{6,4},{7,5},{8,10},{9,11},{10,... | collective-permute-start | bytes 1572872 | tf_op jit(solution)/shard_map/ppermute | solution.py:556
  9.0 2.3 %shard_map.114 = (f32[64,32,128]{2,1,0:T(8,128)S(1)}, f32[64,32,128]{2,1,0:T(8,128)S(1)}, f32[64,32,128]{2,1,0:T(8,128)S(1)}) custom-call(s32[6]{0:T(128)S(1)} %stack.27.place, bf16[256,128,128]{2,1,0:T(8,128)(2,1)} %bitcast.29), custom_call_target="tpu_custom_call" | custom-call | tf_op jit(solution)/shard_map/pallas_call | solution.py:391
  12.6 6.2 %shard_map.115 = (f32[4,960,128]{2,1,0:T(8,128)}, f32[2,960,128]{2,1,0:T(8,128)}, f32[16,32,128]{2,1,0:T(8,128)S(1)}) custom-call(s32[6]{0:T(128)S(1)} %stack.27.place, bf16[256,128,128]{2,1,0:T(8,128)(2,1)} %bitcast.30, f32[64,112,128]{2,1,0:T(8,128)} %collective-permute-done.2.r_ref.theirs_ref, bf16[64,192]{1,0:T(8,128)(2,1)S(1)} %copy-done.6, ...), custom_call_target="tpu_custom_call" | custom-call | tf_op jit(solution)/shard_map/pallas_call | solution.py:391
  18.9 2.1 %collective-permute-start.12 = (f32[4,960,128]{2,1,0:T(8,128)}, f32[4,960,128]{2,1,0:T(8,128)S(1)}, u32[]{:S(2)}, u32[]{:S(2)}) collective-permute-start(f32[4,960,128]{2,1,0:T(8,128)} %get-tuple-element.42), channel_id=1, source_target_pairs={{0,2},{1,3},{2,0},{3,1},{4,6},{5,7},{6,4},{7,5},{8,10},{9,11},{10,... | collective-permute-start | bytes 5898248 | tf_op jit(solution)/shard_map/ppermute | solution.py:556
  21.5 1.8 %shard_map.116 = f32[64,32,128]{2,1,0:T(8,128)S(1)} custom-call(s32[6]{0:T(128)S(1)} %stack.27.place, bf16[256,128,128]{2,1,0:T(8,128)(2,1)} %bitcast.31), custom_call_target="tpu_custom_call" | custom-call | tf_op jit(solution)/shard_map/pallas_call | solution.py:391
  23.4 1.4 %collective-permute-start.9 = (f32[2,960,128]{2,1,0:T(8,128)}, f32[2,960,128]{2,1,0:T(8,128)}, u32[]{:S(2)}, u32[]{:S(2)}) collective-permute-start(f32[2,960,128]{2,1,0:T(8,128)} %get-tuple-element.50), channel_id=1, source_target_pairs={{0,2},{1,3},{2,0},{3,1},{4,6},{5,7},{6,4},{7,5},{8,10},{9,11},{10,... | collective-permute-start | bytes 2949128 | tf_op jit(solution)/shard_map/ppermute | solution.py:556
  24.8 2.8 %collective-permute-start.10 = (f32[16,32,128]{2,1,0:T(8,128)S(1)}, f32[16,32,128]{2,1,0:T(8,128)S(1)}, u32[]{:S(2)}, u32[]{:S(2)}) collective-permute-start(f32[16,32,128]{2,1,0:T(8,128)S(1)} %get-tuple-element.52), channel_id=1, source_target_pairs={{0,66},{1,67},{2,64},{3,65},{4,70},{5,71},{6,68},{7,69},{8,74},{9,... | collective-permute-start | bytes 786440 | tf_op jit(solution)/shard_map/ppermute | solution.py:572
  27.7 11.2 %shard_map.117 = (f32[64,128,128]{2,1,0:T(8,128)}, f32[48,16,128]{2,1,0:T(8,128)S(1)}, f32[16,16,128]{2,1,0:T(8,128)S(1)}, f32[16,32,128]{2,1,0:T(8,128)S(1)}) custom-call(s32[6]{0:T(128)S(1)} %stack.27.place, f32[64,128,128]{2,1,0:T(8,128)} %bitcast.34, bf16[256,128,128]{2,1,0:T(8,128)(2,1)} %bitcast.32, ...), custom_call_target="tpu_custom_call" | custom-call | tf_op jit(solution)/shard_map/pallas_call | solution.py:391
  41.0 7.1 %all-to-all-start = ((f32[16,32,128]{2,1,0:T(8,128)}), f32[16,32,128]{2,1,0:T(8,128)}, u32[]{:S(2)}, u32[]{:S(2)}) async-start(f32[16,32,128]{2,1,0:T(8,128)} %add.19), calls=%async_computation | async-start | bytes 524288 | tf_op jit(solution)/shard_map/all_to_all | solution.py:579
  48.9 7.8 %all-to-all-done = f32[16,32,128]{2,1,0:T(8,128)} async-done(((f32[16,32,128]{2,1,0:T(8,128)}), f32[16,32,128]{2,1,0:T(8,128)}, u32[]{:S(2)}, u32[]{:S(2)}) %all-to-all-start) | async-done | bytes 262176 | tf_op jit(solution)/shard_map/all_to_all | solution.py:579
  56.6 1.6 %reduce_sum.9 = f32[32,128]{1,0:T(8,128)} reduce(f32[16,32,128]{2,1,0:T(8,128)} %all-to-all-done, f32[]{:T(128)} %constant.53.clone.1), dimensions={0}, to_apply=%region_0.1 | reduce | flops 61440 | bytes 278532 | tf_op jit(solution)/shard_map/reduce_sum | solution.py:580
  58.2 3.4 %collective-permute-start.11 = (f32[32,128]{1,0:T(8,128)}, f32[32,128]{1,0:T(8,128)S(1)}, u32[]{:S(2)}, u32[]{:S(2)}) collective-permute-start(f32[32,128]{1,0:T(8,128)} %reduce_sum.9), channel_id=1, source_target_pairs={{0,112},{1,113},{2,114},{3,115},{4,116},{5,117},{6,118},{7,119},{8... | collective-permute-start | bytes 49160 | tf_op jit(solution)/shard_map/ppermute | solution.py:581
  61.6 4.3 %collective-permute-done.11 = f32[32,128]{1,0:T(8,128)S(1)} collective-permute-done((f32[32,128]{1,0:T(8,128)}, f32[32,128]{1,0:T(8,128)S(1)}, u32[]{:S(2)}, u32[]{:S(2)}) %collective-permute-start.11) | collective-permute-done | bytes 16416 | tf_op jit(solution)/shard_map/ppermute | solution.py:581
  67.4 4.2 %all-to-all-start.1 = ((f32[16,32,128]{2,1,0:T(8,128)}), f32[16,32,128]{2,1,0:T(8,128)}, u32[]{:S(2)}, u32[]{:S(2)}) async-start(f32[16,32,128]{2,1,0:T(8,128)} %broadcast_in_dim.2), calls=%async_computation.1 | async-start | bytes 524288 | tf_op jit(solution)/shard_map/all_to_all | solution.py:583
  72.4 7.7 %all-to-all-done.1.band_ref = f32[16,32,128]{2,1,0:T(8,128)} async-done(((f32[16,32,128]{2,1,0:T(8,128)}), f32[16,32,128]{2,1,0:T(8,128)}, u32[]{:S(2)}, u32[]{:S(2)}) %all-to-all-start.1) | async-done | bytes 262176 | tf_op jit(solution)/shard_map/all_to_all | solution.py:583
  80.7 4.7 %shard_map.118 = f32[64,128,128]{2,1,0:T(8,128)} custom-call(s32[6]{0:T(128)S(1)} %copy-done.8, f32[16,32,128]{2,1,0:T(8,128)} %all-to-all-done.1.band_ref, bf16[64,48]{1,0:T(8,128)(2,1)S(1)} %copy-done.5, bf16[384,512]{1,0:T(8,128)(2,1)S(1)} %copy-done.2), custom_call_target="tpu_custom_call" | custom-call | tf_op jit(solution)/shard_map/pallas_call | solution.py:391
  85.4 1.0 collective-permute-done.9.pay_ref
  86.4 5.0 %shard_map.119.base_ref = f32[64,128,128]{2,1,0:T(8,128)} custom-call(f32[4,960,128]{2,1,0:T(8,128)S(1)} %collective-permute-done.12.pay_ref, bf16[64,192]{1,0:T(8,128)(2,1)S(1)} %copy-done.4, bf16[1152,512]{1,0:T(8,128)(2,1)S(1)} %copy-done, f32[64,128,128]{2,1,0:T(8,128)} %get-tuple-element.56.base_ref), custom_call_target="tpu_custom_call", output_to_operand_aliasing={{}: (3, {})} | custom-call | tf_op jit(solution)/shard_map/pallas_call | solution.py:391
  91.4 3.3 %shard_map.120.base_ref = f32[64,128,128]{2,1,0:T(8,128)} custom-call(f32[2,960,128]{2,1,0:T(8,128)} %collective-permute-done.9.pay_ref, bf16[64,192]{1,0:T(8,128)(2,1)S(1)} %copy-done.4, bf16[1152,512]{1,0:T(8,128)(2,1)S(1)} %copy-done, f32[64,128,128]{2,1,0:T(8,128)} %shard_map.119.base_ref), custom_call_target="tpu_custom_call", output_to_operand_aliasing={{}: (3, {})} | custom-call | tf_op jit(solution)/shard_map/pallas_call | solution.py:391
  94.8 1.9 %shard_map.121.base_ref = f32[64,128,128]{2,1,0:T(8,128)} custom-call(f32[48,16,128]{2,1,0:T(8,128)} %collective-permute-done.8.there_ref, f32[64,128,128]{2,1,0:T(8,128)} %shard_map.120.base_ref), custom_call_target="tpu_custom_call", output_to_operand_aliasing={{}: (1, {})} | custom-call | tf_op jit(solution)/shard_map/pallas_call | solution.py:391
  97.1 1.7 %shard_map.122 = f32[64,128,128]{2,1,0:T(8,128)} custom-call(f32[16,16,128]{2,1,0:T(8,128)} %collective-permute-done.7.there_ref, f32[64,128,128]{2,1,0:T(8,128)} %shard_map.121.base_ref), custom_call_target="tpu_custom_call", output_to_operand_aliasing={{}: (1, {})} | custom-call | tf_op jit(solution)/shard_map/pallas_call | solution.py:391
  (47 shorter events, 8.9 us)
Async XLA Ops:
  1.7 25.9 %copy-start.7 = (s32[6]{0:T(128)}, s32[6]{0:T(128)S(1)}, u32[]{:S(2)}) copy-start(s32[6]{0:T(128)S(1)} %stack.27.place) | copy-start | bytes 76
  1.7 3.5 %collective-permute-start = (f32[64,16,128]{2,1,0:T(8,128)S(1)}, f32[64,16,128]{2,1,0:T(8,128)S(1)}, u32[]{:S(2)}, u32[]{:S(2)}) collective-permute-start(f32[64,16,128]{2,1,0:T(8,128)S(1)} %dynamic-slice_convert_fusion), channel_id=1, source_target_pairs={{0,1},{1,0},{2,3},{3,2},{4,5},{5,4},{6,7},{7,6},{8,9},{9,8},{10,11... | collective-permute-start | bytes 1572872 | tf_op jit(solution)/shard_map/ppermute | solution.py:553
  5.3 7.0 %collective-permute-start.2 = (f32[64,112,128]{2,1,0:T(8,128)}, f32[64,112,128]{2,1,0:T(8,128)}, u32[]{:S(2)}, u32[]{:S(2)}) collective-permute-start(f32[64,112,128]{2,1,0:T(8,128)} %shard_map.113), channel_id=1, source_target_pairs={{0,1},{1,0},{2,3},{3,2},{4,5},{5,4},{6,7},{7,6},{8,9},{9,8},{10,11... | collective-permute-start | bytes 11010056 | tf_op jit(solution)/shard_map/ppermute | solution.py:553
  6.9 5.7 %copy-start.1 = (bf16[1536,512]{1,0:T(8,128)(2,1)S(1)}, bf16[1536,512]{1,0:T(8,128)(2,1)}, u32[]{:S(2)}) copy-start(bf16[1536,512]{1,0:T(8,128)(2,1)} %constant.58.clone.lanes) | copy-start | bytes 4718596
  6.9 5.7 %copy-start.6 = (bf16[64,192]{1,0:T(8,128)(2,1)S(1)}, bf16[64,192]{1,0:T(8,128)(2,1)}, u32[]{:S(2)}) copy-start(bf16[64,192]{1,0:T(8,128)(2,1)} %constant.54.clone.rows) | copy-start | bytes 73732
  6.9 14.6 %collective-permute-start.1 = (f32[64,16,128]{2,1,0:T(8,128)S(1)}, f32[64,16,128]{2,1,0:T(8,128)S(1)}, u32[]{:S(2)}, u32[]{:S(2)}) collective-permute-start(f32[64,16,128]{2,1,0:T(8,128)S(1)} %convert_add_fusion), channel_id=1, source_target_pairs={{0,2},{1,3},{2,0},{3,1},{4,6},{5,7},{6,4},{7,5},{8,10},{9,11},{10,... | collective-permute-start | bytes 1572872 | tf_op jit(solution)/shard_map/ppermute | solution.py:556
  12.2 11.1 %collective-permute-start.3 = (f32[64,32,128]{2,1,0:T(8,128)S(1)}, f32[64,32,128]{2,1,0:T(8,128)S(1)}, u32[]{:S(2)}, u32[]{:S(2)}) collective-permute-start(f32[64,32,128]{2,1,0:T(8,128)S(1)} %get-tuple-element.44), channel_id=1, source_target_pairs={{0,1},{1,0},{2,3},{3,2},{4,5},{5,4},{6,7},{7,6},{8,9},{9,8},{10,11... | collective-permute-start | bytes 3145736 | tf_op jit(solution)/shard_map/ppermute | solution.py:553
  18.9 8.8 %copy-start.2 = (bf16[384,512]{1,0:T(8,128)(2,1)S(1)}, bf16[384,512]{1,0:T(8,128)(2,1)}, u32[]{:S(2)}) copy-start(bf16[384,512]{1,0:T(8,128)(2,1)} %constant.61.clone.refs_7_.band_back) | copy-start | bytes 1179652
  18.9 8.8 %copy-start.3 = (bf16[1536,128]{1,0:T(8,128)(2,1)S(1)}, bf16[1536,128]{1,0:T(8,128)(2,1)}, u32[]{:S(2)}) copy-start(bf16[1536,128]{1,0:T(8,128)(2,1)} %constant.60.clone.refs_6_) | copy-start | bytes 1179652
  18.9 8.8 %copy-start.5 = (bf16[64,48]{1,0:T(8,128)(2,1)S(1)}, bf16[64,48]{1,0:T(8,128)(2,1)}, u32[]{:S(2)}) copy-start(bf16[64,48]{1,0:T(8,128)(2,1)} %constant.57.clone.refs_5_.low_back) | copy-start | bytes 18436
  18.9 8.8 %copy-start.9 = (bf16[16,192]{1,0:T(8,128)(2,1)S(1)}, bf16[16,192]{1,0:T(8,128)(2,1)}, u32[]{:S(2)}) copy-start(bf16[16,192]{1,0:T(8,128)(2,1)} %constant.56.clone.refs_4_) | copy-start | bytes 18436
  18.9 67.4 %collective-permute-start.12 = (f32[4,960,128]{2,1,0:T(8,128)}, f32[4,960,128]{2,1,0:T(8,128)S(1)}, u32[]{:S(2)}, u32[]{:S(2)}) collective-permute-start(f32[4,960,128]{2,1,0:T(8,128)} %get-tuple-element.42), channel_id=1, source_target_pairs={{0,2},{1,3},{2,0},{3,1},{4,6},{5,7},{6,4},{7,5},{8,10},{9,11},{10,... | collective-permute-start | bytes 5898248 | tf_op jit(solution)/shard_map/ppermute | solution.py:556
  21.0 3.8 %collective-permute-start.4 = (f32[64,32,128]{2,1,0:T(8,128)S(1)}, f32[64,32,128]{2,1,0:T(8,128)S(1)}, u32[]{:S(2)}, u32[]{:S(2)}) collective-permute-start(f32[64,32,128]{2,1,0:T(8,128)S(1)} %get-tuple-element.45), channel_id=1, source_target_pairs={{0,1},{1,0},{2,3},{3,2},{4,5},{5,4},{6,7},{7,6},{8,9},{9,8},{10,11... | collective-permute-start | bytes 3145736 | tf_op jit(solution)/shard_map/ppermute | solution.py:553
  21.0 6.6 %collective-permute-start.5 = (f32[64,32,128]{2,1,0:T(8,128)S(1)}, f32[64,32,128]{2,1,0:T(8,128)S(1)}, u32[]{:S(2)}, u32[]{:S(2)}) collective-permute-start(f32[64,32,128]{2,1,0:T(8,128)S(1)} %get-tuple-element.46), channel_id=1, source_target_pairs={{0,1},{1,0},{2,3},{3,2},{4,5},{5,4},{6,7},{7,6},{8,9},{9,8},{10,11... | collective-permute-start | bytes 3145736 | tf_op jit(solution)/shard_map/ppermute | solution.py:553
  23.3 4.3 %collective-permute-start.6 = (f32[64,32,128]{2,1,0:T(8,128)S(1)}, f32[64,32,128]{2,1,0:T(8,128)S(1)}, u32[]{:S(2)}, u32[]{:S(2)}) collective-permute-start(f32[64,32,128]{2,1,0:T(8,128)S(1)} %shard_map.116), channel_id=1, source_target_pairs={{0,1},{1,0},{2,3},{3,2},{4,5},{5,4},{6,7},{7,6},{8,9},{9,8},{10,11... | collective-permute-start | bytes 3145736 | tf_op jit(solution)/shard_map/ppermute | solution.py:553
  23.4 63.0 %collective-permute-start.9 = (f32[2,960,128]{2,1,0:T(8,128)}, f32[2,960,128]{2,1,0:T(8,128)}, u32[]{:S(2)}, u32[]{:S(2)}) collective-permute-start(f32[2,960,128]{2,1,0:T(8,128)} %get-tuple-element.50), channel_id=1, source_target_pairs={{0,2},{1,3},{2,0},{3,1},{4,6},{5,7},{6,4},{7,5},{8,10},{9,11},{10,... | collective-permute-start | bytes 2949128 | tf_op jit(solution)/shard_map/ppermute | solution.py:556
  24.8 15.5 %collective-permute-start.10 = (f32[16,32,128]{2,1,0:T(8,128)S(1)}, f32[16,32,128]{2,1,0:T(8,128)S(1)}, u32[]{:S(2)}, u32[]{:S(2)}) collective-permute-start(f32[16,32,128]{2,1,0:T(8,128)S(1)} %get-tuple-element.52), channel_id=1, source_target_pairs={{0,66},{1,67},{2,64},{3,65},{4,70},{5,71},{6,68},{7,69},{8,74},{9,... | collective-permute-start | bytes 786440 | tf_op jit(solution)/shard_map/ppermute | solution.py:572
  40.3 46.1 %copy-start = (bf16[1152,512]{1,0:T(8,128)(2,1)S(1)}, bf16[1152,512]{1,0:T(8,128)(2,1)}, u32[]{:S(2)}) copy-start(bf16[1152,512]{1,0:T(8,128)(2,1)} %constant.59.clone.kept_back) | copy-start | bytes 3538948
  41.0 15.7 %all-to-all-start = ((f32[16,32,128]{2,1,0:T(8,128)}), f32[16,32,128]{2,1,0:T(8,128)}, u32[]{:S(2)}, u32[]{:S(2)}) async-start(f32[16,32,128]{2,1,0:T(8,128)} %add.19), calls=%async_computation | async-start | bytes 524288 | tf_op jit(solution)/shard_map/all_to_all | solution.py:579
  48.1 46.7 %collective-permute-start.8 = (f32[48,16,128]{2,1,0:T(8,128)}, f32[48,16,128]{2,1,0:T(8,128)}, u32[]{:S(2)}, u32[]{:S(2)}) collective-permute-start(f32[48,16,128]{2,1,0:T(8,128)} %copy-done.10), channel_id=1, source_target_pairs={{0,2},{1,3},{2,0},{3,1},{4,6},{5,7},{6,4},{7,5},{8,10},{9,11},{10,... | collective-permute-start | bytes 1179656 | tf_op jit(solution)/shard_map/ppermute | solution.py:556
  58.2 7.7 %collective-permute-start.11 = (f32[32,128]{1,0:T(8,128)}, f32[32,128]{1,0:T(8,128)S(1)}, u32[]{:S(2)}, u32[]{:S(2)}) collective-permute-start(f32[32,128]{1,0:T(8,128)} %reduce_sum.9), channel_id=1, source_target_pairs={{0,112},{1,113},{2,114},{3,115},{4,116},{5,117},{6,118},{7,119},{8... | collective-permute-start | bytes 49160 | tf_op jit(solution)/shard_map/ppermute | solution.py:581
  67.4 12.7 %all-to-all-start.1 = ((f32[16,32,128]{2,1,0:T(8,128)}), f32[16,32,128]{2,1,0:T(8,128)}, u32[]{:S(2)}, u32[]{:S(2)}) async-start(f32[16,32,128]{2,1,0:T(8,128)} %broadcast_in_dim.2), calls=%async_computation.1 | async-start | bytes 524288 | tf_op jit(solution)/shard_map/all_to_all | solution.py:583
  71.6 25.5 %collective-permute-start.7 = (f32[16,16,128]{2,1,0:T(8,128)}, f32[16,16,128]{2,1,0:T(8,128)}, u32[]{:S(2)}, u32[]{:S(2)}) collective-permute-start(f32[16,16,128]{2,1,0:T(8,128)} %copy-done.11), channel_id=1, source_target_pairs={{0,2},{1,3},{2,0},{3,1},{4,6},{5,7},{6,4},{7,5},{8,10},{9,11},{10,... | collective-permute-start | bytes 393224 | tf_op jit(solution)/shard_map/ppermute | solution.py:556
  80.7 5.7 %copy-start.4 = (bf16[64,192]{1,0:T(8,128)(2,1)S(1)}, bf16[64,192]{1,0:T(8,128)(2,1)}, u32[]{:S(2)}) copy-start(bf16[64,192]{1,0:T(8,128)(2,1)} %constant.55.clone.rows_back) | copy-start | bytes 73732
  (3 other events, 2.0 us)

commit v4 on v3

--- a/solution.py
+++ b/solution.py
@@ -19,6 +19,7 @@
 HIGH = SPAN - BAND
 QUARTER = GROUP // 4 * BAND
 PAYLOAD = QUANTUM * HIGH + 3 * SPAN
+SECOND = 4
 SPLIT = 48
 PLANE = 16
 TURN = 4
@@ -121,13 +122,13 @@
     return copies
 
 
-def cast_kernel(first, counts, slot, place, g_ref, *refs):
-    outs, (held, cells, sems) = refs[: len(counts)], refs[len(counts) :]
+def cast_kernel(wanted, place, g_ref, *refs):
+    outs, (held, cells, sems) = refs[: len(wanted)], refs[len(wanted) :]
     into, out = [], []
-    for o, n in zip(outs, counts):
+    for o, (slot, first, n) in zip(outs, wanted):
         for j in range(n):
             k = len(into)
-            source = g_ref.at[rows_of(place, slot), quantum(first + k), :]
+            source = g_ref.at[rows_of(place, slot), quantum(first + j), :]
             into.append(pltpu.make_async_copy(source, held.at[k], sems.at[0, k]))
             out.append(pltpu.make_async_copy(cells.at[k], o.at[:, quantum(j), :], sems.at[1, k]))
             into[-1].start()
@@ -139,18 +140,22 @@
         copy.wait()
 
 
-def encode_kernel(first, counts, slot, place, g_ref, r_ref, rows, lanes, *refs):
+def encode_kernel(first, counts, extra, slot, received, place, g_ref, *refs):
+    come = [(ref, j) for ref, n in zip(refs, received) for j in range(n)]
+    rows, lanes, *refs = refs[len(received) :]
+    refs = refs[extra:]
     pays, refs = refs[: len(counts)], refs[len(counts) :]
     band_ref, g_buf, r_buf, pay_buf, band_buf, low_buf, zero_buf, rows_buf, lanes_buf, sems, more_sems = refs
     high = QUANTUM * HIGH
     sent = sum(counts)
-    count = sent + 1
+    count = sent + extra
     where = [(ref, j) for ref, n in zip(pays, counts) for j in range(n)]
     turn = place[5]
 
-    def into(k):
+    def into(k, ref=None, j=0):
+        ref = come[0][0] if ref is None else ref
         yield pltpu.make_async_copy(g_ref.at[rows_of(place, slot), quantum(first + k), :], g_buf.at[k], sems.at[0, k])
-        yield pltpu.make_async_copy(r_ref.at[:, quantum(k), :], r_buf.at[k], sems.at[1, k])
+        yield pltpu.make_async_copy(ref.at[:, quantum(j), :], r_buf.at[k], sems.at[1, k])
 
     def out_high(k, ref, j):
         at = pl.ds(0, high)
@@ -163,15 +168,17 @@
     def out_band(k):
         return pltpu.make_async_copy(band_buf.at[k], band_ref.at[band_at(first + k, turn)], sems.at[4, k])
 
-    blank = pltpu.make_async_copy(zero_buf, band_ref.at[band_at(0, turn)], more_sems.at[2])
-    for copy in into(0):
+    if not extra:
+        blank = pltpu.make_async_copy(zero_buf, band_ref.at[band_at(0, turn)], more_sems.at[2])
+    for copy in into(0, *come[0]):
         copy.start()
     consts = load((rows, lanes), (rows_buf, lanes_buf), more_sems)
     for k in range(1, count):
-        for copy in into(k):
+        for copy in into(k, *come[k]):
             copy.start()
-    zero_buf[...] = jnp.zeros_like(zero_buf)
-    blank.start()
+    if not extra:
+        zero_buf[...] = jnp.zeros_like(zero_buf)
+        blank.start()
     consts[0].wait()
 
     def low_of(k, c, s):
@@ -217,92 +224,124 @@
             out_high(k, *where[k]).wait()
             out_low(k, *where[k]).wait()
         out_band(k).wait()
-    blank.wait()
-
-
-def base_kernel(counts, mine, theirs, place, m_ref, g_ref, early_ref, theirs_ref, *refs):
+    if not extra:
+        blank.wait()
+
+
+def moment_kernel(counts, slot, place, m_ref, g_ref, early_ref, *refs):
     received, refs = refs[: len(counts)], refs[len(counts) :]
-    constants, refs = refs[:4], refs[4:]
-    out_ref, top_ref, bottom_ref, band_ref = refs[:4]
-    m_buf, g_buf, r_buf, out_buf, band_buf, low_buf, early_buf = refs[4:11]
-    buffers, (sems, const_sems, more_sems) = refs[11:15], refs[15:]
+    constants, refs = refs[:2], refs[2:]
+    cells_ref, band_ref, m_buf, g_buf, r_buf, band_buf, low_buf, early_buf = refs[:8]
+    buffers, (sems, more_sems) = refs[8:10], refs[10:]
     total = sum(counts)
-    where = [(r, j) for r, n in zip(received, counts) for j in range(n)] + [(theirs_ref, theirs_ref.shape[1] // QUANTUM - 1)]
-    split = top_ref.shape[0]
+    where = [(r, j) for r, n in zip(received, counts) for j in range(n)]
 
     def into(k, r=None, j=0):
-        r, slot, at = (received[0], mine, k) if r is None else (r, theirs if r is theirs_ref else mine, min(k, total - 1))
-        yield pltpu.make_async_copy(g_ref.at[rows_of(place, slot), quantum(at), :], g_buf.at[k], sems.at[0, k])
+        r = received[0] if r is None else r
+        yield pltpu.make_async_copy(g_ref.at[rows_of(place, slot), quantum(k), :], g_buf.at[k], sems.at[0, k])
         yield pltpu.make_async_copy(r.at[:, quantum(j), :], r_buf.at[k], sems.at[1, k])
-
-    def moment(k):
-        return pltpu.make_async_copy(m_ref.at[:, quantum(k), :], m_buf.at[k], sems.at[2, k])
+        yield pltpu.make_async_copy(m_ref.at[:, quantum(k), :], m_buf.at[k], sems.at[2, k])
 
     def out(k):
-        return pltpu.make_async_copy(out_buf.at[k], out_ref.at[:, quantum(k), :], sems.at[3, k])
+        return pltpu.make_async_copy(m_buf.at[k], cells_ref.at[:, quantum(k), :], sems.at[3, k])
 
     def out_band(k):
         return pltpu.make_async_copy(band_buf.at[k], band_ref.at[band_at(k, place[4])], sems.at[4, k])
 
-    def out_last():
-        yield pltpu.make_async_copy(out_buf.at[total, pl.ds(0, split)], top_ref, more_sems.at[0])
-        yield pltpu.make_async_copy(out_buf.at[total, pl.ds(split, SPAN - split)], bottom_ref, more_sems.at[1])
-
     early = pltpu.make_async_copy(early_ref, early_buf, more_sems.at[2])
-    for copy in (*into(0, *where[0]), moment(0), early):
+    for copy in (*into(0, *where[0]), early):
         copy.start()
-    consts = load(constants, buffers, const_sems)
-    for k in range(1, total + 1):
+    consts = load(constants, buffers, more_sems)
+    for k in range(1, total):
         for copy in into(k, *where[k]):
             copy.start()
-        if k < total:
-            moment(k).start()
     for copy in consts:
         copy.wait()
-    low, low_back, band, band_back = buffers
-
-    def cells_of(k, add):
-        for copy in into(k, *(where[k] if isinstance(k, int) else ())):
+    low, band = buffers
+
+    def cells_of(k, more=None):
+        for copy in into(k):
             copy.wait()
-        cells = add(g_buf[k].astype(jnp.float32) + r_buf[k])
+        cells = DECAY * m_buf[k] + (g_buf[k].astype(jnp.float32) + r_buf[k])
+        if more is not None:
+            cells = cells + more
         m_buf[k] = cells
+        out(k).start()
         for s, c in enumerate(forward(cells, low[...])):
             low_buf[k, s * BAND : (s + 1) * BAND, :] = c
 
-    def own_cells(k, more=None):
-        moment(k).wait()
-        decayed = DECAY * m_buf[k]
-        cells_of(k, lambda x: decayed + (x if more is None else x + more))
-
     def body(k, _):
-        own_cells(k)
+        cells_of(k)
         return 0
 
     early.wait()
-    own_cells(0, early_buf[...])
+    cells_of(0, early_buf[...])
     lax.fori_loop(1, total, body, 0)
-    cells_of(total, lambda x: x)
-    b = dot(long(low_buf[...].reshape((total + 1) * SPAN, 4 * LANES)), band[...])
-    band_buf[...] = b.reshape(total + 1, 2, QUARTER, LANES)
+    b = dot(long(low_buf[...].reshape(total * SPAN, 4 * LANES)), band[...])
+    band_buf[...] = b.reshape(total, 2, QUARTER, LANES)
     for k in range(total):
         out_band(k).start()
-    low_buf[...] = dot(long(b), band_back[...]).reshape(total + 1, SPAN, 4 * LANES)
-
-    def without_band(k):
-        out_buf[k] = m_buf[k] - back(bands_of(low_buf[k]), low_back[...])
-
-    def body_back(k, _):
-        without_band(k)
-        out(k).start()
-        return 0
-
-    without_band(total)
-    for copy in out_last():
-        copy.start()
-    lax.fori_loop(0, total, body_back, 0)
     for k in range(total):
         out(k).wait()
         out_band(k).wait()
+
+
+def rest_kernel(slot, place, cells_ref, bands_ref, g_ref, r_ref, *refs):
+    constants, refs = refs[:4], refs[4:]
+    out_ref, last_ref, top_ref, bottom_ref = refs[:4]
+    cells_buf, band_buf, low_buf, g_buf, r_buf, theirs_buf = refs[4:10]
+    buffers, (sems, more_sems) = refs[10:14], refs[14:]
+    total = cells_buf.shape[0]
+    split = top_ref.shape[0]
+
+    def into(k):
+        return pltpu.make_async_copy(cells_ref.at[:, quantum(k), :], cells_buf.at[k], sems.at[0, k])
+
+    def out(k):
+        return pltpu.make_async_copy(cells_buf.at[k], out_ref.at[:, quantum(k), :], sems.at[1, k])
+
+    def out_last():
+        yield pltpu.make_async_copy(cells_buf.at[total - 1], last_ref, more_sems.at[4])
+        yield pltpu.make_async_copy(theirs_buf.at[pl.ds(0, split)], top_ref, more_sems.at[5])
+        yield pltpu.make_async_copy(theirs_buf.at[pl.ds(split, SPAN - split)], bottom_ref, more_sems.at[6])
+
+    theirs = [
+        pltpu.make_async_copy(g_ref.at[rows_of(place, slot), quantum(total - 1), :], g_buf, more_sems.at[7]),
+        pltpu.make_async_copy(r_ref.at[:, quantum(r_ref.shape[1] // QUANTUM - 1), :], r_buf, more_sems.at[8]),
+        pltpu.make_async_copy(bands_ref, band_buf, more_sems.at[9]),
+    ]
+    for copy in theirs:
+        copy.start()
+    consts = load(constants, buffers, more_sems)
+    for k in range(total):
+        into(k).start()
+    for copy in (*theirs, *consts):
+        copy.wait()
+    low, low_back, band, band_back = buffers
+
+    theirs_buf[...] = g_buf[...].astype(jnp.float32) + r_buf[...]
+    c = jnp.concatenate(forward(theirs_buf[...], low[...]), axis=0)
+    theirs_band = dot(long(c), band[...])
+    b = jnp.concatenate([band_buf[...].reshape(total * SPAN, LANES), theirs_band], axis=0)
+    low_buf[...] = dot(long(b), band_back[...]).reshape(total + 1, SPAN, 4 * LANES)
+    theirs_buf[...] = theirs_buf[...] - back(bands_of(low_buf[total]), low_back[...])
+
+    def body(k, _):
+        into(k).wait()
+        turned = lax.rem(k + total - lax.div(place[4], 2), total)
+        cells_buf[k] = cells_buf[k] - back(bands_of(low_buf[turned]), low_back[...])
+
+        @pl.when(k < total - 1)
+        def _():
+            out(k).start()
+
+        return 0
+
+    lax.fori_loop(0, total, body, 0)
+    for copy in out_last():
+        copy.start()
+    for k in range(total - 1):
+        out(k).wait()
     for copy in out_last():
         copy.wait()
 
@@ -346,18 +385,18 @@
         out(k).wait()
 
 
-def add_kernel(first, row, there_ref, base_ref, out_ref, there_buf, base_buf, sems):
-    at = (pl.ds(row, there_ref.shape[0]), quantum(first))
+def add_kernel(first, row, there_ref, last_ref, base_ref, out_ref, there_buf, last_buf, sems):
+    rows = pl.ds(row, there_ref.shape[0])
     into = [
         pltpu.make_async_copy(there_ref, there_buf, sems.at[0]),
-        pltpu.make_async_copy(base_ref.at[at], base_buf, sems.at[1]),
+        pltpu.make_async_copy(last_ref.at[rows], last_buf, sems.at[1]),
     ]
     for copy in into:
         copy.start()
     for copy in into:
         copy.wait()
-    base_buf[...] += there_buf[...]
-    out = pltpu.make_async_copy(base_buf, out_ref.at[at], sems.at[2])
+    last_buf[...] += there_buf[...]
+    out = pltpu.make_async_copy(last_buf, out_ref.at[rows, quantum(first)], sems.at[2])
     out.start()
     out.wait()
 
@@ -424,66 +463,93 @@
     return pltpu.SemaphoreType.DMA(shape)
 
 
-def cast(place, g, first, counts, slot):
-    n = sum(counts)
+def cast(place, g, *wanted):
+    n = sum(count for _, _, count in wanted)
     return call(
-        functools.partial(cast_kernel, first, counts, slot),
+        functools.partial(cast_kernel, wanted),
         place,
         [g],
-        [floats(SPAN, c * QUANTUM, LANES) for c in counts],
+        [floats(SPAN, count * QUANTUM, LANES) for _, _, count in wanted],
         held(n, jnp.bfloat16, jnp.float32) + [sems(2, n)],
         {},
         MOST,
     )
 
 
-def encoded(place, g, received, first, counts, slot, mats):
+def encoded(place, g, received, first, counts, slot, mats, bands=None):
     values = [mats["rows"], mats["lanes"]]
+    extra = int(bands is not None)
     sent = sum(counts)
+    n = sent + extra
     return call(
-        functools.partial(encode_kernel, first, counts, slot),
+        functools.partial(encode_kernel, first, counts, extra, slot, [r.shape[1] // QUANTUM for r in received]),
         place,
-        [g, received, *values],
-        [floats(n, PAYLOAD, LANES) for n in counts] + [BANDS],
-        held(sent + 1, jnp.bfloat16, jnp.float32)
-        + [pltpu.VMEM((sent, PAYLOAD, LANES), jnp.float32), pltpu.VMEM((sent + 1, 2, QUARTER, LANES), jnp.float32)]
-        + lows(sent + 1)
+        [g, *received, *values, *([bands] * extra)],
+        [floats(c, PAYLOAD, LANES) for c in counts] + [BANDS],
+        held(n, jnp.bfloat16, jnp.float32)
+        + [pltpu.VMEM((sent, PAYLOAD, LANES), jnp.float32), pltpu.VMEM((n, 2, QUARTER, LANES), jnp.float32)]
+        + lows(n)
         + [pltpu.VMEM((2, QUARTER, LANES), jnp.float32)]
         + same(values)
-        + [sems(5, sent + 1), sems(3)],
-        {},
+        + [sems(5, n), sems(3)],
+        {4 + len(received): len(counts)} if extra else {},
         MOST,
     )
 
 
-def based(place, m, g, early, other, received, mine, theirs, mats):
-    values = [mats[name] for name in ("low", "low_back", "band", "band_back")]
+def moments(place, m, g, early, received, slot, mats):
+    values = [mats["low"], mats["band"]]
     counts = [r.shape[1] // QUANTUM for r in received]
-    n = sum(counts) + 1
+    n = sum(counts)
     return call(
-        functools.partial(base_kernel, counts, mine, theirs),
+        functools.partial(moment_kernel, counts, slot),
         place,
-        [m, g, early, other, *received, *values],
-        [floats(*m.shape), floats(SPLIT, QUANTUM, LANES), floats(SPAN - SPLIT, QUANTUM, LANES), BANDS],
-        held(n, jnp.float32, jnp.bfloat16, jnp.float32, jnp.float32)
+        [m, g, early, *received, *values],
+        [floats(*m.shape), BANDS],
+        held(n, jnp.float32, jnp.bfloat16, jnp.float32)
         + [pltpu.VMEM((n, 2, QUARTER, LANES), jnp.float32)]
         + lows(n)
         + [pltpu.VMEM((SPAN, QUANTUM, LANES), jnp.float32)]
         + same(values)
-        + [sems(5, n), sems(4), sems(3)],
+        + [sems(5, n), sems(3)],
         {},
         MOST,
     )
 
 
-def added(there, base, first, row, mats):
+def rest(place, cells, bands, g, received, slot, mats):
+    values = [mats[name] for name in ("low", "low_back", "band", "band_back")]
+    n = cells.shape[1] // QUANTUM
+    one = [pltpu.VMEM((SPAN, QUANTUM, LANES), dtype) for dtype in (jnp.bfloat16, jnp.float32, jnp.float32)]
+    return call(
+        functools.partial(rest_kernel, slot),
+        place,
+        [cells, bands, g, received, *values],
+        [
+            floats(*cells.shape),
+            floats(SPAN, QUANTUM, LANES),
+            floats(SPLIT, QUANTUM, LANES),
+            floats(SPAN - SPLIT, QUANTUM, LANES),
+        ],
+        held(n, jnp.float32)
+        + [pltpu.VMEM(BANDS.shape, jnp.float32)]
+        + lows(n + 1)
+        + one
+        + same(values)
+        + [sems(2, n), sems(10)],
+        {1: 0},
+        MOST,
+    )
+
+
+def added(there, last, base, first, row):
     return call(
         functools.partial(add_kernel, first, row),
         None,
-        [there, base],
+        [there, last, base],
         [floats(*base.shape)],
         same([there, there]) + [sems(3)],
-        {1: 0},
+        {2: 0},
         MOST,
     )[0]
 
@@ -559,40 +625,43 @@
         return lax.dynamic_slice(g, (place[slot] * SPAN, 0, 0), (SPAN, QUANTUM, LANES)).astype(jnp.float32)
 
     place1, cells = tie(place, head(3))
-    (more,) = cast(place1, g, 1, (count - 1,), 3)
+    (more,) = cast(place1, g, (3, 1, SECOND))
     got, more = tie(core(cells), more)
     cells = head(2) + got
     early = link(cells)
-    place2, cells = tie(place1, cells)
-    mine = cast(place2, g, 0, (2, 2, 2), 1)
-    got, *mine = tie(core(more), *mine)
-    *pays, other_band = encoded(place, g, got, 1, (4, 2), 2, mats)
-    theres = [link(pay) for pay in pays]
+    pay, other_band = encoded(place, g, [core(more)], 1, (SECOND,), 2, mats)
+    second = link(pay)
+    place2, _ = tie(place1, pay)
+    wanted = [(3, k, 1) for k in range(1 + SECOND, count)] + [(1, k, 2) for k in range(0, count, 2)]
+    *cells, later = cast(place2, g, *wanted)
+    early, later, _ = tie(early, later, pay)
+    pieces = [core(c) for c in [*cells, later]]
+    got, mine = pieces[: -count // 2], pieces[-count // 2 :]
+    pay, other_band = encoded(place, g, got, 1 + SECOND, (count - 2 - SECOND,), 2, mats, other_band)
+    third = link(pay)
     names = ("rep", "fsdp")
     wrapped = lax.ppermute(other_band, names, steps(rep_count, 0, 2))
-    place3, early, _ = tie(place2, early, pays[0])
-    mine = [core(c) for c in [*mine, *cast(place3, g, 6, (2,), 1)]]
-    base, top, bottom, own_band = based(place, m, g, early, got, mine, 0, 2, mats)
-    top, bottom = link(top), link(bottom)
+    cells, own_band = moments(place, m, g, early, mine, 0, mats)
+    base, last, top, bottom = rest(place, cells, own_band, g, got[-1], 2, mats)
 
     groups = [[h * PLANE + i for i in range(PLANE)] for h in range(rep_count // PLANE)]
     met = lax.all_to_all(own_band + wrapped, "rep", 0, 0, axis_index_groups=groups, tiled=True)
+    met, bottom = tie(met, bottom)
+    top, bottom = link(top), link(bottom)
     part = jnp.sum(met.reshape(PLANE, QUARTER, LANES), axis=0)
     total = part + lax.ppermute(part, names, steps(rep_count, TURN, 0))
+    total, second = tie(total, second)
     spread = jnp.broadcast_to(total[None], (PLANE,) + total.shape)
     band_total = lax.all_to_all(spread, "rep", 0, 0, axis_index_groups=groups, tiled=True)
+    out, band_total = tie(decoded(second, base, 1, mats), band_total)
     update = updated(place, band_total, 1.0 / rep_count, m.shape, mats)
 
-    theres[1], update = tie(theres[1], update)
-    out, first = base, 1
-    for there in theres:
-        there, out = tie(there, out)
-        out = decoded(there, out, first, mats)
-        first += there.shape[0]
+    third, update = tie(third, update)
+    out = decoded(third, out, 1 + SECOND, mats)
     top, out = tie(top, out)
-    out = added(top, out, count - 1, 0, mats)
+    out = added(top, last, out, count - 1, 0)
     bottom, out = tie(bottom, out)
-    out = added(bottom, out, count - 1, SPLIT, mats)
+    out = added(bottom, last, out, count - 1, SPLIT)
     return (untiles(out, mat_count)[None], untiles(update, mat_count))
 
 

time: 99.9 us -> 97.4 us (0.975)
  starting transfers between devices: 26.2 us -> 31.5 us
  waiting for transfers between devices: 22.2 us -> 19.3 us
  local copies, waits for them, and re-layouts: 2.86 us -> 0.86 us
  Pallas kernels: 41.6 us -> 40.1 us
  other arithmetic: 5.05 us -> 3.74 us
    ppermute x5, waiting for transfers between devices: 1.43 us -> 9.42 us  [link(): return lax.ppermute(x, 'fsdp', over_z)]
    all_to_all x1, waiting for transfers between devices: 7.69 us -> 1.72 us  [per_device(): lax.all_to_all(spread, 'rep', 0, 0, axis_index_groups=groups, tiled=True)]
    all_to_all x1, waiting for transfers between devices: 7.79 us -> 2.49 us  [per_device(): lax.all_to_all(own_band + wrapped, 'rep', 0, 0, axis_index_groups=groups,...]
    all_to_all x1, starting transfers between devices: 4.2 us -> 7.13 us  [per_device(): lax.all_to_all(spread, 'rep', 0, 0, axis_index_groups=groups, tiled=True)]
    unnamed x24 -> x16, local copies, waits for them, and re-layouts: 2.04 us -> 0.04 us
    pallas_call x10 -> x11, Pallas kernels: 41.6 us -> 40.1 us  [call(): pl.pallas_call(kernel, grid_spec=pltpu.PrefetchScalarGridSpec(num_scalar_...]
    ppermute x1, waiting for transfers between devices: 4.3 us -> 3.27 us  [per_device(): total = part + lax.ppermute(part, names, steps(rep_count, TURN, 0))]
    ppermute x6 -> x9, starting transfers between devices: 1.57 us -> 2.4 us  [core(): return lax.ppermute(x, 'fsdp', over_core)]
  transfers between devices with their start and end apart: 15 -> 18, of which waited for: 7 -> 12; matrix products, arithmetic and copies ran while one was open for 5% -> 4% of each run, Pallas kernels for 40% -> 41%
where the time goes in v4:
time: 97.4 us; the launch traced here: 96.4 us
  Pallas kernels  40.1 us (41%)
  starting transfers between devices  31.5 us (32%)
  waiting for transfers between devices  19.3 us (20%)
  other arithmetic  3.74 us (4%)
    pallas_call x11, Pallas kernels, call(): pl.pallas_call(kernel, grid_spec=pltpu.PrefetchScalarGridSpec(num_scalar_...  40.1 us
    ppermute x5, waiting for transfers between devices, link(): return lax.ppermute(x, 'fsdp', over_z)  9.42 us
    ppermute x5, starting transfers between devices, link(): return lax.ppermute(x, 'fsdp', over_z)  7.65 us
    all_to_all x1, starting transfers between devices, per_device(): lax.all_to_all(spread, 'rep', 0, 0, axis_index_groups=groups, tiled=True)  7.13 us
    all_to_all x1, starting transfers between devices, per_device(): lax.all_to_all(own_band + wrapped, 'rep', 0, 0, axis_index_groups=groups,...  7.08 us
    ppermute x1, starting transfers between devices, per_device(): total = part + lax.ppermute(part, names, steps(rep_count, TURN, 0))  4.27 us
    ppermute x1, waiting for transfers between devices, per_device(): total = part + lax.ppermute(part, names, steps(rep_count, TURN, 0))  3.27 us
    ppermute x1, starting transfers between devices, per_device(): wrapped = lax.ppermute(other_band, names, steps(rep_count, 0, 2))  3.01 us
  transfers between devices with their start and end apart: 18, of which 12 were waited for; matrix products, arithmetic and copies ran while one was open for 4% of the time, Pallas kernels for 41%

profile of v4, /device:TPU:0, one launch (start us, length us, event | category | flops | bytes accessed | tf_op | source)
XLA Modules:
  0.0 96.4 jit_solution(1520648859977553407)
XLA Ops:
  1.8 2.9 %shard_map.113 = f32[64,64,128]{2,1,0:T(8,128)} custom-call(s32[6]{0:T(128)S(1)} %stack.27.place, bf16[256,128,128]{2,1,0:T(8,128)(2,1)} %bitcast.27), custom_call_target="tpu_custom_call" | custom-call | tf_op jit(solution)/shard_map/pallas_call | solution.py:430
  6.3 2.1 %collective-permute-start.1 = (f32[64,16,128]{2,1,0:T(8,128)S(1)}, f32[64,16,128]{2,1,0:T(8,128)S(1)}, u32[]{:S(2)}, u32[]{:S(2)}) collective-permute-start(f32[64,16,128]{2,1,0:T(8,128)S(1)} %convert_add_fusion), channel_id=1, source_target_pairs={{0,2},{1,3},{2,0},{3,1},{4,6},{5,7},{6,4},{7,5},{8,10},{9,11},{10,... | collective-permute-start | bytes 1572872 | tf_op jit(solution)/shard_map/ppermute | solution.py:622
  9.5 4.7 %shard_map.114 = (f32[4,960,128]{2,1,0:T(8,128)}, f32[16,32,128]{2,1,0:T(8,128)S(1)}) custom-call(s32[6]{0:T(128)S(1)} %stack.27.place, bf16[256,128,128]{2,1,0:T(8,128)(2,1)} %bitcast.29, f32[64,64,128]{2,1,0:T(8,128)} %collective-permute-done.2.refs_0_, bf16[64,192]{1,0:T(8,128)(2,1)S(1)} %copy-done.5, bf16[1536,512]{1,0:T(8,128)(2,1)S(1)} %copy-done), custom_call_target="tpu_custom_call" | custom-call | tf_op jit(solution)/shard_map/pallas_call | solution.py:430
  14.1 2.8 %shard_map.115 = (f32[64,16,128]{2,1,0:T(8,128)S(1)}, f32[64,16,128]{2,1,0:T(8,128)S(1)}, f32[64,16,128]{2,1,0:T(8,128)S(1)}, f32[64,32,128]{2,1,0:T(8,128)S(1)}...) custom-call(s32[6]{0:T(128)S(1)} %stack.27.place, bf16[256,128,128]{2,1,0:T(8,128)(2,1)} %bitcast.30), custom_call_target="tpu_custom_call" | custom-call | tf_op jit(solution)/shard_map/pallas_call | solution.py:430
  17.4 2.0 %collective-permute-start.15 = (f32[4,960,128]{2,1,0:T(8,128)}, f32[4,960,128]{2,1,0:T(8,128)}, u32[]{:S(2)}, u32[]{:S(2)}) collective-permute-start(f32[4,960,128]{2,1,0:T(8,128)} %get-tuple-element.42), channel_id=1, source_target_pairs={{0,2},{1,3},{2,0},{3,1},{4,6},{5,7},{6,4},{7,5},{8,10},{9,11},{10,... | collective-permute-start | bytes 5898248 | tf_op jit(solution)/shard_map/ppermute | solution.py:622
  22.2 3.8 %shard_map.117 = (f32[2,960,128]{2,1,0:T(8,128)}, f32[16,32,128]{2,1,0:T(8,128)S(1)}) custom-call(s32[6]{0:T(128)S(1)} %stack.27.place, bf16[256,128,128]{2,1,0:T(8,128)(2,1)} %bitcast.31, f32[64,16,128]{2,1,0:T(8,128)S(1)} %collective-permute-done.7.refs_0_, f32[64,16,128]{2,1,0:T(8,128)S(1)} %collective-permute-done.8.refs_1_, ...), custom_call_target="tpu_custom_call", output_to_operand_aliasing={{1}: (7, {})} | custom-call | tf_op jit(solution)/shard_map/pallas_call | solution.py:430
  26.0 1.2 %collective-permute-start.13 = (f32[2,960,128]{2,1,0:T(8,128)}, f32[2,960,128]{2,1,0:T(8,128)}, u32[]{:S(2)}, u32[]{:S(2)}) collective-permute-start(f32[2,960,128]{2,1,0:T(8,128)} %get-tuple-element.60), channel_id=1, source_target_pairs={{0,2},{1,3},{2,0},{3,1},{4,6},{5,7},{6,4},{7,5},{8,10},{9,11},{10,... | collective-permute-start | bytes 2949128 | tf_op jit(solution)/shard_map/ppermute | solution.py:622
  27.3 3.0 %collective-permute-start.10 = (f32[16,32,128]{2,1,0:T(8,128)S(1)}, f32[16,32,128]{2,1,0:T(8,128)S(1)}, u32[]{:S(2)}, u32[]{:S(2)}) collective-permute-start(f32[16,32,128]{2,1,0:T(8,128)S(1)} %get-tuple-element.55), channel_id=1, source_target_pairs={{0,66},{1,67},{2,64},{3,65},{4,70},{5,71},{6,68},{7,69},{8,74},{9,... | collective-permute-start | bytes 786440 | tf_op jit(solution)/shard_map/ppermute | solution.py:643
  30.3 6.0 %shard_map.116 = (f32[64,128,128]{2,1,0:T(8,128)}, f32[16,32,128]{2,1,0:T(8,128)S(1)}) custom-call(s32[6]{0:T(128)S(1)} %stack.27.place, f32[64,128,128]{2,1,0:T(8,128)} %bitcast.35, bf16[256,128,128]{2,1,0:T(8,128)(2,1)} %bitcast.32, f32[64,16,128]{2,1,0:T(8,128)S(1)} %collective-permute-done.1.early_ref, ...), custom_call_target="tpu_custom_call" | custom-call | tf_op jit(solution)/shard_map/pallas_call | solution.py:430
  37.6 7.1 %all-to-all-start = ((f32[16,32,128]{2,1,0:T(8,128)}), f32[16,32,128]{2,1,0:T(8,128)}, u32[]{:S(2)}, u32[]{:S(2)}) async-start(f32[16,32,128]{2,1,0:T(8,128)} %add.19), calls=%async_computation | async-start | bytes 524288 | tf_op jit(solution)/shard_map/all_to_all | solution.py:648
  44.7 5.7 %shard_map.118 = (f32[64,128,128]{2,1,0:T(8,128)}, f32[64,16,128]{2,1,0:T(8,128)S(1)}, f32[48,16,128]{2,1,0:T(8,128)}, f32[16,16,128]{2,1,0:T(8,128)S(1)}) custom-call(s32[6]{0:T(128)S(1)} %stack.27.place, f32[64,128,128]{2,1,0:T(8,128)} %get-tuple-element.56.cells_ref, ...), custom_call_target="tpu_custom_call", output_to_operand_aliasing={{0}: (1, {})} | custom-call | tf_op jit(solution)/shard_map/pallas_call | solution.py:430
  50.7 2.5 %all-to-all-done = f32[16,32,128]{2,1,0:T(8,128)} async-done(((f32[16,32,128]{2,1,0:T(8,128)}), f32[16,32,128]{2,1,0:T(8,128)}, u32[]{:S(2)}, u32[]{:S(2)}) %all-to-all-start) | async-done | bytes 262176 | tf_op jit(solution)/shard_map/all_to_all | solution.py:648
  54.2 4.3 %collective-permute-start.14 = (f32[32,128]{1,0:T(8,128)S(1)}, f32[32,128]{1,0:T(8,128)S(1)}, u32[]{:S(2)}, u32[]{:S(2)}) collective-permute-start(f32[32,128]{1,0:T(8,128)S(1)} %reduce_sum.9), channel_id=1, source_target_pairs={{0,112},{1,113},{2,114},{3,115},{4,116},{5,117},{6,118},{7,119},{8... | collective-permute-start | bytes 49160 | tf_op jit(solution)/shard_map/ppermute | solution.py:652
  58.5 3.3 %collective-permute-done.14 = f32[32,128]{1,0:T(8,128)S(1)} collective-permute-done((f32[32,128]{1,0:T(8,128)S(1)}, f32[32,128]{1,0:T(8,128)S(1)}, u32[]{:S(2)}, u32[]{:S(2)}) %collective-permute-start.14) | collective-permute-done | bytes 16416 | tf_op jit(solution)/shard_map/ppermute | solution.py:652
  61.8 1.9 %collective-permute-done.15.pay_ref = f32[4,960,128]{2,1,0:T(8,128)} collective-permute-done((f32[4,960,128]{2,1,0:T(8,128)}, f32[4,960,128]{2,1,0:T(8,128)}, u32[]{:S(2)}, u32[]{:S(2)}) %collective-permute-start.15) | collective-permute-done | bytes 1966112 | tf_op jit(solution)/shard_map/ppermute | solution.py:622
  64.4 7.1 %all-to-all-start.1 = ((f32[16,32,128]{2,1,0:T(8,128)}), f32[16,32,128]{2,1,0:T(8,128)S(1)}, u32[]{:S(2)}, u32[]{:S(2)}) async-start(f32[16,32,128]{2,1,0:T(8,128)} %broadcast_in_dim.2), calls=%async_computation.1 | async-start | bytes 524288 | tf_op jit(solution)/shard_map/all_to_all | solution.py:655
  71.5 2.0 %collective-permute-start.11 = (f32[16,16,128]{2,1,0:T(8,128)S(1)}, f32[16,16,128]{2,1,0:T(8,128)S(1)}, u32[]{:S(2)}, u32[]{:S(2)}) collective-permute-start(f32[16,16,128]{2,1,0:T(8,128)S(1)} %get-tuple-element.58), channel_id=1, source_target_pairs={{0,2},{1,3},{2,0},{3,1},{4,6},{5,7},{6,4},{7,5},{8,10},{9,11},{10,... | collective-permute-start | bytes 393224 | tf_op jit(solution)/shard_map/ppermute | solution.py:622
  73.6 4.7 %shard_map.119.base_ref = f32[64,128,128]{2,1,0:T(8,128)} custom-call(f32[4,960,128]{2,1,0:T(8,128)} %collective-permute-done.15.pay_ref, bf16[64,192]{1,0:T(8,128)(2,1)S(1)} %copy-done.4, bf16[1152,512]{1,0:T(8,128)(2,1)S(1)} %copy-done.1, f32[64,128,128]{2,1,0:T(8,128)} %get-tuple-element.63.base_ref), custom_call_target="tpu_custom_call", output_to_operand_aliasing={{}: (3, {})} | custom-call | tf_op jit(solution)/shard_map/pallas_call | solution.py:430
  78.3 1.7 %all-to-all-done.1.band_ref = f32[16,32,128]{2,1,0:T(8,128)S(1)} async-done(((f32[16,32,128]{2,1,0:T(8,128)}), f32[16,32,128]{2,1,0:T(8,128)S(1)}, u32[]{:S(2)}, u32[]{:S(2)}) %all-to-all-start.1) | async-done | bytes 262176 | tf_op jit(solution)/shard_map/all_to_all | solution.py:655
  80.0 4.0 %shard_map.120 = f32[64,128,128]{2,1,0:T(8,128)} custom-call(s32[6]{0:T(128)S(1)} %stack.27.place, f32[16,32,128]{2,1,0:T(8,128)S(1)} %all-to-all-done.1.band_ref, bf16[64,48]{1,0:T(8,128)(2,1)S(1)} %copy-done.6, bf16[384,512]{1,0:T(8,128)(2,1)S(1)} %copy-done.2), custom_call_target="tpu_custom_call" | custom-call | tf_op jit(solution)/shard_map/pallas_call | solution.py:430
  84.7 3.3 %shard_map.121.base_ref = f32[64,128,128]{2,1,0:T(8,128)} custom-call(f32[2,960,128]{2,1,0:T(8,128)} %collective-permute-done.13.pay_ref, bf16[64,192]{1,0:T(8,128)(2,1)S(1)} %copy-done.4, bf16[1152,512]{1,0:T(8,128)(2,1)S(1)} %copy-done.1, f32[64,128,128]{2,1,0:T(8,128)} %shard_map.119.base_ref), custom_call_target="tpu_custom_call", output_to_operand_aliasing={{}: (3, {})} | custom-call | tf_op jit(solution)/shard_map/pallas_call | solution.py:430
  88.0 5.0 %collective-permute-done.12.there_ref = f32[48,16,128]{2,1,0:T(8,128)S(1)} collective-permute-done((f32[48,16,128]{2,1,0:T(8,128)}, f32[48,16,128]{2,1,0:T(8,128)S(1)}, u32[]{:S(2)}, u32[]{:S(2)}) %collective-permute-start.12) | collective-permute-done | bytes 393248 | tf_op jit(solution)/shard_map/ppermute | solution.py:622
  93.1 1.2 %shard_map.122.base_ref = f32[64,128,128]{2,1,0:T(8,128)} custom-call(f32[48,16,128]{2,1,0:T(8,128)S(1)} %collective-permute-done.12.there_ref, f32[64,16,128]{2,1,0:T(8,128)S(1)} %get-tuple-element.69.last_ref, f32[64,128,128]{2,1,0:T(8,128)} %shard_map.121.base_ref), custom_call_target="tpu_custom_call", output_to_operand_aliasing={{}: (2, {})} | custom-call | tf_op jit(solution)/shard_map/pallas_call | solution.py:430
  94.2 1.1 %collective-permute-done.11.there_ref = f32[16,16,128]{2,1,0:T(8,128)S(1)} collective-permute-done((f32[16,16,128]{2,1,0:T(8,128)S(1)}, f32[16,16,128]{2,1,0:T(8,128)S(1)}, u32[]{:S(2)}, u32[]{:S(2)}) %collective-permute-start.11) | collective-permute-done | bytes 131104 | tf_op jit(solution)/shard_map/ppermute | solution.py:622
  (46 shorter events, 12.1 us)
Async XLA Ops:
  1.8 3.0 %collective-permute-start = (f32[64,16,128]{2,1,0:T(8,128)S(1)}, f32[64,16,128]{2,1,0:T(8,128)S(1)}, u32[]{:S(2)}, u32[]{:S(2)}) collective-permute-start(f32[64,16,128]{2,1,0:T(8,128)S(1)} %dynamic-slice_convert_fusion), channel_id=1, source_target_pairs={{0,1},{1,0},{2,3},{3,2},{4,5},{5,4},{6,7},{7,6},{8,9},{9,8},{10,11... | collective-permute-start | bytes 1572872 | tf_op jit(solution)/shard_map/ppermute | solution.py:619
  4.8 4.7 %collective-permute-start.2 = (f32[64,64,128]{2,1,0:T(8,128)}, f32[64,64,128]{2,1,0:T(8,128)}, u32[]{:S(2)}, u32[]{:S(2)}) collective-permute-start(f32[64,64,128]{2,1,0:T(8,128)} %shard_map.113), channel_id=1, source_target_pairs={{0,1},{1,0},{2,3},{3,2},{4,5},{5,4},{6,7},{7,6},{8,9},{9,8},{10,11... | collective-permute-start | bytes 6291464 | tf_op jit(solution)/shard_map/ppermute | solution.py:619
  6.3 14.2 %collective-permute-start.1 = (f32[64,16,128]{2,1,0:T(8,128)S(1)}, f32[64,16,128]{2,1,0:T(8,128)S(1)}, u32[]{:S(2)}, u32[]{:S(2)}) collective-permute-start(f32[64,16,128]{2,1,0:T(8,128)S(1)} %convert_add_fusion), channel_id=1, source_target_pairs={{0,2},{1,3},{2,0},{3,1},{4,6},{5,7},{6,4},{7,5},{8,10},{9,11},{10,... | collective-permute-start | bytes 1572872 | tf_op jit(solution)/shard_map/ppermute | solution.py:622
  16.9 3.6 %collective-permute-start.7 = (f32[64,16,128]{2,1,0:T(8,128)S(1)}, f32[64,16,128]{2,1,0:T(8,128)S(1)}, u32[]{:S(2)}, u32[]{:S(2)}) collective-permute-start(f32[64,16,128]{2,1,0:T(8,128)S(1)} %get-tuple-element.51), channel_id=1, source_target_pairs={{0,1},{1,0},{2,3},{3,2},{4,5},{5,4},{6,7},{7,6},{8,9},{9,8},{10,11... | collective-permute-start | bytes 1572872 | tf_op jit(solution)/shard_map/ppermute | solution.py:619
  17.4 46.3 %collective-permute-start.15 = (f32[4,960,128]{2,1,0:T(8,128)}, f32[4,960,128]{2,1,0:T(8,128)}, u32[]{:S(2)}, u32[]{:S(2)}) collective-permute-start(f32[4,960,128]{2,1,0:T(8,128)} %get-tuple-element.42), channel_id=1, source_target_pairs={{0,2},{1,3},{2,0},{3,1},{4,6},{5,7},{6,4},{7,5},{8,10},{9,11},{10,... | collective-permute-start | bytes 5898248 | tf_op jit(solution)/shard_map/ppermute | solution.py:622
  19.4 1.9 %collective-permute-start.8 = (f32[64,16,128]{2,1,0:T(8,128)S(1)}, f32[64,16,128]{2,1,0:T(8,128)S(1)}, u32[]{:S(2)}, u32[]{:S(2)}) collective-permute-start(f32[64,16,128]{2,1,0:T(8,128)S(1)} %get-tuple-element.52), channel_id=1, source_target_pairs={{0,1},{1,0},{2,3},{3,2},{4,5},{5,4},{6,7},{7,6},{8,9},{9,8},{10,11... | collective-permute-start | bytes 1572872 | tf_op jit(solution)/shard_map/ppermute | solution.py:619
  19.4 2.7 %collective-permute-start.9 = (f32[64,16,128]{2,1,0:T(8,128)S(1)}, f32[64,16,128]{2,1,0:T(8,128)S(1)}, u32[]{:S(2)}, u32[]{:S(2)}) collective-permute-start(f32[64,16,128]{2,1,0:T(8,128)S(1)} %get-tuple-element.53), channel_id=1, source_target_pairs={{0,1},{1,0},{2,3},{3,2},{4,5},{5,4},{6,7},{7,6},{8,9},{9,8},{10,11... | collective-permute-start | bytes 1572872 | tf_op jit(solution)/shard_map/ppermute | solution.py:619
  20.6 5.5 %collective-permute-start.6 = (f32[64,32,128]{2,1,0:T(8,128)S(1)}, f32[64,32,128]{2,1,0:T(8,128)S(1)}, u32[]{:S(2)}, u32[]{:S(2)}) collective-permute-start(f32[64,32,128]{2,1,0:T(8,128)S(1)} %get-tuple-element.49), channel_id=1, source_target_pairs={{0,1},{1,0},{2,3},{3,2},{4,5},{5,4},{6,7},{7,6},{8,9},{9,8},{10,11... | collective-permute-start | bytes 3145736 | tf_op jit(solution)/shard_map/ppermute | solution.py:619
  20.6 6.7 %collective-permute-start.3 = (f32[64,32,128]{2,1,0:T(8,128)S(1)}, f32[64,32,128]{2,1,0:T(8,128)S(1)}, u32[]{:S(2)}, u32[]{:S(2)}) collective-permute-start(f32[64,32,128]{2,1,0:T(8,128)S(1)} %get-tuple-element.46), channel_id=1, source_target_pairs={{0,1},{1,0},{2,3},{3,2},{4,5},{5,4},{6,7},{7,6},{8,9},{9,8},{10,11... | collective-permute-start | bytes 3145736 | tf_op jit(solution)/shard_map/ppermute | solution.py:619
  21.3 9.0 %collective-permute-start.4 = (f32[64,32,128]{2,1,0:T(8,128)S(1)}, f32[64,32,128]{2,1,0:T(8,128)S(1)}, u32[]{:S(2)}, u32[]{:S(2)}) collective-permute-start(f32[64,32,128]{2,1,0:T(8,128)S(1)} %get-tuple-element.47), channel_id=1, source_target_pairs={{0,1},{1,0},{2,3},{3,2},{4,5},{5,4},{6,7},{7,6},{8,9},{9,8},{10,11... | collective-permute-start | bytes 3145736 | tf_op jit(solution)/shard_map/ppermute | solution.py:619
  22.0 8.2 %collective-permute-start.5 = (f32[64,32,128]{2,1,0:T(8,128)S(1)}, f32[64,32,128]{2,1,0:T(8,128)S(1)}, u32[]{:S(2)}, u32[]{:S(2)}) collective-permute-start(f32[64,32,128]{2,1,0:T(8,128)S(1)} %get-tuple-element.48), channel_id=1, source_target_pairs={{0,1},{1,0},{2,3},{3,2},{4,5},{5,4},{6,7},{7,6},{8,9},{9,8},{10,11... | collective-permute-start | bytes 3145736 | tf_op jit(solution)/shard_map/ppermute | solution.py:619
  22.2 8.1 %copy-start.3 = (bf16[1536,128]{1,0:T(8,128)(2,1)S(1)}, bf16[1536,128]{1,0:T(8,128)(2,1)}, u32[]{:S(2)}) copy-start(bf16[1536,128]{1,0:T(8,128)(2,1)} %constant.60.clone.refs_5_.refs_2_) | copy-start | bytes 1179652
  22.2 8.1 %copy-start.7 = (bf16[16,192]{1,0:T(8,128)(2,1)S(1)}, bf16[16,192]{1,0:T(8,128)(2,1)}, u32[]{:S(2)}) copy-start(bf16[16,192]{1,0:T(8,128)(2,1)} %constant.56.clone.refs_4_.refs_0_) | copy-start | bytes 18436
  26.0 58.7 %collective-permute-start.13 = (f32[2,960,128]{2,1,0:T(8,128)}, f32[2,960,128]{2,1,0:T(8,128)}, u32[]{:S(2)}, u32[]{:S(2)}) collective-permute-start(f32[2,960,128]{2,1,0:T(8,128)} %get-tuple-element.60), channel_id=1, source_target_pairs={{0,2},{1,3},{2,0},{3,1},{4,6},{5,7},{6,4},{7,5},{8,10},{9,11},{10,... | collective-permute-start | bytes 2949128 | tf_op jit(solution)/shard_map/ppermute | solution.py:622
  27.3 9.6 %collective-permute-start.10 = (f32[16,32,128]{2,1,0:T(8,128)S(1)}, f32[16,32,128]{2,1,0:T(8,128)S(1)}, u32[]{:S(2)}, u32[]{:S(2)}) collective-permute-start(f32[16,32,128]{2,1,0:T(8,128)S(1)} %get-tuple-element.55), channel_id=1, source_target_pairs={{0,66},{1,67},{2,64},{3,65},{4,70},{5,71},{6,68},{7,69},{8,74},{9,... | collective-permute-start | bytes 786440 | tf_op jit(solution)/shard_map/ppermute | solution.py:643
  30.3 14.4 %copy-start.2 = (bf16[384,512]{1,0:T(8,128)(2,1)S(1)}, bf16[384,512]{1,0:T(8,128)(2,1)}, u32[]{:S(2)}) copy-start(bf16[384,512]{1,0:T(8,128)(2,1)} %constant.61.clone.refs_3_.band_back) | copy-start | bytes 1179652
  30.3 14.4 %copy-start.6 = (bf16[64,48]{1,0:T(8,128)(2,1)S(1)}, bf16[64,48]{1,0:T(8,128)(2,1)}, u32[]{:S(2)}) copy-start(bf16[64,48]{1,0:T(8,128)(2,1)} %constant.57.clone.refs_1_.low_back) | copy-start | bytes 18436
  37.6 15.7 %all-to-all-start = ((f32[16,32,128]{2,1,0:T(8,128)}), f32[16,32,128]{2,1,0:T(8,128)}, u32[]{:S(2)}, u32[]{:S(2)}) async-start(f32[16,32,128]{2,1,0:T(8,128)} %add.19), calls=%async_computation | async-start | bytes 524288 | tf_op jit(solution)/shard_map/all_to_all | solution.py:648
  44.7 28.9 %copy-start.1 = (bf16[1152,512]{1,0:T(8,128)(2,1)S(1)}, bf16[1152,512]{1,0:T(8,128)(2,1)}, u32[]{:S(2)}) copy-start(bf16[1152,512]{1,0:T(8,128)(2,1)} %constant.59.clone.kept_back) | copy-start | bytes 3538948
  44.7 28.9 %copy-start.4 = (bf16[64,192]{1,0:T(8,128)(2,1)S(1)}, bf16[64,192]{1,0:T(8,128)(2,1)}, u32[]{:S(2)}) copy-start(bf16[64,192]{1,0:T(8,128)(2,1)} %constant.55.clone.rows_back) | copy-start | bytes 73732
  50.4 42.6 %collective-permute-start.12 = (f32[48,16,128]{2,1,0:T(8,128)}, f32[48,16,128]{2,1,0:T(8,128)S(1)}, u32[]{:S(2)}, u32[]{:S(2)}) collective-permute-start(f32[48,16,128]{2,1,0:T(8,128)} %get-tuple-element.59), channel_id=1, source_target_pairs={{0,2},{1,3},{2,0},{3,1},{4,6},{5,7},{6,4},{7,5},{8,10},{9,11},{10,... | collective-permute-start | bytes 1179656 | tf_op jit(solution)/shard_map/ppermute | solution.py:622
  54.2 7.5 %collective-permute-start.14 = (f32[32,128]{1,0:T(8,128)S(1)}, f32[32,128]{1,0:T(8,128)S(1)}, u32[]{:S(2)}, u32[]{:S(2)}) collective-permute-start(f32[32,128]{1,0:T(8,128)S(1)} %reduce_sum.9), channel_id=1, source_target_pairs={{0,112},{1,113},{2,114},{3,115},{4,116},{5,117},{6,118},{7,119},{8... | collective-permute-start | bytes 49160 | tf_op jit(solution)/shard_map/ppermute | solution.py:652
  64.4 15.6 %all-to-all-start.1 = ((f32[16,32,128]{2,1,0:T(8,128)}), f32[16,32,128]{2,1,0:T(8,128)S(1)}, u32[]{:S(2)}, u32[]{:S(2)}) async-start(f32[16,32,128]{2,1,0:T(8,128)} %broadcast_in_dim.2), calls=%async_computation.1 | async-start | bytes 524288 | tf_op jit(solution)/shard_map/all_to_all | solution.py:655
  71.5 23.8 %collective-permute-start.11 = (f32[16,16,128]{2,1,0:T(8,128)S(1)}, f32[16,16,128]{2,1,0:T(8,128)S(1)}, u32[]{:S(2)}, u32[]{:S(2)}) collective-permute-start(f32[16,16,128]{2,1,0:T(8,128)S(1)} %get-tuple-element.58), channel_id=1, source_target_pairs={{0,2},{1,3},{2,0},{3,1},{4,6},{5,7},{6,4},{7,5},{8,10},{9,11},{10,... | collective-permute-start | bytes 393224 | tf_op jit(solution)/shard_map/ppermute | solution.py:622
  (2 other events, 15.4 us)

commit v5 on v4

--- a/solution.py
+++ b/solution.py
@@ -103,8 +103,14 @@
     return [c[s * BAND : (s + 1) * BAND] for s in range(4)]
 
 
-def rows_of(place, slot):
-    return pl.ds(pl.multiple_of(place[slot] * SPAN, SPAN), SPAN)
+def rows_of(slot):
+    member = lax.axis_index("fsdp") ^ slot
+    return pl.ds(pl.multiple_of(member * SPAN, SPAN), SPAN)
+
+
+def turn(other=False):
+    own = lax.div(lax.axis_index("rep"), PLANE) * TURN
+    return TURN - own if other else own
 
 
 def quantum(k):
@@ -128,7 +134,7 @@
     for o, (slot, first, n) in zip(outs, wanted):
         for j in range(n):
             k = len(into)
-            source = g_ref.at[rows_of(place, slot), quantum(first + j), :]
+            source = g_ref.at[rows_of(slot), quantum(first + j), :]
             into.append(pltpu.make_async_copy(source, held.at[k], sems.at[0, k]))
             out.append(pltpu.make_async_copy(cells.at[k], o.at[:, quantum(j), :], sems.at[1, k]))
             into[-1].start()
@@ -150,11 +156,11 @@
     sent = sum(counts)
     count = sent + extra
     where = [(ref, j) for ref, n in zip(pays, counts) for j in range(n)]
-    turn = place[5]
+    other_turn = turn(other=True)
 
     def into(k, ref=None, j=0):
         ref = come[0][0] if ref is None else ref
-        yield pltpu.make_async_copy(g_ref.at[rows_of(place, slot), quantum(first + k), :], g_buf.at[k], sems.at[0, k])
+        yield pltpu.make_async_copy(g_ref.at[rows_of(slot), quantum(first + k), :], g_buf.at[k], sems.at[0, k])
         yield pltpu.make_async_copy(ref.at[:, quantum(j), :], r_buf.at[k], sems.at[1, k])
 
     def out_high(k, ref, j):
@@ -166,10 +172,10 @@
         return pltpu.make_async_copy(pay_buf.at[k, at], ref.at[j, at], sems.at[3, k])
 
     def out_band(k):
-        return pltpu.make_async_copy(band_buf.at[k], band_ref.at[band_at(first + k, turn)], sems.at[4, k])
+        return pltpu.make_async_copy(band_buf.at[k], band_ref.at[band_at(first + k, other_turn)], sems.at[4, k])
 
     if not extra:
-        blank = pltpu.make_async_copy(zero_buf, band_ref.at[band_at(0, turn)], more_sems.at[2])
+        blank = pltpu.make_async_copy(zero_buf, band_ref.at[band_at(0, other_turn)], more_sems.at[2])
     for copy in into(0, *come[0]):
         copy.start()
     consts = load((rows, lanes), (rows_buf, lanes_buf), more_sems)
@@ -233,12 +239,13 @@
     constants, refs = refs[:2], refs[2:]
     cells_ref, band_ref, m_buf, g_buf, r_buf, band_buf, low_buf, early_buf = refs[:8]
     buffers, (sems, more_sems) = refs[8:10], refs[10:]
+    own_turn = turn()
     total = sum(counts)
     where = [(r, j) for r, n in zip(received, counts) for j in range(n)]
 
     def into(k, r=None, j=0):
         r = received[0] if r is None else r
-        yield pltpu.make_async_copy(g_ref.at[rows_of(place, slot), quantum(k), :], g_buf.at[k], sems.at[0, k])
+        yield pltpu.make_async_copy(g_ref.at[rows_of(slot), quantum(k), :], g_buf.at[k], sems.at[0, k])
         yield pltpu.make_async_copy(r.at[:, quantum(j), :], r_buf.at[k], sems.at[1, k])
         yield pltpu.make_async_copy(m_ref.at[:, quantum(k), :], m_buf.at[k], sems.at[2, k])
 
@@ -246,7 +253,7 @@
         return pltpu.make_async_copy(m_buf.at[k], cells_ref.at[:, quantum(k), :], sems.at[3, k])
 
     def out_band(k):
-        return pltpu.make_async_copy(band_buf.at[k], band_ref.at[band_at(k, place[4])], sems.at[4, k])
+        return pltpu.make_async_copy(band_buf.at[k], band_ref.at[band_at(k, own_turn)], sems.at[4, k])
 
     early = pltpu.make_async_copy(early_ref, early_buf, more_sems.at[2])
     for copy in (*into(0, *where[0]), early):
@@ -291,6 +298,7 @@
     out_ref, last_ref, top_ref, bottom_ref = refs[:4]
     cells_buf, band_buf, low_buf, g_buf, r_buf, theirs_buf = refs[4:10]
     buffers, (sems, more_sems) = refs[10:14], refs[14:]
+    own_turn = turn()
     total = cells_buf.shape[0]
     split = top_ref.shape[0]
 
@@ -306,7 +314,7 @@
         yield pltpu.make_async_copy(theirs_buf.at[pl.ds(split, SPAN - split)], bottom_ref, more_sems.at[6])
 
     theirs = [
-        pltpu.make_async_copy(g_ref.at[rows_of(place, slot), quantum(total - 1), :], g_buf, more_sems.at[7]),
+        pltpu.make_async_copy(g_ref.at[rows_of(slot), quantum(total - 1), :], g_buf, more_sems.at[7]),
         pltpu.make_async_copy(r_ref.at[:, quantum(r_ref.shape[1] // QUANTUM - 1), :], r_buf, more_sems.at[8]),
         pltpu.make_async_copy(bands_ref, band_buf, more_sems.at[9]),
     ]
@@ -328,7 +336,7 @@
 
     def body(k, _):
         into(k).wait()
-        turned = lax.rem(k + total - lax.div(place[4], 2), total)
+        turned = lax.rem(k + total - lax.div(own_turn, 2), total)
         cells_buf[k] = cells_buf[k] - back(bands_of(low_buf[turned]), low_back[...])
 
         @pl.when(k < total - 1)
@@ -402,6 +410,7 @@
 
 
 def update_kernel(scale, count, place, band_ref, low_back, band_back, out_ref, band_buf, low_rows, back_buf, out_buf, low_buf, sems, const_sems):
+    own_turn = turn()
     for copy in load((band_ref, low_back, band_back), (band_buf, low_rows, back_buf), const_sems):
         copy.wait()
     b = band_buf[...].reshape(count * SPAN, LANES) * scale
@@ -411,7 +420,7 @@
         return pltpu.make_async_copy(out_buf.at[k], out_ref.at[:, quantum(k), :], sems.at[k])
 
     def body(k, _):
-        turned = lax.rem(k + count - lax.div(place[4], 2), count)
+        turned = lax.rem(k + count - lax.div(own_turn, 2), count)
         out_buf[k] = back(bands_of(low_buf[turned]), low_rows[...])
         out(k).start()
         return 0
@@ -426,11 +435,11 @@
 
 
 def call(kernel, place, operands, outs, scratch, aliases, vmem):
-    scalars = [] if place is None else [place]
+    operands = operands if place is None else [place, *operands]
     return pl.pallas_call(
         kernel,
         grid_spec=pltpu.PrefetchScalarGridSpec(
-            num_scalar_prefetch=len(scalars),
+            num_scalar_prefetch=0,
             grid=(),
             in_specs=[ANY] * len(operands),
             out_specs=[ANY] * len(outs),
@@ -440,7 +449,7 @@
         input_output_aliases=aliases,
         cost_estimate=pl.CostEstimate(flops=0, bytes_accessed=0, transcendentals=0),
         compiler_params=pltpu.CompilerParams(vmem_limit_bytes=vmem * 1024 * 1024),
-    )(*scalars, *operands)
+    )(*operands)
 
 
 def floats(*shape):
@@ -610,8 +619,7 @@
     m = tiles(momentum[0])
     count = m.shape[1] // QUANTUM
     member = lax.axis_index("fsdp")
-    turn = lax.axis_index("rep") // PLANE * TURN
-    place = jnp.stack([member, member ^ 1, member ^ 2, member ^ 3, turn, TURN - turn]).astype(jnp.int32)
+    place = jnp.full((8, LANES), member, jnp.int32)
     over_core = [(f, f ^ 1) for f in range(4)]
     over_z = [(f, f ^ 2) for f in range(4)]
 
@@ -622,12 +630,12 @@
         return lax.ppermute(x, "fsdp", over_z)
 
     def head(slot):
-        return lax.dynamic_slice(g, (place[slot] * SPAN, 0, 0), (SPAN, QUANTUM, LANES)).astype(jnp.float32)
+        return lax.dynamic_slice(g, ((member ^ slot) * SPAN, 0, 0), (SPAN, QUANTUM, LANES)).astype(jnp.float32)
 
     place1, cells = tie(place, head(3))
-    (more,) = cast(place1, g, (3, 1, SECOND))
+    more, own = cast(place1, g, (3, 1, SECOND), (2, 0, 1))
     got, more = tie(core(cells), more)
-    cells = head(2) + got
+    cells = own + got
     early = link(cells)
     pay, other_band = encoded(place, g, [core(more)], 1, (SECOND,), 2, mats)
     second = link(pay)

time: 97.4 us -> 95.4 us (0.979)
  Pallas kernels: 40.1 us -> 35.6 us
  waiting for transfers between devices: 19.3 us -> 23.1 us
    pallas_call x11, Pallas kernels: 40.1 us -> 35.6 us  [call(): pl.pallas_call(kernel, grid_spec=pltpu.PrefetchScalarGridSpec(num_scalar_...]
    ppermute x5, waiting for transfers between devices: 9.42 us -> 11.4 us  [link(): return lax.ppermute(x, 'fsdp', over_z)]
    ppermute x5, starting transfers between devices: 7.65 us -> 8.64 us  [link(): return lax.ppermute(x, 'fsdp', over_z)]
  transfers between devices with their start and end apart: 18 -> 18, of which waited for: 12 -> 11; matrix products, arithmetic and copies ran while one was open for 4% -> 3% of each run, Pallas kernels for 41% -> 37%
where the time goes in v5:
time: 95.4 us; the launch traced here: 94.2 us
  Pallas kernels  35.6 us (37%)
  starting transfers between devices  31 us (32%)
  waiting for transfers between devices  23.1 us (24%)
  other arithmetic  2.79 us (3%)
    pallas_call x11, Pallas kernels, call(): pl.pallas_call(kernel, grid_spec=pltpu.PrefetchScalarGridSpec(num_scalar_...  35.6 us
    ppermute x5, waiting for transfers between devices, link(): return lax.ppermute(x, 'fsdp', over_z)  11.4 us
    ppermute x5, starting transfers between devices, link(): return lax.ppermute(x, 'fsdp', over_z)  8.64 us
    all_to_all x1, starting transfers between devices, per_device(): lax.all_to_all(spread, 'rep', 0, 0, axis_index_groups=groups, tiled=True)  7.13 us
    all_to_all x1, starting transfers between devices, per_device(): lax.all_to_all(own_band + wrapped, 'rep', 0, 0, axis_index_groups=groups,...  7.09 us
    ppermute x1, waiting for transfers between devices, per_device(): total = part + lax.ppermute(part, names, steps(rep_count, TURN, 0))  4.15 us
    ppermute x1, starting transfers between devices, per_device(): total = part + lax.ppermute(part, names, steps(rep_count, TURN, 0))  3.38 us
    all_to_all x1, waiting for transfers between devices, per_device(): lax.all_to_all(own_band + wrapped, 'rep', 0, 0, axis_index_groups=groups,...  2.61 us
  transfers between devices with their start and end apart: 18, of which 11 were waited for; matrix products, arithmetic and copies ran while one was open for 3% of the time, Pallas kernels for 37%

profile of v5, /device:TPU:0, one launch (start us, length us, event | category | flops | bytes accessed | tf_op | source)
XLA Modules:
  0.0 94.2 jit_solution(10313810475306888562)
XLA Ops:
  1.8 1.7 %shard_map.113 = (f32[64,64,128]{2,1,0:T(8,128)S(1)}, f32[64,16,128]{2,1,0:T(8,128)S(1)}) custom-call(s32[8,128]{1,0:T(8,128)S(1)} %broadcast_in_dim.4.place, bf16[256,128,128]{2,1,0:T(8,128)(2,1)} %bitcast.21), custom_call_target="tpu_custom_call" | custom-call | tf_op jit(solution)/shard_map/pallas_call | solution.py:439
  4.0 2.1 %collective-permute-start.1 = (f32[64,16,128]{2,1,0:T(8,128)S(1)}, f32[64,16,128]{2,1,0:T(8,128)S(1)}, u32[]{:S(2)}, u32[]{:S(2)}) collective-permute-start(f32[64,16,128]{2,1,0:T(8,128)S(1)} %add.13), channel_id=1, source_target_pairs={{0,2},{1,3},{2,0},{3,1},{4,6},{5,7},{6,4},{7,5},{8,10},{9,11},{10,... | collective-permute-start | bytes 1572872 | tf_op jit(solution)/shard_map/ppermute | solution.py:630
  6.1 1.7 %collective-permute-done.2.refs_0_ = f32[64,64,128]{2,1,0:T(8,128)S(1)} collective-permute-done((f32[64,64,128]{2,1,0:T(8,128)S(1)}, f32[64,64,128]{2,1,0:T(8,128)S(1)}, u32[]{:S(2)}, u32[]{:S(2)}) %collective-permute-start.2) | collective-permute-done | bytes 2097184 | tf_op jit(solution)/shard_map/ppermute | solution.py:627
  7.8 3.9 %shard_map.114 = (f32[4,960,128]{2,1,0:T(8,128)}, f32[16,32,128]{2,1,0:T(8,128)S(1)}) custom-call(s32[8,128]{1,0:T(8,128)S(1)} %broadcast_in_dim.4.place, bf16[256,128,128]{2,1,0:T(8,128)(2,1)} %bitcast.22, f32[64,64,128]{2,1,0:T(8,128)S(1)} %collective-permute-done.2.refs_0_, bf16[64,192]{1,0:T(8,128)(2,1)S(1)} %copy-done.5, bf16[1536,512]{1,0:T(8,128)(2,1)S(1)} %copy-done), custom_call_target="tpu_custom_call" | custom-call | tf_op jit(solution)/shard_map/pallas_call | solution.py:439
  11.8 2.3 %shard_map.115 = (f32[64,16,128]{2,1,0:T(8,128)S(1)}, f32[64,16,128]{2,1,0:T(8,128)S(1)}, f32[64,16,128]{2,1,0:T(8,128)S(1)}, f32[64,32,128]{2,1,0:T(8,128)S(1)}...) custom-call(s32[8,128]{1,0:T(8,128)S(1)} %broadcast_in_dim.4.place, ...), custom_call_target="tpu_custom_call" | custom-call | tf_op jit(solution)/shard_map/pallas_call | solution.py:439
  14.5 2.0 %collective-permute-start.15 = (f32[4,960,128]{2,1,0:T(8,128)}, f32[4,960,128]{2,1,0:T(8,128)}, u32[]{:S(2)}, u32[]{:S(2)}) collective-permute-start(f32[4,960,128]{2,1,0:T(8,128)} %get-tuple-element.46), channel_id=1, source_target_pairs={{0,2},{1,3},{2,0},{3,1},{4,6},{5,7},{6,4},{7,5},{8,10},{9,11},{10,... | collective-permute-start | bytes 5898248 | tf_op jit(solution)/shard_map/ppermute | solution.py:630
  17.0 1.8 %collective-permute-done.1.early_ref = f32[64,16,128]{2,1,0:T(8,128)S(1)} collective-permute-done((f32[64,16,128]{2,1,0:T(8,128)S(1)}, f32[64,16,128]{2,1,0:T(8,128)S(1)}, u32[]{:S(2)}, u32[]{:S(2)}) %collective-permute-start.1) | collective-permute-done | bytes 524320 | tf_op jit(solution)/shard_map/ppermute | solution.py:630
  19.9 3.3 %shard_map.117 = (f32[2,960,128]{2,1,0:T(8,128)}, f32[16,32,128]{2,1,0:T(8,128)S(1)}) custom-call(s32[8,128]{1,0:T(8,128)S(1)} %broadcast_in_dim.4.place, bf16[256,128,128]{2,1,0:T(8,128)(2,1)} %bitcast.24, f32[64,16,128]{2,1,0:T(8,128)S(1)} %collective-permute-done.7.refs_0_, ...), custom_call_target="tpu_custom_call", output_to_operand_aliasing={{1}: (7, {})} | custom-call | tf_op jit(solution)/shard_map/pallas_call | solution.py:439
  23.2 2.0 %collective-permute-start.13 = (f32[2,960,128]{2,1,0:T(8,128)}, f32[2,960,128]{2,1,0:T(8,128)}, u32[]{:S(2)}, u32[]{:S(2)}) collective-permute-start(f32[2,960,128]{2,1,0:T(8,128)} %get-tuple-element.64), channel_id=1, source_target_pairs={{0,2},{1,3},{2,0},{3,1},{4,6},{5,7},{6,4},{7,5},{8,10},{9,11},{10,... | collective-permute-start | bytes 2949128 | tf_op jit(solution)/shard_map/ppermute | solution.py:630
  25.2 2.5 %collective-permute-start.10 = (f32[16,32,128]{2,1,0:T(8,128)S(1)}, f32[16,32,128]{2,1,0:T(8,128)S(1)}, u32[]{:S(2)}, u32[]{:S(2)}) collective-permute-start(f32[16,32,128]{2,1,0:T(8,128)S(1)} %get-tuple-element.59), channel_id=1, source_target_pairs={{0,66},{1,67},{2,64},{3,65},{4,70},{5,71},{6,68},{7,69},{8,74},{9,... | collective-permute-start | bytes 786440 | tf_op jit(solution)/shard_map/ppermute | solution.py:651
  27.8 5.5 %shard_map.116 = (f32[64,128,128]{2,1,0:T(8,128)}, f32[16,32,128]{2,1,0:T(8,128)S(1)}) custom-call(s32[8,128]{1,0:T(8,128)S(1)} %broadcast_in_dim.4.place, f32[64,128,128]{2,1,0:T(8,128)} %bitcast.28, bf16[256,128,128]{2,1,0:T(8,128)(2,1)} %bitcast.25, f32[64,16,128]{2,1,0:T(8,128)S(1)} %collective-permute-done.1.early_ref, ...), custom_call_target="tpu_custom_call" | custom-call | tf_op jit(solution)/shard_map/pallas_call | solution.py:439
  35.2 7.1 %all-to-all-start = ((f32[16,32,128]{2,1,0:T(8,128)}), f32[16,32,128]{2,1,0:T(8,128)}, u32[]{:S(2)}, u32[]{:S(2)}) async-start(f32[16,32,128]{2,1,0:T(8,128)} %add.14), calls=%async_computation | async-start | bytes 524288 | tf_op jit(solution)/shard_map/all_to_all | solution.py:656
  42.3 5.2 %shard_map.118 = (f32[64,128,128]{2,1,0:T(8,128)}, f32[64,16,128]{2,1,0:T(8,128)S(1)}, f32[48,16,128]{2,1,0:T(8,128)}, f32[16,16,128]{2,1,0:T(8,128)S(1)}) custom-call(s32[8,128]{1,0:T(8,128)S(1)} %broadcast_in_dim.4.place, f32[64,128,128]{2,1,0:T(8,128)} %get-tuple-element.60.cells_ref, ...), custom_call_target="tpu_custom_call", output_to_operand_aliasing={{0}: (1, {})} | custom-call | tf_op jit(solution)/shard_map/pallas_call | solution.py:439
  48.2 2.6 %all-to-all-done = f32[16,32,128]{2,1,0:T(8,128)} async-done(((f32[16,32,128]{2,1,0:T(8,128)}), f32[16,32,128]{2,1,0:T(8,128)}, u32[]{:S(2)}, u32[]{:S(2)}) %all-to-all-start) | async-done | bytes 262176 | tf_op jit(solution)/shard_map/all_to_all | solution.py:656
  51.8 3.4 %collective-permute-start.14 = (f32[32,128]{1,0:T(8,128)S(1)}, f32[32,128]{1,0:T(8,128)S(1)}, u32[]{:S(2)}, u32[]{:S(2)}) collective-permute-start(f32[32,128]{1,0:T(8,128)S(1)} %reduce_sum.9), channel_id=1, source_target_pairs={{0,112},{1,113},{2,114},{3,115},{4,116},{5,117},{6,118},{7,119},{8... | collective-permute-start | bytes 49160 | tf_op jit(solution)/shard_map/ppermute | solution.py:660
  55.1 4.2 %collective-permute-done.14 = f32[32,128]{1,0:T(8,128)S(1)} collective-permute-done((f32[32,128]{1,0:T(8,128)S(1)}, f32[32,128]{1,0:T(8,128)S(1)}, u32[]{:S(2)}, u32[]{:S(2)}) %collective-permute-start.14) | collective-permute-done | bytes 16416 | tf_op jit(solution)/shard_map/ppermute | solution.py:660
  59.3 2.1 %collective-permute-done.15.pay_ref = f32[4,960,128]{2,1,0:T(8,128)} collective-permute-done((f32[4,960,128]{2,1,0:T(8,128)}, f32[4,960,128]{2,1,0:T(8,128)}, u32[]{:S(2)}, u32[]{:S(2)}) %collective-permute-start.15) | collective-permute-done | bytes 1966112 | tf_op jit(solution)/shard_map/ppermute | solution.py:630
  62.1 7.1 %all-to-all-start.1 = ((f32[16,32,128]{2,1,0:T(8,128)}), f32[16,32,128]{2,1,0:T(8,128)S(1)}, u32[]{:S(2)}, u32[]{:S(2)}) async-start(f32[16,32,128]{2,1,0:T(8,128)} %broadcast_in_dim.10), calls=%async_computation.1 | async-start | bytes 524288 | tf_op jit(solution)/shard_map/all_to_all | solution.py:663
  69.3 1.9 %collective-permute-start.11 = (f32[16,16,128]{2,1,0:T(8,128)S(1)}, f32[16,16,128]{2,1,0:T(8,128)S(1)}, u32[]{:S(2)}, u32[]{:S(2)}) collective-permute-start(f32[16,16,128]{2,1,0:T(8,128)S(1)} %get-tuple-element.62), channel_id=1, source_target_pairs={{0,2},{1,3},{2,0},{3,1},{4,6},{5,7},{6,4},{7,5},{8,10},{9,11},{10,... | collective-permute-start | bytes 393224 | tf_op jit(solution)/shard_map/ppermute | solution.py:630
  71.2 4.7 %shard_map.119.base_ref = f32[64,128,128]{2,1,0:T(8,128)} custom-call(f32[4,960,128]{2,1,0:T(8,128)} %collective-permute-done.15.pay_ref, bf16[64,192]{1,0:T(8,128)(2,1)S(1)} %copy-done.4, bf16[1152,512]{1,0:T(8,128)(2,1)S(1)} %copy-done.1, f32[64,128,128]{2,1,0:T(8,128)} %get-tuple-element.67.base_ref), custom_call_target="tpu_custom_call", output_to_operand_aliasing={{}: (3, {})} | custom-call | tf_op jit(solution)/shard_map/pallas_call | solution.py:439
  75.9 1.8 %all-to-all-done.1.band_ref = f32[16,32,128]{2,1,0:T(8,128)S(1)} async-done(((f32[16,32,128]{2,1,0:T(8,128)}), f32[16,32,128]{2,1,0:T(8,128)S(1)}, u32[]{:S(2)}, u32[]{:S(2)}) %all-to-all-start.1) | async-done | bytes 262176 | tf_op jit(solution)/shard_map/all_to_all | solution.py:663
  77.7 3.4 %shard_map.120 = f32[64,128,128]{2,1,0:T(8,128)} custom-call(s32[8,128]{1,0:T(8,128)S(1)} %broadcast_in_dim.4.place, f32[16,32,128]{2,1,0:T(8,128)S(1)} %all-to-all-done.1.band_ref, bf16[64,48]{1,0:T(8,128)(2,1)S(1)} %copy-done.6, bf16[384,512]{1,0:T(8,128)(2,1)S(1)} %copy-done.2), custom_call_target="tpu_custom_call" | custom-call | tf_op jit(solution)/shard_map/pallas_call | solution.py:439
  82.5 3.3 %shard_map.121.base_ref = f32[64,128,128]{2,1,0:T(8,128)} custom-call(f32[2,960,128]{2,1,0:T(8,128)} %collective-permute-done.13.pay_ref, bf16[64,192]{1,0:T(8,128)(2,1)S(1)} %copy-done.4, bf16[1152,512]{1,0:T(8,128)(2,1)S(1)} %copy-done.1, f32[64,128,128]{2,1,0:T(8,128)} %shard_map.119.base_ref), custom_call_target="tpu_custom_call", output_to_operand_aliasing={{}: (3, {})} | custom-call | tf_op jit(solution)/shard_map/pallas_call | solution.py:439
  85.8 5.0 %collective-permute-done.12.there_ref = f32[48,16,128]{2,1,0:T(8,128)S(1)} collective-permute-done((f32[48,16,128]{2,1,0:T(8,128)}, f32[48,16,128]{2,1,0:T(8,128)S(1)}, u32[]{:S(2)}, u32[]{:S(2)}) %collective-permute-start.12) | collective-permute-done | bytes 393248 | tf_op jit(solution)/shard_map/ppermute | solution.py:630
  (46 shorter events, 12.5 us)
Async XLA Ops:
  1.7 2.0 %collective-permute-start = (f32[64,16,128]{2,1,0:T(8,128)S(1)}, f32[64,16,128]{2,1,0:T(8,128)S(1)}, u32[]{:S(2)}, u32[]{:S(2)}) collective-permute-start(f32[64,16,128]{2,1,0:T(8,128)S(1)} %dynamic-slice_convert_fusion), channel_id=1, source_target_pairs={{0,1},{1,0},{2,3},{3,2},{4,5},{5,4},{6,7},{7,6},{8,9},{9,8},{10,11... | collective-permute-start | bytes 1572872 | tf_op jit(solution)/shard_map/ppermute | solution.py:627
  3.7 4.2 %collective-permute-start.2 = (f32[64,64,128]{2,1,0:T(8,128)S(1)}, f32[64,64,128]{2,1,0:T(8,128)S(1)}, u32[]{:S(2)}, u32[]{:S(2)}) collective-permute-start(f32[64,64,128]{2,1,0:T(8,128)S(1)} %get-tuple-element.45), channel_id=1, source_target_pairs={{0,1},{1,0},{2,3},{3,2},{4,5},{5,4},{6,7},{7,6},{8,9},{9,8},{10,11... | collective-permute-start | bytes 6291464 | tf_op jit(solution)/shard_map/ppermute | solution.py:627
  4.0 14.8 %collective-permute-start.1 = (f32[64,16,128]{2,1,0:T(8,128)S(1)}, f32[64,16,128]{2,1,0:T(8,128)S(1)}, u32[]{:S(2)}, u32[]{:S(2)}) collective-permute-start(f32[64,16,128]{2,1,0:T(8,128)S(1)} %add.13), channel_id=1, source_target_pairs={{0,2},{1,3},{2,0},{3,1},{4,6},{5,7},{6,4},{7,5},{8,10},{9,11},{10,... | collective-permute-start | bytes 1572872 | tf_op jit(solution)/shard_map/ppermute | solution.py:630
  14.1 4.7 %collective-permute-start.7 = (f32[64,16,128]{2,1,0:T(8,128)S(1)}, f32[64,16,128]{2,1,0:T(8,128)S(1)}, u32[]{:S(2)}, u32[]{:S(2)}) collective-permute-start(f32[64,16,128]{2,1,0:T(8,128)S(1)} %get-tuple-element.55), channel_id=1, source_target_pairs={{0,1},{1,0},{2,3},{3,2},{4,5},{5,4},{6,7},{7,6},{8,9},{9,8},{10,11... | collective-permute-start | bytes 1572872 | tf_op jit(solution)/shard_map/ppermute | solution.py:627
  14.5 46.9 %collective-permute-start.15 = (f32[4,960,128]{2,1,0:T(8,128)}, f32[4,960,128]{2,1,0:T(8,128)}, u32[]{:S(2)}, u32[]{:S(2)}) collective-permute-start(f32[4,960,128]{2,1,0:T(8,128)} %get-tuple-element.46), channel_id=1, source_target_pairs={{0,2},{1,3},{2,0},{3,1},{4,6},{5,7},{6,4},{7,5},{8,10},{9,11},{10,... | collective-permute-start | bytes 5898248 | tf_op jit(solution)/shard_map/ppermute | solution.py:630
  16.5 2.8 %collective-permute-start.8 = (f32[64,16,128]{2,1,0:T(8,128)S(1)}, f32[64,16,128]{2,1,0:T(8,128)S(1)}, u32[]{:S(2)}, u32[]{:S(2)}) collective-permute-start(f32[64,16,128]{2,1,0:T(8,128)S(1)} %get-tuple-element.56), channel_id=1, source_target_pairs={{0,1},{1,0},{2,3},{3,2},{4,5},{5,4},{6,7},{7,6},{8,9},{9,8},{10,11... | collective-permute-start | bytes 1572872 | tf_op jit(solution)/shard_map/ppermute | solution.py:627
  16.5 2.9 %collective-permute-start.9 = (f32[64,16,128]{2,1,0:T(8,128)S(1)}, f32[64,16,128]{2,1,0:T(8,128)S(1)}, u32[]{:S(2)}, u32[]{:S(2)}) collective-permute-start(f32[64,16,128]{2,1,0:T(8,128)S(1)} %get-tuple-element.57), channel_id=1, source_target_pairs={{0,1},{1,0},{2,3},{3,2},{4,5},{5,4},{6,7},{7,6},{8,9},{9,8},{10,11... | collective-permute-start | bytes 1572872 | tf_op jit(solution)/shard_map/ppermute | solution.py:627
  18.8 4.4 %collective-permute-start.6 = (f32[64,32,128]{2,1,0:T(8,128)S(1)}, f32[64,32,128]{2,1,0:T(8,128)S(1)}, u32[]{:S(2)}, u32[]{:S(2)}) collective-permute-start(f32[64,32,128]{2,1,0:T(8,128)S(1)} %get-tuple-element.53), channel_id=1, source_target_pairs={{0,1},{1,0},{2,3},{3,2},{4,5},{5,4},{6,7},{7,6},{8,9},{9,8},{10,11... | collective-permute-start | bytes 3145736 | tf_op jit(solution)/shard_map/ppermute | solution.py:627
  18.8 6.4 %collective-permute-start.3 = (f32[64,32,128]{2,1,0:T(8,128)S(1)}, f32[64,32,128]{2,1,0:T(8,128)S(1)}, u32[]{:S(2)}, u32[]{:S(2)}) collective-permute-start(f32[64,32,128]{2,1,0:T(8,128)S(1)} %get-tuple-element.50), channel_id=1, source_target_pairs={{0,1},{1,0},{2,3},{3,2},{4,5},{5,4},{6,7},{7,6},{8,9},{9,8},{10,11... | collective-permute-start | bytes 3145736 | tf_op jit(solution)/shard_map/ppermute | solution.py:627
  19.3 8.4 %collective-permute-start.4 = (f32[64,32,128]{2,1,0:T(8,128)S(1)}, f32[64,32,128]{2,1,0:T(8,128)S(1)}, u32[]{:S(2)}, u32[]{:S(2)}) collective-permute-start(f32[64,32,128]{2,1,0:T(8,128)S(1)} %get-tuple-element.51), channel_id=1, source_target_pairs={{0,1},{1,0},{2,3},{3,2},{4,5},{5,4},{6,7},{7,6},{8,9},{9,8},{10,11... | collective-permute-start | bytes 3145736 | tf_op jit(solution)/shard_map/ppermute | solution.py:627
  19.4 8.3 %collective-permute-start.5 = (f32[64,32,128]{2,1,0:T(8,128)S(1)}, f32[64,32,128]{2,1,0:T(8,128)S(1)}, u32[]{:S(2)}, u32[]{:S(2)}) collective-permute-start(f32[64,32,128]{2,1,0:T(8,128)S(1)} %get-tuple-element.52), channel_id=1, source_target_pairs={{0,1},{1,0},{2,3},{3,2},{4,5},{5,4},{6,7},{7,6},{8,9},{9,8},{10,11... | collective-permute-start | bytes 3145736 | tf_op jit(solution)/shard_map/ppermute | solution.py:627
  19.8 7.9 %copy-start.3 = (bf16[1536,128]{1,0:T(8,128)(2,1)S(1)}, bf16[1536,128]{1,0:T(8,128)(2,1)}, u32[]{:S(2)}) copy-start(bf16[1536,128]{1,0:T(8,128)(2,1)} %constant.36.clone.refs_5_.refs_2_) | copy-start | bytes 1179652
  19.8 7.9 %copy-start.7 = (bf16[16,192]{1,0:T(8,128)(2,1)S(1)}, bf16[16,192]{1,0:T(8,128)(2,1)}, u32[]{:S(2)}) copy-start(bf16[16,192]{1,0:T(8,128)(2,1)} %constant.32.clone.refs_4_.refs_0_) | copy-start | bytes 18436
  23.2 59.3 %collective-permute-start.13 = (f32[2,960,128]{2,1,0:T(8,128)}, f32[2,960,128]{2,1,0:T(8,128)}, u32[]{:S(2)}, u32[]{:S(2)}) collective-permute-start(f32[2,960,128]{2,1,0:T(8,128)} %get-tuple-element.64), channel_id=1, source_target_pairs={{0,2},{1,3},{2,0},{3,1},{4,6},{5,7},{6,4},{7,5},{8,10},{9,11},{10,... | collective-permute-start | bytes 2949128 | tf_op jit(solution)/shard_map/ppermute | solution.py:630
  25.2 9.2 %collective-permute-start.10 = (f32[16,32,128]{2,1,0:T(8,128)S(1)}, f32[16,32,128]{2,1,0:T(8,128)S(1)}, u32[]{:S(2)}, u32[]{:S(2)}) collective-permute-start(f32[16,32,128]{2,1,0:T(8,128)S(1)} %get-tuple-element.59), channel_id=1, source_target_pairs={{0,66},{1,67},{2,64},{3,65},{4,70},{5,71},{6,68},{7,69},{8,74},{9,... | collective-permute-start | bytes 786440 | tf_op jit(solution)/shard_map/ppermute | solution.py:651
  27.7 14.5 %copy-start.2 = (bf16[384,512]{1,0:T(8,128)(2,1)S(1)}, bf16[384,512]{1,0:T(8,128)(2,1)}, u32[]{:S(2)}) copy-start(bf16[384,512]{1,0:T(8,128)(2,1)} %constant.37.clone.refs_3_.band_back) | copy-start | bytes 1179652
  27.8 14.5 %copy-start.6 = (bf16[64,48]{1,0:T(8,128)(2,1)S(1)}, bf16[64,48]{1,0:T(8,128)(2,1)}, u32[]{:S(2)}) copy-start(bf16[64,48]{1,0:T(8,128)(2,1)} %constant.33.clone.refs_1_.low_back) | copy-start | bytes 18436
  35.2 15.6 %all-to-all-start = ((f32[16,32,128]{2,1,0:T(8,128)}), f32[16,32,128]{2,1,0:T(8,128)}, u32[]{:S(2)}, u32[]{:S(2)}) async-start(f32[16,32,128]{2,1,0:T(8,128)} %add.14), calls=%async_computation | async-start | bytes 524288 | tf_op jit(solution)/shard_map/all_to_all | solution.py:656
  42.3 28.9 %copy-start.1 = (bf16[1152,512]{1,0:T(8,128)(2,1)S(1)}, bf16[1152,512]{1,0:T(8,128)(2,1)}, u32[]{:S(2)}) copy-start(bf16[1152,512]{1,0:T(8,128)(2,1)} %constant.35.clone.kept_back) | copy-start | bytes 3538948
  42.3 28.9 %copy-start.4 = (bf16[64,192]{1,0:T(8,128)(2,1)S(1)}, bf16[64,192]{1,0:T(8,128)(2,1)}, u32[]{:S(2)}) copy-start(bf16[64,192]{1,0:T(8,128)(2,1)} %constant.31.clone.rows_back) | copy-start | bytes 73732
  47.5 43.3 %collective-permute-start.12 = (f32[48,16,128]{2,1,0:T(8,128)}, f32[48,16,128]{2,1,0:T(8,128)S(1)}, u32[]{:S(2)}, u32[]{:S(2)}) collective-permute-start(f32[48,16,128]{2,1,0:T(8,128)} %get-tuple-element.63), channel_id=1, source_target_pairs={{0,2},{1,3},{2,0},{3,1},{4,6},{5,7},{6,4},{7,5},{8,10},{9,11},{10,... | collective-permute-start | bytes 1179656 | tf_op jit(solution)/shard_map/ppermute | solution.py:630
  51.8 7.5 %collective-permute-start.14 = (f32[32,128]{1,0:T(8,128)S(1)}, f32[32,128]{1,0:T(8,128)S(1)}, u32[]{:S(2)}, u32[]{:S(2)}) collective-permute-start(f32[32,128]{1,0:T(8,128)S(1)} %reduce_sum.9), channel_id=1, source_target_pairs={{0,112},{1,113},{2,114},{3,115},{4,116},{5,117},{6,118},{7,119},{8... | collective-permute-start | bytes 49160 | tf_op jit(solution)/shard_map/ppermute | solution.py:660
  62.1 15.6 %all-to-all-start.1 = ((f32[16,32,128]{2,1,0:T(8,128)}), f32[16,32,128]{2,1,0:T(8,128)S(1)}, u32[]{:S(2)}, u32[]{:S(2)}) async-start(f32[16,32,128]{2,1,0:T(8,128)} %broadcast_in_dim.10), calls=%async_computation.1 | async-start | bytes 524288 | tf_op jit(solution)/shard_map/all_to_all | solution.py:663
  69.3 23.9 %collective-permute-start.11 = (f32[16,16,128]{2,1,0:T(8,128)S(1)}, f32[16,16,128]{2,1,0:T(8,128)S(1)}, u32[]{:S(2)}, u32[]{:S(2)}) collective-permute-start(f32[16,16,128]{2,1,0:T(8,128)S(1)} %get-tuple-element.62), channel_id=1, source_target_pairs={{0,2},{1,3},{2,0},{3,1},{4,6},{5,7},{6,4},{7,5},{8,10},{9,11},{10,... | collective-permute-start | bytes 393224 | tf_op jit(solution)/shard_map/ppermute | solution.py:630
  (2 other events, 12.3 us)

commit v6 on v5

--- a/solution.py
+++ b/solution.py
@@ -57,7 +57,7 @@
     kept, band = lanes[:, : 3 * LANES], lanes[:, 3 * LANES :]
     mats = dict(
         rows=left(t), rows_back=left(t.T), low=left(t[:BAND]), low_back=left(t[:BAND].T),
-        lanes=right(lanes), kept_back=right(kept.T), band=right(band), band_back=right(band.T),
+        lanes=right(lanes), kept=right(kept), kept_back=right(kept.T), band=right(band), band_back=right(band.T),
     )
     return {name: jnp.asarray(a) for name, a in mats.items()}
 
@@ -294,10 +294,10 @@
 
 
 def rest_kernel(slot, place, cells_ref, bands_ref, g_ref, r_ref, *refs):
-    constants, refs = refs[:4], refs[4:]
-    out_ref, last_ref, top_ref, bottom_ref = refs[:4]
-    cells_buf, band_buf, low_buf, g_buf, r_buf, theirs_buf = refs[4:10]
-    buffers, (sems, more_sems) = refs[10:14], refs[14:]
+    constants, refs = refs[:5], refs[5:]
+    out_ref, last_ref, half_ref, top_ref, bottom_ref = refs[:5]
+    cells_buf, band_buf, low_buf, g_buf, r_buf, half_buf, raw_buf = refs[5:12]
+    buffers, (sems, more_sems) = refs[12:17], refs[17:]
     own_turn = turn()
     total = cells_buf.shape[0]
     split = top_ref.shape[0]
@@ -309,30 +309,41 @@
         return pltpu.make_async_copy(cells_buf.at[k], out_ref.at[:, quantum(k), :], sems.at[1, k])
 
     def out_last():
-        yield pltpu.make_async_copy(cells_buf.at[total - 1], last_ref, more_sems.at[4])
-        yield pltpu.make_async_copy(theirs_buf.at[pl.ds(0, split)], top_ref, more_sems.at[5])
-        yield pltpu.make_async_copy(theirs_buf.at[pl.ds(split, SPAN - split)], bottom_ref, more_sems.at[6])
-
-    theirs = [
-        pltpu.make_async_copy(g_ref.at[rows_of(slot), quantum(total - 1), :], g_buf, more_sems.at[7]),
-        pltpu.make_async_copy(r_ref.at[:, quantum(r_ref.shape[1] // QUANTUM - 1), :], r_buf, more_sems.at[8]),
-        pltpu.make_async_copy(bands_ref, band_buf, more_sems.at[9]),
+        yield pltpu.make_async_copy(cells_buf.at[total - 1], last_ref, more_sems.at[5])
+        yield pltpu.make_async_copy(half_buf, half_ref, more_sems.at[6])
+        yield pltpu.make_async_copy(raw_buf.at[pl.ds(0, split)], top_ref, more_sems.at[7])
+        yield pltpu.make_async_copy(raw_buf.at[pl.ds(split, SPAN - split)], bottom_ref, more_sems.at[8])
+
+    copies = [
+        pltpu.make_async_copy(g_ref.at[rows_of(slot), quantum(total - 1), :], g_buf, more_sems.at[9]),
+        pltpu.make_async_copy(r_ref.at[:, quantum(r_ref.shape[1] // QUANTUM - 1), :], r_buf, more_sems.at[10]),
+        pltpu.make_async_copy(bands_ref, band_buf, more_sems.at[11]),
     ]
-    for copy in theirs:
+    for copy in copies:
         copy.start()
     consts = load(constants, buffers, more_sems)
     for k in range(total):
         into(k).start()
-    for copy in (*theirs, *consts):
+    for copy in (*copies, *consts):
         copy.wait()
-    low, low_back, band, band_back = buffers
-
-    theirs_buf[...] = g_buf[...].astype(jnp.float32) + r_buf[...]
-    c = jnp.concatenate(forward(theirs_buf[...], low[...]), axis=0)
-    theirs_band = dot(long(c), band[...])
+    rows, kept, low_back, band, band_back = buffers
+
+    theirs = g_buf[...].astype(jnp.float32) + r_buf[...]
+    c = []
+    for s, x in enumerate(beside(theirs)):
+        c.append(dot(rows[...] if s < 2 else rows[:BAND, :], tall(x)))
+    for k in range(GROUP):
+        half_buf[k * HIGH : (k + 1) * HIGH, :] = c[k // 4][BAND:, k % 4 * LANES : (k % 4 + 1) * LANES]
+    w = dot(long(jnp.concatenate([c[0][:BAND], c[1][:BAND]], axis=0)), kept[...])
+    for i in range(3):
+        at = GROUP * HIGH + i * QUARTER
+        half_buf[at : at + QUARTER, :] = w[:, i * LANES : (i + 1) * LANES]
+    theirs_band = dot(long(jnp.concatenate(c[2:], axis=0)), band[...])
     b = jnp.concatenate([band_buf[...].reshape(total * SPAN, LANES), theirs_band], axis=0)
-    low_buf[...] = dot(long(b), band_back[...]).reshape(total + 1, SPAN, 4 * LANES)
-    theirs_buf[...] = theirs_buf[...] - back(bands_of(low_buf[total]), low_back[...])
+    wide = dot(long(b), band_back[...])
+    low_buf[...] = wide[: total * SPAN].reshape(total, SPAN, 4 * LANES)
+    low = wide[total * SPAN :]
+    raw_buf[...] = theirs[:, GROUP:, :] - back([low[:BAND], low[BAND:]], low_back[...])
 
     def body(k, _):
         into(k).wait()
@@ -393,18 +404,24 @@
         out(k).wait()
 
 
-def add_kernel(first, row, there_ref, last_ref, base_ref, out_ref, there_buf, last_buf, sems):
+def add_kernel(first, row, there_ref, last_ref, base_ref, out_ref, sum_buf, sem):
     rows = pl.ds(row, there_ref.shape[0])
-    into = [
-        pltpu.make_async_copy(there_ref, there_buf, sems.at[0]),
-        pltpu.make_async_copy(last_ref.at[rows], last_buf, sems.at[1]),
-    ]
-    for copy in into:
-        copy.start()
-    for copy in into:
-        copy.wait()
-    last_buf[...] += there_buf[...]
-    out = pltpu.make_async_copy(last_buf, out_ref.at[rows, quantum(first)], sems.at[2])
+    sum_buf[...] = last_ref[rows, GROUP:, :] + there_ref[...]
+    out = pltpu.make_async_copy(sum_buf, out_ref.at[rows, pl.ds(first * QUANTUM + GROUP, GROUP)], sem.at[0])
+    out.start()
+    out.wait()
+
+
+def half_kernel(first, half_ref, last_ref, rows_back, kept_back, base_ref, out_ref, sum_buf, sem):
+    at = GROUP * HIGH
+    w = jnp.concatenate([half_ref[at + i * QUARTER : at + (i + 1) * QUARTER, :] for i in range(3)], axis=1)
+    low = dot(long(w), kept_back[...])
+    parts = []
+    for s in range(2):
+        high = [half_ref[k * HIGH : (k + 1) * HIGH, :] for k in range(4 * s, 4 * s + 4)]
+        parts.append(jnp.concatenate([low[s * BAND : (s + 1) * BAND], jnp.concatenate(high, axis=1)], axis=0))
+    sum_buf[...] = last_ref[:, :GROUP, :] + back(parts, rows_back[...])
+    out = pltpu.make_async_copy(sum_buf, out_ref.at[:, pl.ds(first * QUANTUM, GROUP)], sem.at[0])
     out.start()
     out.wait()
 
@@ -434,14 +451,14 @@
 BANDS = jax.ShapeDtypeStruct((PLANE, QUARTER, LANES), jnp.float32)
 
 
-def call(kernel, place, operands, outs, scratch, aliases, vmem):
+def call(kernel, place, operands, outs, scratch, aliases, vmem, near=0):
     operands = operands if place is None else [place, *operands]
     return pl.pallas_call(
         kernel,
         grid_spec=pltpu.PrefetchScalarGridSpec(
             num_scalar_prefetch=0,
             grid=(),
-            in_specs=[ANY] * len(operands),
+            in_specs=[pl.BlockSpec(memory_space=pltpu.VMEM)] * near + [ANY] * (len(operands) - near),
             out_specs=[ANY] * len(outs),
             scratch_shapes=scratch,
         ),
@@ -527,9 +544,9 @@
 
 
 def rest(place, cells, bands, g, received, slot, mats):
-    values = [mats[name] for name in ("low", "low_back", "band", "band_back")]
+    values = [mats[name] for name in ("rows", "kept", "low_back", "band", "band_back")]
     n = cells.shape[1] // QUANTUM
-    one = [pltpu.VMEM((SPAN, QUANTUM, LANES), dtype) for dtype in (jnp.bfloat16, jnp.float32, jnp.float32)]
+    half = (GROUP * HIGH + 3 * QUARTER, LANES)
     return call(
         functools.partial(rest_kernel, slot),
         place,
@@ -537,15 +554,17 @@
         [
             floats(*cells.shape),
             floats(SPAN, QUANTUM, LANES),
-            floats(SPLIT, QUANTUM, LANES),
-            floats(SPAN - SPLIT, QUANTUM, LANES),
+            floats(*half),
+            floats(SPLIT, GROUP, LANES),
+            floats(SPAN - SPLIT, GROUP, LANES),
         ],
         held(n, jnp.float32)
         + [pltpu.VMEM(BANDS.shape, jnp.float32)]
-        + lows(n + 1)
-        + one
+        + lows(n)
+        + [pltpu.VMEM((SPAN, QUANTUM, LANES), dtype) for dtype in (jnp.bfloat16, jnp.float32)]
+        + [pltpu.VMEM(half, jnp.float32), pltpu.VMEM((SPAN, GROUP, LANES), jnp.float32)]
         + same(values)
-        + [sems(2, n), sems(10)],
+        + [sems(2, n), sems(12)],
         {1: 0},
         MOST,
     )
@@ -557,9 +576,23 @@
         None,
         [there, last, base],
         [floats(*base.shape)],
-        same([there, there]) + [sems(3)],
+        same([there]) + [sems(1)],
         {2: 0},
         MOST,
+        2,
+    )[0]
+
+
+def added_half(there, last, base, first, mats):
+    return call(
+        functools.partial(half_kernel, first),
+        None,
+        [there, last, mats["rows_back"], mats["kept_back"], base],
+        [floats(*base.shape)],
+        [pltpu.VMEM((SPAN, GROUP, LANES), jnp.float32), sems(1)],
+        {4: 0},
+        MOST,
+        4,
     )[0]
 
 
@@ -650,12 +683,12 @@
     names = ("rep", "fsdp")
     wrapped = lax.ppermute(other_band, names, steps(rep_count, 0, 2))
     cells, own_band = moments(place, m, g, early, mine, 0, mats)
-    base, last, top, bottom = rest(place, cells, own_band, g, got[-1], 2, mats)
+    base, last, half, top, bottom = rest(place, cells, own_band, g, got[-1], 2, mats)
 
     groups = [[h * PLANE + i for i in range(PLANE)] for h in range(rep_count // PLANE)]
     met = lax.all_to_all(own_band + wrapped, "rep", 0, 0, axis_index_groups=groups, tiled=True)
     met, bottom = tie(met, bottom)
-    top, bottom = link(top), link(bottom)
+    half, top, bottom = link(half), link(top), link(bottom)
     part = jnp.sum(met.reshape(PLANE, QUARTER, LANES), axis=0)
     total = part + lax.ppermute(part, names, steps(rep_count, TURN, 0))
     total, second = tie(total, second)
@@ -666,6 +699,8 @@
 
     third, update = tie(third, update)
     out = decoded(third, out, 1 + SECOND, mats)
+    half, out = tie(half, out)
+    out = added_half(half, last, out, count - 1, mats)
     top, out = tie(top, out)
     out = added(top, last, out, count - 1, 0)
     bottom, out = tie(bottom, out)

time: 95.4 us -> 94.7 us (level)
  waiting for transfers between devices: 23.1 us -> 17 us
  local copies, waits for them, and re-layouts: 0.78 us -> 3.4 us
  starting transfers between devices: 31 us -> 33.3 us
    unnamed x16 -> x22, local copies, waits for them, and re-layouts: 0.05 us -> 2.67 us
    all_to_all x1, waiting for transfers between devices: 2.61 us -> 0.63 us  [per_device(): lax.all_to_all(own_band + wrapped, 'rep', 0, 0, axis_index_groups=groups,...]
    all_to_all x1, waiting for transfers between devices: 1.85 us -> 0.01 us  [per_device(): lax.all_to_all(spread, 'rep', 0, 0, axis_index_groups=groups, tiled=True)]
    ppermute x5 -> x6, waiting for transfers between devices: 11.4 us -> 10 us  [link(): return lax.ppermute(x, 'fsdp', over_z)]
    ppermute x5 -> x6, starting transfers between devices: 8.64 us -> 9.97 us  [link(): return lax.ppermute(x, 'fsdp', over_z)]
    ppermute x1, starting transfers between devices: 3.38 us -> 4.35 us  [per_device(): total = part + lax.ppermute(part, names, steps(rep_count, TURN, 0))]
    ppermute x1, waiting for transfers between devices: 4.15 us -> 3.19 us  [per_device(): total = part + lax.ppermute(part, names, steps(rep_count, TURN, 0))]
    pallas_call x11 -> x12, Pallas kernels: 35.6 us -> 36.2 us  [call(): pl.pallas_call(kernel, grid_spec=pltpu.PrefetchScalarGridSpec(num_scalar_...]
  transfers between devices with their start and end apart: 18 -> 19, of which waited for: 11 -> 11; matrix products, arithmetic and copies ran while one was open for 3% -> 3% of each run, Pallas kernels for 37% -> 38%
where the time goes in v6:
time: 94.7 us; the launch traced here: 93.5 us
  Pallas kernels  36.2 us (38%)
  starting transfers between devices  33.3 us (35%)
  waiting for transfers between devices  17 us (18%)
  local copies, waits for them, and re-layouts  3.4 us (4%)
  other arithmetic  2.79 us (3%)
    pallas_call x12, Pallas kernels, call(): pl.pallas_call(kernel, grid_spec=pltpu.PrefetchScalarGridSpec(num_scalar_...  36.2 us
    ppermute x6, waiting for transfers between devices, link(): return lax.ppermute(x, 'fsdp', over_z)  10 us
    ppermute x6, starting transfers between devices, link(): return lax.ppermute(x, 'fsdp', over_z)  9.97 us
    all_to_all x1, starting transfers between devices, per_device(): lax.all_to_all(spread, 'rep', 0, 0, axis_index_groups=groups, tiled=True)  7.13 us
    all_to_all x1, starting transfers between devices, per_device(): lax.all_to_all(own_band + wrapped, 'rep', 0, 0, axis_index_groups=groups,...  7.08 us
    ppermute x1, starting transfers between devices, per_device(): total = part + lax.ppermute(part, names, steps(rep_count, TURN, 0))  4.35 us
    ppermute x1, waiting for transfers between devices, per_device(): total = part + lax.ppermute(part, names, steps(rep_count, TURN, 0))  3.19 us
    unnamed x22, local copies, waits for them, and re-layouts  2.67 us
  transfers between devices with their start and end apart: 19, of which 11 were waited for; matrix products, arithmetic and copies ran while one was open for 3% of the time, Pallas kernels for 38%

profile of v6, /device:TPU:0, one launch (start us, length us, event | category | flops | bytes accessed | tf_op | source)
XLA Modules:
  0.0 93.5 jit_solution(3628468977024812574)
XLA Ops:
  1.8 1.7 %shard_map.122 = (f32[64,64,128]{2,1,0:T(8,128)S(1)}, f32[64,16,128]{2,1,0:T(8,128)S(1)}) custom-call(s32[8,128]{1,0:T(8,128)S(1)} %broadcast_in_dim.4.place, bf16[256,128,128]{2,1,0:T(8,128)(2,1)} %bitcast.21), custom_call_target="tpu_custom_call" | custom-call | tf_op jit(solution)/shard_map/pallas_call | solution.py:456
  4.0 2.1 %collective-permute-start.1 = (f32[64,16,128]{2,1,0:T(8,128)S(1)}, f32[64,16,128]{2,1,0:T(8,128)S(1)}, u32[]{:S(2)}, u32[]{:S(2)}) collective-permute-start(f32[64,16,128]{2,1,0:T(8,128)S(1)} %add.13), channel_id=1, source_target_pairs={{0,2},{1,3},{2,0},{3,1},{4,6},{5,7},{6,4},{7,5},{8,10},{9,11},{10,... | collective-permute-start | bytes 1572872 | tf_op jit(solution)/shard_map/ppermute | solution.py:663
  6.1 1.7 %collective-permute-done.2.refs_0_ = f32[64,64,128]{2,1,0:T(8,128)S(1)} collective-permute-done((f32[64,64,128]{2,1,0:T(8,128)S(1)}, f32[64,64,128]{2,1,0:T(8,128)S(1)}, u32[]{:S(2)}, u32[]{:S(2)}) %collective-permute-start.2) | collective-permute-done | bytes 2097184 | tf_op jit(solution)/shard_map/ppermute | solution.py:660
  7.8 4.0 %shard_map.123 = (f32[4,960,128]{2,1,0:T(8,128)}, f32[16,32,128]{2,1,0:T(8,128)S(1)}) custom-call(s32[8,128]{1,0:T(8,128)S(1)} %broadcast_in_dim.4.place, bf16[256,128,128]{2,1,0:T(8,128)(2,1)} %bitcast.22, f32[64,64,128]{2,1,0:T(8,128)S(1)} %collective-permute-done.2.refs_0_, bf16[64,192]{1,0:T(8,128)(2,1)S(1)} %copy-done.6, bf16[1536,512]{1,0:T(8,128)(2,1)S(1)} %copy-done.1), custom_call_target="tpu_custom_call" | custom-call | tf_op jit(solution)/shard_map/pallas_call | solution.py:456
  11.8 2.3 %shard_map.124 = (f32[64,16,128]{2,1,0:T(8,128)S(1)}, f32[64,16,128]{2,1,0:T(8,128)S(1)}, f32[64,16,128]{2,1,0:T(8,128)S(1)}, f32[64,32,128]{2,1,0:T(8,128)S(1)}...) custom-call(s32[8,128]{1,0:T(8,128)S(1)} %broadcast_in_dim.4.place, ...), custom_call_target="tpu_custom_call" | custom-call | tf_op jit(solution)/shard_map/pallas_call | solution.py:456
  14.5 2.0 %collective-permute-start.16 = (f32[4,960,128]{2,1,0:T(8,128)}, f32[4,960,128]{2,1,0:T(8,128)}, u32[]{:S(2)}, u32[]{:S(2)}) collective-permute-start(f32[4,960,128]{2,1,0:T(8,128)} %get-tuple-element.49), channel_id=1, source_target_pairs={{0,2},{1,3},{2,0},{3,1},{4,6},{5,7},{6,4},{7,5},{8,10},{9,11},{10,... | collective-permute-start | bytes 5898248 | tf_op jit(solution)/shard_map/ppermute | solution.py:663
  17.0 1.8 %collective-permute-done.1.early_ref = f32[64,16,128]{2,1,0:T(8,128)S(1)} collective-permute-done((f32[64,16,128]{2,1,0:T(8,128)S(1)}, f32[64,16,128]{2,1,0:T(8,128)S(1)}, u32[]{:S(2)}, u32[]{:S(2)}) %collective-permute-start.1) | collective-permute-done | bytes 524320 | tf_op jit(solution)/shard_map/ppermute | solution.py:663
  19.9 3.4 %shard_map.126 = (f32[2,960,128]{2,1,0:T(8,128)}, f32[16,32,128]{2,1,0:T(8,128)S(1)}) custom-call(s32[8,128]{1,0:T(8,128)S(1)} %broadcast_in_dim.4.place, bf16[256,128,128]{2,1,0:T(8,128)(2,1)} %bitcast.24, f32[64,16,128]{2,1,0:T(8,128)S(1)} %collective-permute-done.7.refs_0_, ...), custom_call_target="tpu_custom_call", output_to_operand_aliasing={{1}: (7, {})} | custom-call | tf_op jit(solution)/shard_map/pallas_call | solution.py:456
  23.2 2.0 %collective-permute-start.14 = (f32[2,960,128]{2,1,0:T(8,128)}, f32[2,960,128]{2,1,0:T(8,128)}, u32[]{:S(2)}, u32[]{:S(2)}) collective-permute-start(f32[2,960,128]{2,1,0:T(8,128)} %get-tuple-element.68), channel_id=1, source_target_pairs={{0,2},{1,3},{2,0},{3,1},{4,6},{5,7},{6,4},{7,5},{8,10},{9,11},{10,... | collective-permute-start | bytes 2949128 | tf_op jit(solution)/shard_map/ppermute | solution.py:663
  25.2 2.5 %collective-permute-start.10 = (f32[16,32,128]{2,1,0:T(8,128)S(1)}, f32[16,32,128]{2,1,0:T(8,128)S(1)}, u32[]{:S(2)}, u32[]{:S(2)}) collective-permute-start(f32[16,32,128]{2,1,0:T(8,128)S(1)} %get-tuple-element.62), channel_id=1, source_target_pairs={{0,66},{1,67},{2,64},{3,65},{4,70},{5,71},{6,68},{7,69},{8,74},{9,... | collective-permute-start | bytes 786440 | tf_op jit(solution)/shard_map/ppermute | solution.py:684
  27.8 5.5 %shard_map.125 = (f32[64,128,128]{2,1,0:T(8,128)}, f32[16,32,128]{2,1,0:T(8,128)S(1)}) custom-call(s32[8,128]{1,0:T(8,128)S(1)} %broadcast_in_dim.4.place, f32[64,128,128]{2,1,0:T(8,128)} %bitcast.28, bf16[256,128,128]{2,1,0:T(8,128)(2,1)} %bitcast.25, f32[64,16,128]{2,1,0:T(8,128)S(1)} %collective-permute-done.1.early_ref, ...), custom_call_target="tpu_custom_call" | custom-call | tf_op jit(solution)/shard_map/pallas_call | solution.py:456
  35.2 7.1 %all-to-all-start = ((f32[16,32,128]{2,1,0:T(8,128)}), f32[16,32,128]{2,1,0:T(8,128)}, u32[]{:S(2)}, u32[]{:S(2)}) async-start(f32[16,32,128]{2,1,0:T(8,128)} %add.14), calls=%async_computation | async-start | bytes 524288 | tf_op jit(solution)/shard_map/all_to_all | solution.py:689
  43.6 5.2 %shard_map.127 = (f32[64,128,128]{2,1,0:T(8,128)}, f32[64,16,128]{2,1,0:T(8,128)S(1)}, f32[480,128]{1,0:T(8,128)S(1)}, f32[48,8,128]{2,1,0:T(8,128)S(1)}, f32[16,8,128]{2,1,0:T(8,128)S(1)}) custom-call(s32[8,128]{1,0:T(8,128)S(1)} %broadcast_in_dim.4.place, f32[64,128,128]{2,1,0:T(8,128)} %get-tuple-element.63.cells_ref, ...), custom_call_target="tpu_custom_call", output_to_operand_aliasing={{0}: (1, {})} | custom-call | tf_op jit(solution)/shard_map/pallas_call | solution.py:456
  51.8 4.3 %collective-permute-start.15 = (f32[32,128]{1,0:T(8,128)S(1)}, f32[32,128]{1,0:T(8,128)S(1)}, u32[]{:S(2)}, u32[]{:S(2)}) collective-permute-start(f32[32,128]{1,0:T(8,128)S(1)} %reduce_sum.9), channel_id=1, source_target_pairs={{0,112},{1,113},{2,114},{3,115},{4,116},{5,117},{6,118},{7,119},{8... | collective-permute-start | bytes 49160 | tf_op jit(solution)/shard_map/ppermute | solution.py:693
  56.1 3.2 %collective-permute-done.15 = f32[32,128]{1,0:T(8,128)S(1)} collective-permute-done((f32[32,128]{1,0:T(8,128)S(1)}, f32[32,128]{1,0:T(8,128)S(1)}, u32[]{:S(2)}, u32[]{:S(2)}) %collective-permute-start.15) | collective-permute-done | bytes 16416 | tf_op jit(solution)/shard_map/ppermute | solution.py:693
  59.3 2.1 %collective-permute-done.16.pay_ref = f32[4,960,128]{2,1,0:T(8,128)} collective-permute-done((f32[4,960,128]{2,1,0:T(8,128)}, f32[4,960,128]{2,1,0:T(8,128)}, u32[]{:S(2)}, u32[]{:S(2)}) %collective-permute-start.16) | collective-permute-done | bytes 1966112 | tf_op jit(solution)/shard_map/ppermute | solution.py:663
  62.1 7.1 %all-to-all-start.1 = ((f32[16,32,128]{2,1,0:T(8,128)}), f32[16,32,128]{2,1,0:T(8,128)S(1)}, u32[]{:S(2)}, u32[]{:S(2)}) async-start(f32[16,32,128]{2,1,0:T(8,128)} %broadcast_in_dim.10), calls=%async_computation.1 | async-start | bytes 524288 | tf_op jit(solution)/shard_map/all_to_all | solution.py:696
  69.3 1.9 %collective-permute-start.13 = (f32[480,128]{1,0:T(8,128)}, f32[480,128]{1,0:T(8,128)S(1)}, u32[]{:S(2)}, u32[]{:S(2)}) collective-permute-start(f32[480,128]{1,0:T(8,128)} %copy-done.9), channel_id=1, source_target_pairs={{0,2},{1,3},{2,0},{3,1},{4,6},{5,7},{6,4},{7,5},{8,10},{9,11},{10,... | collective-permute-start | bytes 737288 | tf_op jit(solution)/shard_map/ppermute | solution.py:663
  71.4 1.8 %collective-permute-start.11 = (f32[16,8,128]{2,1,0:T(8,128)S(1)}, f32[16,8,128]{2,1,0:T(8,128)S(1)}, u32[]{:S(2)}, u32[]{:S(2)}) collective-permute-start(f32[16,8,128]{2,1,0:T(8,128)S(1)} %get-tuple-element.65), channel_id=1, source_target_pairs={{0,2},{1,3},{2,0},{3,1},{4,6},{5,7},{6,4},{7,5},{8,10},{9,11},{10,... | collective-permute-start | bytes 196616 | tf_op jit(solution)/shard_map/ppermute | solution.py:663
  73.2 4.7 %shard_map.128.base_ref = f32[64,128,128]{2,1,0:T(8,128)} custom-call(f32[4,960,128]{2,1,0:T(8,128)} %collective-permute-done.16.pay_ref, bf16[64,192]{1,0:T(8,128)(2,1)S(1)} %copy-done.5, bf16[1152,512]{1,0:T(8,128)(2,1)S(1)} %copy-done, f32[64,128,128]{2,1,0:T(8,128)} %get-tuple-element.71.base_ref), custom_call_target="tpu_custom_call", output_to_operand_aliasing={{}: (3, {})} | custom-call | tf_op jit(solution)/shard_map/pallas_call | solution.py:456
  77.9 3.5 %shard_map.129 = f32[64,128,128]{2,1,0:T(8,128)} custom-call(s32[8,128]{1,0:T(8,128)S(1)} %broadcast_in_dim.4.place, f32[16,32,128]{2,1,0:T(8,128)S(1)} %all-to-all-done.1.band_ref, bf16[64,48]{1,0:T(8,128)(2,1)S(1)} %copy-done.7, bf16[384,512]{1,0:T(8,128)(2,1)S(1)} %copy-done.2), custom_call_target="tpu_custom_call" | custom-call | tf_op jit(solution)/shard_map/pallas_call | solution.py:456
  82.5 3.3 %shard_map.130.base_ref = f32[64,128,128]{2,1,0:T(8,128)} custom-call(f32[2,960,128]{2,1,0:T(8,128)} %collective-permute-done.14.pay_ref, bf16[64,192]{1,0:T(8,128)(2,1)S(1)} %copy-done.5, bf16[1152,512]{1,0:T(8,128)(2,1)S(1)} %copy-done, f32[64,128,128]{2,1,0:T(8,128)} %shard_map.128.base_ref), custom_call_target="tpu_custom_call", output_to_operand_aliasing={{}: (3, {})} | custom-call | tf_op jit(solution)/shard_map/pallas_call | solution.py:456
  85.8 1.9 %collective-permute-done.13.half_ref = f32[480,128]{1,0:T(8,128)S(1)} collective-permute-done((f32[480,128]{1,0:T(8,128)}, f32[480,128]{1,0:T(8,128)S(1)}, u32[]{:S(2)}, u32[]{:S(2)}) %collective-permute-start.13) | collective-permute-done | bytes 245792 | tf_op jit(solution)/shard_map/ppermute | solution.py:663
  88.9 3.0 %collective-permute-done.12.there_ref = f32[48,8,128]{2,1,0:T(8,128)S(1)} collective-permute-done((f32[48,8,128]{2,1,0:T(8,128)}, f32[48,8,128]{2,1,0:T(8,128)S(1)}, u32[]{:S(2)}, u32[]{:S(2)}) %collective-permute-start.12) | collective-permute-done | bytes 196640 | tf_op jit(solution)/shard_map/ppermute | solution.py:663
  (55 shorter events, 14.6 us)
Async XLA Ops:
  1.7 2.0 %collective-permute-start = (f32[64,16,128]{2,1,0:T(8,128)S(1)}, f32[64,16,128]{2,1,0:T(8,128)S(1)}, u32[]{:S(2)}, u32[]{:S(2)}) collective-permute-start(f32[64,16,128]{2,1,0:T(8,128)S(1)} %dynamic-slice_convert_fusion), channel_id=1, source_target_pairs={{0,1},{1,0},{2,3},{3,2},{4,5},{5,4},{6,7},{7,6},{8,9},{9,8},{10,11... | collective-permute-start | bytes 1572872 | tf_op jit(solution)/shard_map/ppermute | solution.py:660
  3.7 4.2 %collective-permute-start.2 = (f32[64,64,128]{2,1,0:T(8,128)S(1)}, f32[64,64,128]{2,1,0:T(8,128)S(1)}, u32[]{:S(2)}, u32[]{:S(2)}) collective-permute-start(f32[64,64,128]{2,1,0:T(8,128)S(1)} %get-tuple-element.48), channel_id=1, source_target_pairs={{0,1},{1,0},{2,3},{3,2},{4,5},{5,4},{6,7},{7,6},{8,9},{9,8},{10,11... | collective-permute-start | bytes 6291464 | tf_op jit(solution)/shard_map/ppermute | solution.py:660
  4.0 14.8 %collective-permute-start.1 = (f32[64,16,128]{2,1,0:T(8,128)S(1)}, f32[64,16,128]{2,1,0:T(8,128)S(1)}, u32[]{:S(2)}, u32[]{:S(2)}) collective-permute-start(f32[64,16,128]{2,1,0:T(8,128)S(1)} %add.13), channel_id=1, source_target_pairs={{0,2},{1,3},{2,0},{3,1},{4,6},{5,7},{6,4},{7,5},{8,10},{9,11},{10,... | collective-permute-start | bytes 1572872 | tf_op jit(solution)/shard_map/ppermute | solution.py:663
  14.1 4.7 %collective-permute-start.7 = (f32[64,16,128]{2,1,0:T(8,128)S(1)}, f32[64,16,128]{2,1,0:T(8,128)S(1)}, u32[]{:S(2)}, u32[]{:S(2)}) collective-permute-start(f32[64,16,128]{2,1,0:T(8,128)S(1)} %get-tuple-element.58), channel_id=1, source_target_pairs={{0,1},{1,0},{2,3},{3,2},{4,5},{5,4},{6,7},{7,6},{8,9},{9,8},{10,11... | collective-permute-start | bytes 1572872 | tf_op jit(solution)/shard_map/ppermute | solution.py:660
  14.5 46.9 %collective-permute-start.16 = (f32[4,960,128]{2,1,0:T(8,128)}, f32[4,960,128]{2,1,0:T(8,128)}, u32[]{:S(2)}, u32[]{:S(2)}) collective-permute-start(f32[4,960,128]{2,1,0:T(8,128)} %get-tuple-element.49), channel_id=1, source_target_pairs={{0,2},{1,3},{2,0},{3,1},{4,6},{5,7},{6,4},{7,5},{8,10},{9,11},{10,... | collective-permute-start | bytes 5898248 | tf_op jit(solution)/shard_map/ppermute | solution.py:663
  16.5 2.8 %collective-permute-start.8 = (f32[64,16,128]{2,1,0:T(8,128)S(1)}, f32[64,16,128]{2,1,0:T(8,128)S(1)}, u32[]{:S(2)}, u32[]{:S(2)}) collective-permute-start(f32[64,16,128]{2,1,0:T(8,128)S(1)} %get-tuple-element.59), channel_id=1, source_target_pairs={{0,1},{1,0},{2,3},{3,2},{4,5},{5,4},{6,7},{7,6},{8,9},{9,8},{10,11... | collective-permute-start | bytes 1572872 | tf_op jit(solution)/shard_map/ppermute | solution.py:660
  16.5 2.9 %collective-permute-start.9 = (f32[64,16,128]{2,1,0:T(8,128)S(1)}, f32[64,16,128]{2,1,0:T(8,128)S(1)}, u32[]{:S(2)}, u32[]{:S(2)}) collective-permute-start(f32[64,16,128]{2,1,0:T(8,128)S(1)} %get-tuple-element.60), channel_id=1, source_target_pairs={{0,1},{1,0},{2,3},{3,2},{4,5},{5,4},{6,7},{7,6},{8,9},{9,8},{10,11... | collective-permute-start | bytes 1572872 | tf_op jit(solution)/shard_map/ppermute | solution.py:660
  18.8 4.4 %collective-permute-start.6 = (f32[64,32,128]{2,1,0:T(8,128)S(1)}, f32[64,32,128]{2,1,0:T(8,128)S(1)}, u32[]{:S(2)}, u32[]{:S(2)}) collective-permute-start(f32[64,32,128]{2,1,0:T(8,128)S(1)} %get-tuple-element.56), channel_id=1, source_target_pairs={{0,1},{1,0},{2,3},{3,2},{4,5},{5,4},{6,7},{7,6},{8,9},{9,8},{10,11... | collective-permute-start | bytes 3145736 | tf_op jit(solution)/shard_map/ppermute | solution.py:660
  18.8 6.4 %collective-permute-start.3 = (f32[64,32,128]{2,1,0:T(8,128)S(1)}, f32[64,32,128]{2,1,0:T(8,128)S(1)}, u32[]{:S(2)}, u32[]{:S(2)}) collective-permute-start(f32[64,32,128]{2,1,0:T(8,128)S(1)} %get-tuple-element.53), channel_id=1, source_target_pairs={{0,1},{1,0},{2,3},{3,2},{4,5},{5,4},{6,7},{7,6},{8,9},{9,8},{10,11... | collective-permute-start | bytes 3145736 | tf_op jit(solution)/shard_map/ppermute | solution.py:660
  19.3 8.4 %collective-permute-start.4 = (f32[64,32,128]{2,1,0:T(8,128)S(1)}, f32[64,32,128]{2,1,0:T(8,128)S(1)}, u32[]{:S(2)}, u32[]{:S(2)}) collective-permute-start(f32[64,32,128]{2,1,0:T(8,128)S(1)} %get-tuple-element.54), channel_id=1, source_target_pairs={{0,1},{1,0},{2,3},{3,2},{4,5},{5,4},{6,7},{7,6},{8,9},{9,8},{10,11... | collective-permute-start | bytes 3145736 | tf_op jit(solution)/shard_map/ppermute | solution.py:660
  19.4 8.3 %collective-permute-start.5 = (f32[64,32,128]{2,1,0:T(8,128)S(1)}, f32[64,32,128]{2,1,0:T(8,128)S(1)}, u32[]{:S(2)}, u32[]{:S(2)}) collective-permute-start(f32[64,32,128]{2,1,0:T(8,128)S(1)} %get-tuple-element.55), channel_id=1, source_target_pairs={{0,1},{1,0},{2,3},{3,2},{4,5},{5,4},{6,7},{7,6},{8,9},{9,8},{10,11... | collective-permute-start | bytes 3145736 | tf_op jit(solution)/shard_map/ppermute | solution.py:660
  19.8 7.9 %copy-start.8 = (bf16[16,192]{1,0:T(8,128)(2,1)S(1)}, bf16[16,192]{1,0:T(8,128)(2,1)}, u32[]{:S(2)}) copy-start(bf16[16,192]{1,0:T(8,128)(2,1)} %constant.34.clone.refs_4_) | copy-start | bytes 18436
  23.2 59.2 %collective-permute-start.14 = (f32[2,960,128]{2,1,0:T(8,128)}, f32[2,960,128]{2,1,0:T(8,128)}, u32[]{:S(2)}, u32[]{:S(2)}) collective-permute-start(f32[2,960,128]{2,1,0:T(8,128)} %get-tuple-element.68), channel_id=1, source_target_pairs={{0,2},{1,3},{2,0},{3,1},{4,6},{5,7},{6,4},{7,5},{8,10},{9,11},{10,... | collective-permute-start | bytes 2949128 | tf_op jit(solution)/shard_map/ppermute | solution.py:663
  25.2 9.2 %collective-permute-start.10 = (f32[16,32,128]{2,1,0:T(8,128)S(1)}, f32[16,32,128]{2,1,0:T(8,128)S(1)}, u32[]{:S(2)}, u32[]{:S(2)}) collective-permute-start(f32[16,32,128]{2,1,0:T(8,128)S(1)} %get-tuple-element.62), channel_id=1, source_target_pairs={{0,66},{1,67},{2,64},{3,65},{4,70},{5,71},{6,68},{7,69},{8,74},{9,... | collective-permute-start | bytes 786440 | tf_op jit(solution)/shard_map/ppermute | solution.py:684
  27.8 14.5 %copy-start.2 = (bf16[384,512]{1,0:T(8,128)(2,1)S(1)}, bf16[384,512]{1,0:T(8,128)(2,1)}, u32[]{:S(2)}) copy-start(bf16[384,512]{1,0:T(8,128)(2,1)} %constant.40.clone.refs_4_.band_back) | copy-start | bytes 1179652
  27.8 14.5 %copy-start.7 = (bf16[64,48]{1,0:T(8,128)(2,1)S(1)}, bf16[64,48]{1,0:T(8,128)(2,1)}, u32[]{:S(2)}) copy-start(bf16[64,48]{1,0:T(8,128)(2,1)} %constant.35.clone.refs_2_.low_back) | copy-start | bytes 18436
  35.2 15.6 %all-to-all-start = ((f32[16,32,128]{2,1,0:T(8,128)}), f32[16,32,128]{2,1,0:T(8,128)}, u32[]{:S(2)}, u32[]{:S(2)}) async-start(f32[16,32,128]{2,1,0:T(8,128)} %add.14), calls=%async_computation | async-start | bytes 524288 | tf_op jit(solution)/shard_map/all_to_all | solution.py:689
  43.6 29.6 %copy-start = (bf16[1152,512]{1,0:T(8,128)(2,1)S(1)}, bf16[1152,512]{1,0:T(8,128)(2,1)}, u32[]{:S(2)}) copy-start(bf16[1152,512]{1,0:T(8,128)(2,1)} %constant.38.clone.kept_back) | copy-start | bytes 3538948
  43.6 29.6 %copy-start.5 = (bf16[64,192]{1,0:T(8,128)(2,1)S(1)}, bf16[64,192]{1,0:T(8,128)(2,1)}, u32[]{:S(2)}) copy-start(bf16[64,192]{1,0:T(8,128)(2,1)} %constant.33.clone.rows_back) | copy-start | bytes 73732
  51.8 7.5 %collective-permute-start.15 = (f32[32,128]{1,0:T(8,128)S(1)}, f32[32,128]{1,0:T(8,128)S(1)}, u32[]{:S(2)}, u32[]{:S(2)}) collective-permute-start(f32[32,128]{1,0:T(8,128)S(1)} %reduce_sum.9), channel_id=1, source_target_pairs={{0,112},{1,113},{2,114},{3,115},{4,116},{5,117},{6,118},{7,119},{8... | collective-permute-start | bytes 49160 | tf_op jit(solution)/shard_map/ppermute | solution.py:693
  62.1 15.8 %all-to-all-start.1 = ((f32[16,32,128]{2,1,0:T(8,128)}), f32[16,32,128]{2,1,0:T(8,128)S(1)}, u32[]{:S(2)}, u32[]{:S(2)}) async-start(f32[16,32,128]{2,1,0:T(8,128)} %broadcast_in_dim.10), calls=%async_computation.1 | async-start | bytes 524288 | tf_op jit(solution)/shard_map/all_to_all | solution.py:696
  69.3 18.4 %collective-permute-start.13 = (f32[480,128]{1,0:T(8,128)}, f32[480,128]{1,0:T(8,128)S(1)}, u32[]{:S(2)}, u32[]{:S(2)}) collective-permute-start(f32[480,128]{1,0:T(8,128)} %copy-done.9), channel_id=1, source_target_pairs={{0,2},{1,3},{2,0},{3,1},{4,6},{5,7},{6,4},{7,5},{8,10},{9,11},{10,... | collective-permute-start | bytes 737288 | tf_op jit(solution)/shard_map/ppermute | solution.py:663
  71.2 20.7 %collective-permute-start.12 = (f32[48,8,128]{2,1,0:T(8,128)}, f32[48,8,128]{2,1,0:T(8,128)S(1)}, u32[]{:S(2)}, u32[]{:S(2)}) collective-permute-start(f32[48,8,128]{2,1,0:T(8,128)} %copy-done.10), channel_id=1, source_target_pairs={{0,2},{1,3},{2,0},{3,1},{4,6},{5,7},{6,4},{7,5},{8,10},{9,11},{10,... | collective-permute-start | bytes 589832 | tf_op jit(solution)/shard_map/ppermute | solution.py:663
  71.4 21.5 %collective-permute-start.11 = (f32[16,8,128]{2,1,0:T(8,128)S(1)}, f32[16,8,128]{2,1,0:T(8,128)S(1)}, u32[]{:S(2)}, u32[]{:S(2)}) collective-permute-start(f32[16,8,128]{2,1,0:T(8,128)S(1)} %get-tuple-element.65), channel_id=1, source_target_pairs={{0,2},{1,3},{2,0},{3,1},{4,6},{5,7},{6,4},{7,5},{8,10},{9,11},{10,... | collective-permute-start | bytes 196616 | tf_op jit(solution)/shard_map/ppermute | solution.py:663
  (6 other events, 22.9 us)

commit v7 on v6

--- a/solution.py
+++ b/solution.py
@@ -690,7 +690,8 @@
     met, bottom = tie(met, bottom)
     half, top, bottom = link(half), link(top), link(bottom)
     part = jnp.sum(met.reshape(PLANE, QUARTER, LANES), axis=0)
-    total = part + lax.ppermute(part, names, steps(rep_count, TURN, 0))
+    relayed = lax.ppermute(part, names, steps(rep_count, 0, 2))
+    total = part + lax.ppermute(relayed, names, steps(rep_count, TURN, 2, plane=0))
     total, second = tie(total, second)
     spread = jnp.broadcast_to(total[None], (PLANE,) + total.shape)
     band_total = lax.all_to_all(spread, "rep", 0, 0, axis_index_groups=groups, tiled=True)
@@ -708,11 +709,12 @@
     return (untiles(out, mat_count)[None], untiles(update, mat_count))
 
 
-def steps(rep_count, turn, member):
+def steps(rep_count, turn, member, plane=1):
     pairs = []
     for rep in range(rep_count):
         high, low = divmod(rep, PLANE)
-        to = (high ^ 1) * PLANE + (low + (turn if high else PLANE - turn)) % PLANE
+        on = high == plane
+        to = (high ^ plane) * PLANE + (low + (turn if on else PLANE - turn)) % PLANE
         pairs += [(rep * 4 + f, to * 4 + (f ^ member)) for f in range(4)]
     return pairs
 

time: 94.7 us -> 94.7 us (level)
  starting transfers between devices: 33.3 us -> 30.2 us
  waiting for transfers between devices: 17 us -> 20 us
    ppermute x1 -> x2, waiting for transfers between devices: 3.19 us -> 8.31 us  [the longest x1 5.88 us: per_device(): lax.ppermute(relayed, names, steps(rep_count, TURN, 2, plane=0))]
    ppermute x6, waiting for transfers between devices: 10 us -> 7.96 us  [link(): return lax.ppermute(x, 'fsdp', over_z)]
    ppermute x1 -> x2, starting transfers between devices: 4.35 us -> 2.68 us  [the longest x1 2.61 us: per_device(): relayed = lax.ppermute(part, names, steps(rep_count, 0, 2))]
    all_to_all x1, starting transfers between devices: 7.13 us -> 5.72 us  [per_device(): lax.all_to_all(spread, 'rep', 0, 0, axis_index_groups=groups, tiled=True)]
  transfers between devices with their start and end apart: 19 -> 20, of which waited for: 11 -> 11; matrix products, arithmetic and copies ran while one was open for 3% -> 3% of each run, Pallas kernels for 38% -> 38%
where the time goes in v7:
time: 94.7 us; the launch traced here: 93.5 us
  Pallas kernels  36.2 us (38%)
  starting transfers between devices  30.2 us (32%)
  waiting for transfers between devices  20 us (21%)
  local copies, waits for them, and re-layouts  3.41 us (4%)
  other arithmetic  2.8 us (3%)
    pallas_call x12, Pallas kernels, call(): pl.pallas_call(kernel, grid_spec=pltpu.PrefetchScalarGridSpec(num_scalar_...  36.2 us
    ppermute x6, starting transfers between devices, link(): return lax.ppermute(x, 'fsdp', over_z)  9.97 us
    ppermute x6, waiting for transfers between devices, link(): return lax.ppermute(x, 'fsdp', over_z)  7.96 us
    all_to_all x1, starting transfers between devices, per_device(): lax.all_to_all(own_band + wrapped, 'rep', 0, 0, axis_index_groups=groups,...  7.08 us
    ppermute x1, waiting for transfers between devices, per_device(): lax.ppermute(relayed, names, steps(rep_count, TURN, 2, plane=0))  5.88 us
    all_to_all x1, starting transfers between devices, per_device(): lax.all_to_all(spread, 'rep', 0, 0, axis_index_groups=groups, tiled=True)  5.72 us
    unnamed x22, local copies, waits for them, and re-layouts  2.68 us
    ppermute x1, starting transfers between devices, per_device(): relayed = lax.ppermute(part, names, steps(rep_count, 0, 2))  2.61 us
  transfers between devices with their start and end apart: 20, of which 11 were waited for; matrix products, arithmetic and copies ran while one was open for 3% of the time, Pallas kernels for 38%

profile of v7, /device:TPU:0, one launch (start us, length us, event | category | flops | bytes accessed | tf_op | source)
XLA Modules:
  0.0 93.5 jit_solution(12194157597238476646)
XLA Ops:
  1.8 1.7 %shard_map.122 = (f32[64,64,128]{2,1,0:T(8,128)S(1)}, f32[64,16,128]{2,1,0:T(8,128)S(1)}) custom-call(s32[8,128]{1,0:T(8,128)S(1)} %broadcast_in_dim.4.place, bf16[256,128,128]{2,1,0:T(8,128)(2,1)} %bitcast.21), custom_call_target="tpu_custom_call" | custom-call | tf_op jit(solution)/shard_map/pallas_call | solution.py:456
  4.0 2.1 %collective-permute-start.1 = (f32[64,16,128]{2,1,0:T(8,128)S(1)}, f32[64,16,128]{2,1,0:T(8,128)S(1)}, u32[]{:S(2)}, u32[]{:S(2)}) collective-permute-start(f32[64,16,128]{2,1,0:T(8,128)S(1)} %add.13), channel_id=1, source_target_pairs={{0,2},{1,3},{2,0},{3,1},{4,6},{5,7},{6,4},{7,5},{8,10},{9,11},{10,... | collective-permute-start | bytes 1572872 | tf_op jit(solution)/shard_map/ppermute | solution.py:663
  6.1 1.7 %collective-permute-done.2.refs_0_ = f32[64,64,128]{2,1,0:T(8,128)S(1)} collective-permute-done((f32[64,64,128]{2,1,0:T(8,128)S(1)}, f32[64,64,128]{2,1,0:T(8,128)S(1)}, u32[]{:S(2)}, u32[]{:S(2)}) %collective-permute-start.2) | collective-permute-done | bytes 2097184 | tf_op jit(solution)/shard_map/ppermute | solution.py:660
  7.8 4.0 %shard_map.123 = (f32[4,960,128]{2,1,0:T(8,128)}, f32[16,32,128]{2,1,0:T(8,128)S(1)}) custom-call(s32[8,128]{1,0:T(8,128)S(1)} %broadcast_in_dim.4.place, bf16[256,128,128]{2,1,0:T(8,128)(2,1)} %bitcast.22, f32[64,64,128]{2,1,0:T(8,128)S(1)} %collective-permute-done.2.refs_0_, bf16[64,192]{1,0:T(8,128)(2,1)S(1)} %copy-done.6, bf16[1536,512]{1,0:T(8,128)(2,1)S(1)} %copy-done.1), custom_call_target="tpu_custom_call" | custom-call | tf_op jit(solution)/shard_map/pallas_call | solution.py:456
  11.8 2.3 %shard_map.124 = (f32[64,16,128]{2,1,0:T(8,128)S(1)}, f32[64,16,128]{2,1,0:T(8,128)S(1)}, f32[64,16,128]{2,1,0:T(8,128)S(1)}, f32[64,32,128]{2,1,0:T(8,128)S(1)}...) custom-call(s32[8,128]{1,0:T(8,128)S(1)} %broadcast_in_dim.4.place, ...), custom_call_target="tpu_custom_call" | custom-call | tf_op jit(solution)/shard_map/pallas_call | solution.py:456
  14.5 2.0 %collective-permute-start.17 = (f32[4,960,128]{2,1,0:T(8,128)}, f32[4,960,128]{2,1,0:T(8,128)}, u32[]{:S(2)}, u32[]{:S(2)}) collective-permute-start(f32[4,960,128]{2,1,0:T(8,128)} %get-tuple-element.49), channel_id=1, source_target_pairs={{0,2},{1,3},{2,0},{3,1},{4,6},{5,7},{6,4},{7,5},{8,10},{9,11},{10,... | collective-permute-start | bytes 5898248 | tf_op jit(solution)/shard_map/ppermute | solution.py:663
  17.0 1.8 %collective-permute-done.1.early_ref = f32[64,16,128]{2,1,0:T(8,128)S(1)} collective-permute-done((f32[64,16,128]{2,1,0:T(8,128)S(1)}, f32[64,16,128]{2,1,0:T(8,128)S(1)}, u32[]{:S(2)}, u32[]{:S(2)}) %collective-permute-start.1) | collective-permute-done | bytes 524320 | tf_op jit(solution)/shard_map/ppermute | solution.py:663
  19.9 3.4 %shard_map.126 = (f32[2,960,128]{2,1,0:T(8,128)}, f32[16,32,128]{2,1,0:T(8,128)S(1)}) custom-call(s32[8,128]{1,0:T(8,128)S(1)} %broadcast_in_dim.4.place, bf16[256,128,128]{2,1,0:T(8,128)(2,1)} %bitcast.24, f32[64,16,128]{2,1,0:T(8,128)S(1)} %collective-permute-done.7.refs_0_, ...), custom_call_target="tpu_custom_call", output_to_operand_aliasing={{1}: (7, {})} | custom-call | tf_op jit(solution)/shard_map/pallas_call | solution.py:456
  23.3 2.0 %collective-permute-start.14 = (f32[2,960,128]{2,1,0:T(8,128)}, f32[2,960,128]{2,1,0:T(8,128)}, u32[]{:S(2)}, u32[]{:S(2)}) collective-permute-start(f32[2,960,128]{2,1,0:T(8,128)} %get-tuple-element.68), channel_id=1, source_target_pairs={{0,2},{1,3},{2,0},{3,1},{4,6},{5,7},{6,4},{7,5},{8,10},{9,11},{10,... | collective-permute-start | bytes 2949128 | tf_op jit(solution)/shard_map/ppermute | solution.py:663
  25.2 2.5 %collective-permute-start.10 = (f32[16,32,128]{2,1,0:T(8,128)S(1)}, f32[16,32,128]{2,1,0:T(8,128)S(1)}, u32[]{:S(2)}, u32[]{:S(2)}) collective-permute-start(f32[16,32,128]{2,1,0:T(8,128)S(1)} %get-tuple-element.62), channel_id=1, source_target_pairs={{0,66},{1,67},{2,64},{3,65},{4,70},{5,71},{6,68},{7,69},{8,74},{9,... | collective-permute-start | bytes 786440 | tf_op jit(solution)/shard_map/ppermute | solution.py:684
  27.8 5.5 %shard_map.125 = (f32[64,128,128]{2,1,0:T(8,128)}, f32[16,32,128]{2,1,0:T(8,128)S(1)}) custom-call(s32[8,128]{1,0:T(8,128)S(1)} %broadcast_in_dim.4.place, f32[64,128,128]{2,1,0:T(8,128)} %bitcast.28, bf16[256,128,128]{2,1,0:T(8,128)(2,1)} %bitcast.25, f32[64,16,128]{2,1,0:T(8,128)S(1)} %collective-permute-done.1.early_ref, ...), custom_call_target="tpu_custom_call" | custom-call | tf_op jit(solution)/shard_map/pallas_call | solution.py:456
  35.2 7.1 %all-to-all-start = ((f32[16,32,128]{2,1,0:T(8,128)}), f32[16,32,128]{2,1,0:T(8,128)}, u32[]{:S(2)}, u32[]{:S(2)}) async-start(f32[16,32,128]{2,1,0:T(8,128)} %add.14), calls=%async_computation | async-start | bytes 524288 | tf_op jit(solution)/shard_map/all_to_all | solution.py:689
  43.6 5.2 %shard_map.127 = (f32[64,128,128]{2,1,0:T(8,128)}, f32[64,16,128]{2,1,0:T(8,128)S(1)}, f32[480,128]{1,0:T(8,128)S(1)}, f32[48,8,128]{2,1,0:T(8,128)S(1)}, f32[16,8,128]{2,1,0:T(8,128)S(1)}) custom-call(s32[8,128]{1,0:T(8,128)S(1)} %broadcast_in_dim.4.place, f32[64,128,128]{2,1,0:T(8,128)} %get-tuple-element.63.cells_ref, ...), custom_call_target="tpu_custom_call", output_to_operand_aliasing={{0}: (1, {})} | custom-call | tf_op jit(solution)/shard_map/pallas_call | solution.py:456
  51.8 2.6 %collective-permute-start.15 = (f32[32,128]{1,0:T(8,128)S(1)}, f32[32,128]{1,0:T(8,128)S(1)}, u32[]{:S(2)}, u32[]{:S(2)}) collective-permute-start(f32[32,128]{1,0:T(8,128)S(1)} %reduce_sum.9), channel_id=1, source_target_pairs={{0,66},{1,67},{2,64},{3,65},{4,70},{5,71},{6,68},{7,69},{8,74},{9,... | collective-permute-start | bytes 49160 | tf_op jit(solution)/shard_map/ppermute | solution.py:693
  54.4 2.4 %collective-permute-done.15 = f32[32,128]{1,0:T(8,128)S(1)} collective-permute-done((f32[32,128]{1,0:T(8,128)S(1)}, f32[32,128]{1,0:T(8,128)S(1)}, u32[]{:S(2)}, u32[]{:S(2)}) %collective-permute-start.15) | collective-permute-done | bytes 16416 | tf_op jit(solution)/shard_map/ppermute | solution.py:693
  56.9 5.9 %collective-permute-done.16 = f32[32,128]{1,0:T(8,128)S(1)} collective-permute-done((f32[32,128]{1,0:T(8,128)S(1)}, f32[32,128]{1,0:T(8,128)S(1)}, u32[]{:S(2)}, u32[]{:S(2)}) %collective-permute-start.16) | collective-permute-done | bytes 16416 | tf_op jit(solution)/shard_map/ppermute | solution.py:694
  63.5 5.7 %all-to-all-start.1 = ((f32[16,32,128]{2,1,0:T(8,128)}), f32[16,32,128]{2,1,0:T(8,128)S(1)}, u32[]{:S(2)}, u32[]{:S(2)}) async-start(f32[16,32,128]{2,1,0:T(8,128)} %broadcast_in_dim.10), calls=%async_computation.1 | async-start | bytes 524288 | tf_op jit(solution)/shard_map/all_to_all | solution.py:697
  69.3 1.9 %collective-permute-start.13 = (f32[480,128]{1,0:T(8,128)}, f32[480,128]{1,0:T(8,128)S(1)}, u32[]{:S(2)}, u32[]{:S(2)}) collective-permute-start(f32[480,128]{1,0:T(8,128)} %copy-done.9), channel_id=1, source_target_pairs={{0,2},{1,3},{2,0},{3,1},{4,6},{5,7},{6,4},{7,5},{8,10},{9,11},{10,... | collective-permute-start | bytes 737288 | tf_op jit(solution)/shard_map/ppermute | solution.py:663
  71.4 1.8 %collective-permute-start.11 = (f32[16,8,128]{2,1,0:T(8,128)S(1)}, f32[16,8,128]{2,1,0:T(8,128)S(1)}, u32[]{:S(2)}, u32[]{:S(2)}) collective-permute-start(f32[16,8,128]{2,1,0:T(8,128)S(1)} %get-tuple-element.65), channel_id=1, source_target_pairs={{0,2},{1,3},{2,0},{3,1},{4,6},{5,7},{6,4},{7,5},{8,10},{9,11},{10,... | collective-permute-start | bytes 196616 | tf_op jit(solution)/shard_map/ppermute | solution.py:663
  73.2 4.7 %shard_map.128.base_ref = f32[64,128,128]{2,1,0:T(8,128)} custom-call(f32[4,960,128]{2,1,0:T(8,128)} %collective-permute-done.17.pay_ref, bf16[64,192]{1,0:T(8,128)(2,1)S(1)} %copy-done.5, bf16[1152,512]{1,0:T(8,128)(2,1)S(1)} %copy-done, f32[64,128,128]{2,1,0:T(8,128)} %get-tuple-element.71.base_ref), custom_call_target="tpu_custom_call", output_to_operand_aliasing={{}: (3, {})} | custom-call | tf_op jit(solution)/shard_map/pallas_call | solution.py:456
  77.9 3.5 %shard_map.129 = f32[64,128,128]{2,1,0:T(8,128)} custom-call(s32[8,128]{1,0:T(8,128)S(1)} %broadcast_in_dim.4.place, f32[16,32,128]{2,1,0:T(8,128)S(1)} %all-to-all-done.1.band_ref, bf16[64,48]{1,0:T(8,128)(2,1)S(1)} %copy-done.7, bf16[384,512]{1,0:T(8,128)(2,1)S(1)} %copy-done.2), custom_call_target="tpu_custom_call" | custom-call | tf_op jit(solution)/shard_map/pallas_call | solution.py:456
  82.5 3.3 %shard_map.130.base_ref = f32[64,128,128]{2,1,0:T(8,128)} custom-call(f32[2,960,128]{2,1,0:T(8,128)} %collective-permute-done.14.pay_ref, bf16[64,192]{1,0:T(8,128)(2,1)S(1)} %copy-done.5, bf16[1152,512]{1,0:T(8,128)(2,1)S(1)} %copy-done, f32[64,128,128]{2,1,0:T(8,128)} %shard_map.128.base_ref), custom_call_target="tpu_custom_call", output_to_operand_aliasing={{}: (3, {})} | custom-call | tf_op jit(solution)/shard_map/pallas_call | solution.py:456
  85.8 1.9 %collective-permute-done.13.half_ref = f32[480,128]{1,0:T(8,128)S(1)} collective-permute-done((f32[480,128]{1,0:T(8,128)}, f32[480,128]{1,0:T(8,128)S(1)}, u32[]{:S(2)}, u32[]{:S(2)}) %collective-permute-start.13) | collective-permute-done | bytes 245792 | tf_op jit(solution)/shard_map/ppermute | solution.py:663
  88.9 3.0 %collective-permute-done.12.there_ref = f32[48,8,128]{2,1,0:T(8,128)S(1)} collective-permute-done((f32[48,8,128]{2,1,0:T(8,128)}, f32[48,8,128]{2,1,0:T(8,128)S(1)}, u32[]{:S(2)}, u32[]{:S(2)}) %collective-permute-start.12) | collective-permute-done | bytes 196640 | tf_op jit(solution)/shard_map/ppermute | solution.py:663
  (57 shorter events, 14.7 us)
Async XLA Ops:
  1.7 2.0 %collective-permute-start = (f32[64,16,128]{2,1,0:T(8,128)S(1)}, f32[64,16,128]{2,1,0:T(8,128)S(1)}, u32[]{:S(2)}, u32[]{:S(2)}) collective-permute-start(f32[64,16,128]{2,1,0:T(8,128)S(1)} %dynamic-slice_convert_fusion), channel_id=1, source_target_pairs={{0,1},{1,0},{2,3},{3,2},{4,5},{5,4},{6,7},{7,6},{8,9},{9,8},{10,11... | collective-permute-start | bytes 1572872 | tf_op jit(solution)/shard_map/ppermute | solution.py:660
  3.7 4.2 %collective-permute-start.2 = (f32[64,64,128]{2,1,0:T(8,128)S(1)}, f32[64,64,128]{2,1,0:T(8,128)S(1)}, u32[]{:S(2)}, u32[]{:S(2)}) collective-permute-start(f32[64,64,128]{2,1,0:T(8,128)S(1)} %get-tuple-element.48), channel_id=1, source_target_pairs={{0,1},{1,0},{2,3},{3,2},{4,5},{5,4},{6,7},{7,6},{8,9},{9,8},{10,11... | collective-permute-start | bytes 6291464 | tf_op jit(solution)/shard_map/ppermute | solution.py:660
  4.0 14.8 %collective-permute-start.1 = (f32[64,16,128]{2,1,0:T(8,128)S(1)}, f32[64,16,128]{2,1,0:T(8,128)S(1)}, u32[]{:S(2)}, u32[]{:S(2)}) collective-permute-start(f32[64,16,128]{2,1,0:T(8,128)S(1)} %add.13), channel_id=1, source_target_pairs={{0,2},{1,3},{2,0},{3,1},{4,6},{5,7},{6,4},{7,5},{8,10},{9,11},{10,... | collective-permute-start | bytes 1572872 | tf_op jit(solution)/shard_map/ppermute | solution.py:663
  14.1 4.7 %collective-permute-start.7 = (f32[64,16,128]{2,1,0:T(8,128)S(1)}, f32[64,16,128]{2,1,0:T(8,128)S(1)}, u32[]{:S(2)}, u32[]{:S(2)}) collective-permute-start(f32[64,16,128]{2,1,0:T(8,128)S(1)} %get-tuple-element.58), channel_id=1, source_target_pairs={{0,1},{1,0},{2,3},{3,2},{4,5},{5,4},{6,7},{7,6},{8,9},{9,8},{10,11... | collective-permute-start | bytes 1572872 | tf_op jit(solution)/shard_map/ppermute | solution.py:660
  14.5 48.3 %collective-permute-start.17 = (f32[4,960,128]{2,1,0:T(8,128)}, f32[4,960,128]{2,1,0:T(8,128)}, u32[]{:S(2)}, u32[]{:S(2)}) collective-permute-start(f32[4,960,128]{2,1,0:T(8,128)} %get-tuple-element.49), channel_id=1, source_target_pairs={{0,2},{1,3},{2,0},{3,1},{4,6},{5,7},{6,4},{7,5},{8,10},{9,11},{10,... | collective-permute-start | bytes 5898248 | tf_op jit(solution)/shard_map/ppermute | solution.py:663
  16.5 2.8 %collective-permute-start.8 = (f32[64,16,128]{2,1,0:T(8,128)S(1)}, f32[64,16,128]{2,1,0:T(8,128)S(1)}, u32[]{:S(2)}, u32[]{:S(2)}) collective-permute-start(f32[64,16,128]{2,1,0:T(8,128)S(1)} %get-tuple-element.59), channel_id=1, source_target_pairs={{0,1},{1,0},{2,3},{3,2},{4,5},{5,4},{6,7},{7,6},{8,9},{9,8},{10,11... | collective-permute-start | bytes 1572872 | tf_op jit(solution)/shard_map/ppermute | solution.py:660
  16.5 2.9 %collective-permute-start.9 = (f32[64,16,128]{2,1,0:T(8,128)S(1)}, f32[64,16,128]{2,1,0:T(8,128)S(1)}, u32[]{:S(2)}, u32[]{:S(2)}) collective-permute-start(f32[64,16,128]{2,1,0:T(8,128)S(1)} %get-tuple-element.60), channel_id=1, source_target_pairs={{0,1},{1,0},{2,3},{3,2},{4,5},{5,4},{6,7},{7,6},{8,9},{9,8},{10,11... | collective-permute-start | bytes 1572872 | tf_op jit(solution)/shard_map/ppermute | solution.py:660
  18.8 4.4 %collective-permute-start.6 = (f32[64,32,128]{2,1,0:T(8,128)S(1)}, f32[64,32,128]{2,1,0:T(8,128)S(1)}, u32[]{:S(2)}, u32[]{:S(2)}) collective-permute-start(f32[64,32,128]{2,1,0:T(8,128)S(1)} %get-tuple-element.56), channel_id=1, source_target_pairs={{0,1},{1,0},{2,3},{3,2},{4,5},{5,4},{6,7},{7,6},{8,9},{9,8},{10,11... | collective-permute-start | bytes 3145736 | tf_op jit(solution)/shard_map/ppermute | solution.py:660
  18.8 6.4 %collective-permute-start.3 = (f32[64,32,128]{2,1,0:T(8,128)S(1)}, f32[64,32,128]{2,1,0:T(8,128)S(1)}, u32[]{:S(2)}, u32[]{:S(2)}) collective-permute-start(f32[64,32,128]{2,1,0:T(8,128)S(1)} %get-tuple-element.53), channel_id=1, source_target_pairs={{0,1},{1,0},{2,3},{3,2},{4,5},{5,4},{6,7},{7,6},{8,9},{9,8},{10,11... | collective-permute-start | bytes 3145736 | tf_op jit(solution)/shard_map/ppermute | solution.py:660
  19.3 8.4 %collective-permute-start.4 = (f32[64,32,128]{2,1,0:T(8,128)S(1)}, f32[64,32,128]{2,1,0:T(8,128)S(1)}, u32[]{:S(2)}, u32[]{:S(2)}) collective-permute-start(f32[64,32,128]{2,1,0:T(8,128)S(1)} %get-tuple-element.54), channel_id=1, source_target_pairs={{0,1},{1,0},{2,3},{3,2},{4,5},{5,4},{6,7},{7,6},{8,9},{9,8},{10,11... | collective-permute-start | bytes 3145736 | tf_op jit(solution)/shard_map/ppermute | solution.py:660
  19.4 8.3 %collective-permute-start.5 = (f32[64,32,128]{2,1,0:T(8,128)S(1)}, f32[64,32,128]{2,1,0:T(8,128)S(1)}, u32[]{:S(2)}, u32[]{:S(2)}) collective-permute-start(f32[64,32,128]{2,1,0:T(8,128)S(1)} %get-tuple-element.55), channel_id=1, source_target_pairs={{0,1},{1,0},{2,3},{3,2},{4,5},{5,4},{6,7},{7,6},{8,9},{9,8},{10,11... | collective-permute-start | bytes 3145736 | tf_op jit(solution)/shard_map/ppermute | solution.py:660
  23.3 59.2 %collective-permute-start.14 = (f32[2,960,128]{2,1,0:T(8,128)}, f32[2,960,128]{2,1,0:T(8,128)}, u32[]{:S(2)}, u32[]{:S(2)}) collective-permute-start(f32[2,960,128]{2,1,0:T(8,128)} %get-tuple-element.68), channel_id=1, source_target_pairs={{0,2},{1,3},{2,0},{3,1},{4,6},{5,7},{6,4},{7,5},{8,10},{9,11},{10,... | collective-permute-start | bytes 2949128 | tf_op jit(solution)/shard_map/ppermute | solution.py:663
  25.2 9.2 %collective-permute-start.10 = (f32[16,32,128]{2,1,0:T(8,128)S(1)}, f32[16,32,128]{2,1,0:T(8,128)S(1)}, u32[]{:S(2)}, u32[]{:S(2)}) collective-permute-start(f32[16,32,128]{2,1,0:T(8,128)S(1)} %get-tuple-element.62), channel_id=1, source_target_pairs={{0,66},{1,67},{2,64},{3,65},{4,70},{5,71},{6,68},{7,69},{8,74},{9,... | collective-permute-start | bytes 786440 | tf_op jit(solution)/shard_map/ppermute | solution.py:684
  27.8 14.5 %copy-start.2 = (bf16[384,512]{1,0:T(8,128)(2,1)S(1)}, bf16[384,512]{1,0:T(8,128)(2,1)}, u32[]{:S(2)}) copy-start(bf16[384,512]{1,0:T(8,128)(2,1)} %constant.40.clone.refs_4_.band_back) | copy-start | bytes 1179652
  27.8 14.5 %copy-start.7 = (bf16[64,48]{1,0:T(8,128)(2,1)S(1)}, bf16[64,48]{1,0:T(8,128)(2,1)}, u32[]{:S(2)}) copy-start(bf16[64,48]{1,0:T(8,128)(2,1)} %constant.35.clone.refs_2_.low_back) | copy-start | bytes 18436
  35.2 15.6 %all-to-all-start = ((f32[16,32,128]{2,1,0:T(8,128)}), f32[16,32,128]{2,1,0:T(8,128)}, u32[]{:S(2)}, u32[]{:S(2)}) async-start(f32[16,32,128]{2,1,0:T(8,128)} %add.14), calls=%async_computation | async-start | bytes 524288 | tf_op jit(solution)/shard_map/all_to_all | solution.py:689
  43.6 29.6 %copy-start = (bf16[1152,512]{1,0:T(8,128)(2,1)S(1)}, bf16[1152,512]{1,0:T(8,128)(2,1)}, u32[]{:S(2)}) copy-start(bf16[1152,512]{1,0:T(8,128)(2,1)} %constant.38.clone.kept_back) | copy-start | bytes 3538948
  43.6 29.6 %copy-start.5 = (bf16[64,192]{1,0:T(8,128)(2,1)S(1)}, bf16[64,192]{1,0:T(8,128)(2,1)}, u32[]{:S(2)}) copy-start(bf16[64,192]{1,0:T(8,128)(2,1)} %constant.33.clone.rows_back) | copy-start | bytes 73732
  51.8 5.0 %collective-permute-start.15 = (f32[32,128]{1,0:T(8,128)S(1)}, f32[32,128]{1,0:T(8,128)S(1)}, u32[]{:S(2)}, u32[]{:S(2)}) collective-permute-start(f32[32,128]{1,0:T(8,128)S(1)} %reduce_sum.9), channel_id=1, source_target_pairs={{0,66},{1,67},{2,64},{3,65},{4,70},{5,71},{6,68},{7,69},{8,74},{9,... | collective-permute-start | bytes 49160 | tf_op jit(solution)/shard_map/ppermute | solution.py:693
  56.8 6.0 %collective-permute-start.16 = (f32[32,128]{1,0:T(8,128)S(1)}, f32[32,128]{1,0:T(8,128)S(1)}, u32[]{:S(2)}, u32[]{:S(2)}) collective-permute-start(f32[32,128]{1,0:T(8,128)S(1)} %collective-permute-done.15), channel_id=1, source_target_pairs={{0,18},{1,19},{2,16},{3,17},{4,22},{5,23},{6,20},{7,21},{8,26},{9,... | collective-permute-start | bytes 49160 | tf_op jit(solution)/shard_map/ppermute | solution.py:694
  63.5 14.4 %all-to-all-start.1 = ((f32[16,32,128]{2,1,0:T(8,128)}), f32[16,32,128]{2,1,0:T(8,128)S(1)}, u32[]{:S(2)}, u32[]{:S(2)}) async-start(f32[16,32,128]{2,1,0:T(8,128)} %broadcast_in_dim.10), calls=%async_computation.1 | async-start | bytes 524288 | tf_op jit(solution)/shard_map/all_to_all | solution.py:697
  69.3 18.4 %collective-permute-start.13 = (f32[480,128]{1,0:T(8,128)}, f32[480,128]{1,0:T(8,128)S(1)}, u32[]{:S(2)}, u32[]{:S(2)}) collective-permute-start(f32[480,128]{1,0:T(8,128)} %copy-done.9), channel_id=1, source_target_pairs={{0,2},{1,3},{2,0},{3,1},{4,6},{5,7},{6,4},{7,5},{8,10},{9,11},{10,... | collective-permute-start | bytes 737288 | tf_op jit(solution)/shard_map/ppermute | solution.py:663
  71.2 20.7 %collective-permute-start.12 = (f32[48,8,128]{2,1,0:T(8,128)}, f32[48,8,128]{2,1,0:T(8,128)S(1)}, u32[]{:S(2)}, u32[]{:S(2)}) collective-permute-start(f32[48,8,128]{2,1,0:T(8,128)} %copy-done.10), channel_id=1, source_target_pairs={{0,2},{1,3},{2,0},{3,1},{4,6},{5,7},{6,4},{7,5},{8,10},{9,11},{10,... | collective-permute-start | bytes 589832 | tf_op jit(solution)/shard_map/ppermute | solution.py:663
  71.4 21.5 %collective-permute-start.11 = (f32[16,8,128]{2,1,0:T(8,128)S(1)}, f32[16,8,128]{2,1,0:T(8,128)S(1)}, u32[]{:S(2)}, u32[]{:S(2)}) collective-permute-start(f32[16,8,128]{2,1,0:T(8,128)S(1)} %get-tuple-element.65), channel_id=1, source_target_pairs={{0,2},{1,3},{2,0},{3,1},{4,6},{5,7},{6,4},{7,5},{8,10},{9,11},{10,... | collective-permute-start | bytes 196616 | tf_op jit(solution)/shard_map/ppermute | solution.py:663
  (7 other events, 30.8 us)

commit v8 on v6

--- a/solution.py
+++ b/solution.py
@@ -129,21 +129,15 @@
 
 
 def cast_kernel(wanted, place, g_ref, *refs):
-    outs, (held, cells, sems) = refs[: len(wanted)], refs[len(wanted) :]
-    into, out = [], []
-    for o, (slot, first, n) in zip(outs, wanted):
-        for j in range(n):
-            k = len(into)
-            source = g_ref.at[rows_of(slot), quantum(first + j), :]
-            into.append(pltpu.make_async_copy(source, held.at[k], sems.at[0, k]))
-            out.append(pltpu.make_async_copy(cells.at[k], o.at[:, quantum(j), :], sems.at[1, k]))
-            into[-1].start()
-    for k in range(len(into)):
+    outs, (held, sems) = refs[: len(wanted)], refs[len(wanted) :]
+    where = [(o, j, slot, first + j) for o, (slot, first, n) in zip(outs, wanted) for j in range(n)]
+    into = []
+    for k, (_, _, slot, at) in enumerate(where):
+        into.append(pltpu.make_async_copy(g_ref.at[rows_of(slot), quantum(at), :], held.at[k], sems.at[k]))
+        into[-1].start()
+    for k, (o, j, _, _) in enumerate(where):
         into[k].wait()
-        cells[k] = held[k].astype(jnp.float32)
-        out[k].start()
-    for copy in out:
-        copy.wait()
+        o[:, j * QUANTUM : (j + 1) * QUANTUM, :] = held[k].astype(jnp.float32)
 
 
 def encode_kernel(first, counts, extra, slot, received, place, g_ref, *refs):
@@ -451,7 +445,7 @@
 BANDS = jax.ShapeDtypeStruct((PLANE, QUARTER, LANES), jnp.float32)
 
 
-def call(kernel, place, operands, outs, scratch, aliases, vmem, near=0):
+def call(kernel, place, operands, outs, scratch, aliases, vmem, near=0, out_spec=ANY):
     operands = operands if place is None else [place, *operands]
     return pl.pallas_call(
         kernel,
@@ -459,7 +453,7 @@
             num_scalar_prefetch=0,
             grid=(),
             in_specs=[pl.BlockSpec(memory_space=pltpu.VMEM)] * near + [ANY] * (len(operands) - near),
-            out_specs=[ANY] * len(outs),
+            out_specs=[out_spec] * len(outs),
             scratch_shapes=scratch,
         ),
         out_shape=outs,
@@ -496,9 +490,10 @@
         place,
         [g],
         [floats(SPAN, count * QUANTUM, LANES) for _, _, count in wanted],
-        held(n, jnp.bfloat16, jnp.float32) + [sems(2, n)],
+        held(n, jnp.bfloat16) + [sems(n)],
         {},
         MOST,
+        out_spec=pl.BlockSpec(memory_space=pltpu.VMEM),
     )
 
 

time: 94.7 us -> 94.8 us (level)
  transfers between devices with their start and end apart: 19 -> 19, of which waited for: 11 -> 11; matrix products, arithmetic and copies ran while one was open for 3% -> 3% of each run, Pallas kernels for 38% -> 37%
where the time goes in v8:
time: 94.8 us; the launch traced here: 93.5 us
  Pallas kernels  35.5 us (37%)
  starting transfers between devices  33.3 us (35%)
  waiting for transfers between devices  17.6 us (19%)
  local copies, waits for them, and re-layouts  3.4 us (4%)
  other arithmetic  2.79 us (3%)
    pallas_call x12, Pallas kernels, call(): pl.pallas_call(kernel, grid_spec=pltpu.PrefetchScalarGridSpec(num_scalar_...  35.5 us
    ppermute x6, waiting for transfers between devices, link(): return lax.ppermute(x, 'fsdp', over_z)  10.3 us
    ppermute x6, starting transfers between devices, link(): return lax.ppermute(x, 'fsdp', over_z)  10.3 us
    all_to_all x1, starting transfers between devices, per_device(): lax.all_to_all(spread, 'rep', 0, 0, axis_index_groups=groups, tiled=True)  7.13 us
    all_to_all x1, starting transfers between devices, per_device(): lax.all_to_all(own_band + wrapped, 'rep', 0, 0, axis_index_groups=groups,...  7.08 us
    ppermute x1, starting transfers between devices, per_device(): total = part + lax.ppermute(part, names, steps(rep_count, TURN, 0))  4.35 us
    ppermute x1, waiting for transfers between devices, per_device(): total = part + lax.ppermute(part, names, steps(rep_count, TURN, 0))  3.19 us
    unnamed x22, local copies, waits for them, and re-layouts  2.67 us
  transfers between devices with their start and end apart: 19, of which 11 were waited for; matrix products, arithmetic and copies ran while one was open for 3% of the time, Pallas kernels for 37%

profile of v8, /device:TPU:0, one launch (start us, length us, event | category | flops | bytes accessed | tf_op | source)
XLA Modules:
  0.0 93.5 jit_solution(9475365529122303710)
XLA Ops:
  1.8 1.5 %shard_map.122 = (f32[64,64,128]{2,1,0:T(8,128)S(1)}, f32[64,16,128]{2,1,0:T(8,128)S(1)}) custom-call(s32[8,128]{1,0:T(8,128)S(1)} %broadcast_in_dim.4.place, bf16[256,128,128]{2,1,0:T(8,128)(2,1)} %bitcast.21), custom_call_target="tpu_custom_call" | custom-call | tf_op jit(solution)/shard_map/pallas_call | solution.py:450
  3.9 2.1 %collective-permute-start.1 = (f32[64,16,128]{2,1,0:T(8,128)S(1)}, f32[64,16,128]{2,1,0:T(8,128)S(1)}, u32[]{:S(2)}, u32[]{:S(2)}) collective-permute-start(f32[64,16,128]{2,1,0:T(8,128)S(1)} %add.13), channel_id=1, source_target_pairs={{0,2},{1,3},{2,0},{3,1},{4,6},{5,7},{6,4},{7,5},{8,10},{9,11},{10,... | collective-permute-start | bytes 1572872 | tf_op jit(solution)/shard_map/ppermute | solution.py:658
  6.0 1.9 %collective-permute-done.2.refs_0_ = f32[64,64,128]{2,1,0:T(8,128)S(1)} collective-permute-done((f32[64,64,128]{2,1,0:T(8,128)S(1)}, f32[64,64,128]{2,1,0:T(8,128)S(1)}, u32[]{:S(2)}, u32[]{:S(2)}) %collective-permute-start.2) | collective-permute-done | bytes 2097184 | tf_op jit(solution)/shard_map/ppermute | solution.py:655
  7.8 4.0 %shard_map.123 = (f32[4,960,128]{2,1,0:T(8,128)}, f32[16,32,128]{2,1,0:T(8,128)S(1)}) custom-call(s32[8,128]{1,0:T(8,128)S(1)} %broadcast_in_dim.4.place, bf16[256,128,128]{2,1,0:T(8,128)(2,1)} %bitcast.22, f32[64,64,128]{2,1,0:T(8,128)S(1)} %collective-permute-done.2.refs_0_, bf16[64,192]{1,0:T(8,128)(2,1)S(1)} %copy-done.6, bf16[1536,512]{1,0:T(8,128)(2,1)S(1)} %copy-done.1), custom_call_target="tpu_custom_call" | custom-call | tf_op jit(solution)/shard_map/pallas_call | solution.py:450
  11.8 1.9 %shard_map.124 = (f32[64,16,128]{2,1,0:T(8,128)S(1)}, f32[64,16,128]{2,1,0:T(8,128)S(1)}, f32[64,16,128]{2,1,0:T(8,128)S(1)}, f32[64,32,128]{2,1,0:T(8,128)S(1)}...) custom-call(s32[8,128]{1,0:T(8,128)S(1)} %broadcast_in_dim.4.place, ...), custom_call_target="tpu_custom_call" | custom-call | tf_op jit(solution)/shard_map/pallas_call | solution.py:450
  13.9 2.0 %collective-permute-start.16 = (f32[4,960,128]{2,1,0:T(8,128)}, f32[4,960,128]{2,1,0:T(8,128)}, u32[]{:S(2)}, u32[]{:S(2)}) collective-permute-start(f32[4,960,128]{2,1,0:T(8,128)} %get-tuple-element.49), channel_id=1, source_target_pairs={{0,2},{1,3},{2,0},{3,1},{4,6},{5,7},{6,4},{7,5},{8,10},{9,11},{10,... | collective-permute-start | bytes 5898248 | tf_op jit(solution)/shard_map/ppermute | solution.py:658
  16.5 2.2 %collective-permute-done.1.early_ref = f32[64,16,128]{2,1,0:T(8,128)S(1)} collective-permute-done((f32[64,16,128]{2,1,0:T(8,128)S(1)}, f32[64,16,128]{2,1,0:T(8,128)S(1)}, u32[]{:S(2)}, u32[]{:S(2)}) %collective-permute-start.1) | collective-permute-done | bytes 524320 | tf_op jit(solution)/shard_map/ppermute | solution.py:658
  19.7 3.4 %shard_map.126 = (f32[2,960,128]{2,1,0:T(8,128)}, f32[16,32,128]{2,1,0:T(8,128)S(1)}) custom-call(s32[8,128]{1,0:T(8,128)S(1)} %broadcast_in_dim.4.place, bf16[256,128,128]{2,1,0:T(8,128)(2,1)} %bitcast.24, f32[64,16,128]{2,1,0:T(8,128)S(1)} %collective-permute-done.7.refs_0_, ...), custom_call_target="tpu_custom_call", output_to_operand_aliasing={{1}: (7, {})} | custom-call | tf_op jit(solution)/shard_map/pallas_call | solution.py:450
  23.1 2.1 %collective-permute-start.14 = (f32[2,960,128]{2,1,0:T(8,128)}, f32[2,960,128]{2,1,0:T(8,128)}, u32[]{:S(2)}, u32[]{:S(2)}) collective-permute-start(f32[2,960,128]{2,1,0:T(8,128)} %get-tuple-element.68), channel_id=1, source_target_pairs={{0,2},{1,3},{2,0},{3,1},{4,6},{5,7},{6,4},{7,5},{8,10},{9,11},{10,... | collective-permute-start | bytes 2949128 | tf_op jit(solution)/shard_map/ppermute | solution.py:658
  25.2 2.5 %collective-permute-start.10 = (f32[16,32,128]{2,1,0:T(8,128)S(1)}, f32[16,32,128]{2,1,0:T(8,128)S(1)}, u32[]{:S(2)}, u32[]{:S(2)}) collective-permute-start(f32[16,32,128]{2,1,0:T(8,128)S(1)} %get-tuple-element.62), channel_id=1, source_target_pairs={{0,66},{1,67},{2,64},{3,65},{4,70},{5,71},{6,68},{7,69},{8,74},{9,... | collective-permute-start | bytes 786440 | tf_op jit(solution)/shard_map/ppermute | solution.py:679
  27.8 5.5 %shard_map.125 = (f32[64,128,128]{2,1,0:T(8,128)}, f32[16,32,128]{2,1,0:T(8,128)S(1)}) custom-call(s32[8,128]{1,0:T(8,128)S(1)} %broadcast_in_dim.4.place, f32[64,128,128]{2,1,0:T(8,128)} %bitcast.28, bf16[256,128,128]{2,1,0:T(8,128)(2,1)} %bitcast.25, f32[64,16,128]{2,1,0:T(8,128)S(1)} %collective-permute-done.1.early_ref, ...), custom_call_target="tpu_custom_call" | custom-call | tf_op jit(solution)/shard_map/pallas_call | solution.py:450
  35.2 7.1 %all-to-all-start = ((f32[16,32,128]{2,1,0:T(8,128)}), f32[16,32,128]{2,1,0:T(8,128)}, u32[]{:S(2)}, u32[]{:S(2)}) async-start(f32[16,32,128]{2,1,0:T(8,128)} %add.14), calls=%async_computation | async-start | bytes 524288 | tf_op jit(solution)/shard_map/all_to_all | solution.py:684
  43.6 5.2 %shard_map.127 = (f32[64,128,128]{2,1,0:T(8,128)}, f32[64,16,128]{2,1,0:T(8,128)S(1)}, f32[480,128]{1,0:T(8,128)S(1)}, f32[48,8,128]{2,1,0:T(8,128)S(1)}, f32[16,8,128]{2,1,0:T(8,128)S(1)}) custom-call(s32[8,128]{1,0:T(8,128)S(1)} %broadcast_in_dim.4.place, f32[64,128,128]{2,1,0:T(8,128)} %get-tuple-element.63.cells_ref, ...), custom_call_target="tpu_custom_call", output_to_operand_aliasing={{0}: (1, {})} | custom-call | tf_op jit(solution)/shard_map/pallas_call | solution.py:450
  51.8 4.3 %collective-permute-start.15 = (f32[32,128]{1,0:T(8,128)S(1)}, f32[32,128]{1,0:T(8,128)S(1)}, u32[]{:S(2)}, u32[]{:S(2)}) collective-permute-start(f32[32,128]{1,0:T(8,128)S(1)} %reduce_sum.9), channel_id=1, source_target_pairs={{0,112},{1,113},{2,114},{3,115},{4,116},{5,117},{6,118},{7,119},{8... | collective-permute-start | bytes 49160 | tf_op jit(solution)/shard_map/ppermute | solution.py:688
  56.1 3.2 %collective-permute-done.15 = f32[32,128]{1,0:T(8,128)S(1)} collective-permute-done((f32[32,128]{1,0:T(8,128)S(1)}, f32[32,128]{1,0:T(8,128)S(1)}, u32[]{:S(2)}, u32[]{:S(2)}) %collective-permute-start.15) | collective-permute-done | bytes 16416 | tf_op jit(solution)/shard_map/ppermute | solution.py:688
  59.3 1.9 %collective-permute-done.16.pay_ref = f32[4,960,128]{2,1,0:T(8,128)} collective-permute-done((f32[4,960,128]{2,1,0:T(8,128)}, f32[4,960,128]{2,1,0:T(8,128)}, u32[]{:S(2)}, u32[]{:S(2)}) %collective-permute-start.16) | collective-permute-done | bytes 1966112 | tf_op jit(solution)/shard_map/ppermute | solution.py:658
  62.0 7.1 %all-to-all-start.1 = ((f32[16,32,128]{2,1,0:T(8,128)}), f32[16,32,128]{2,1,0:T(8,128)S(1)}, u32[]{:S(2)}, u32[]{:S(2)}) async-start(f32[16,32,128]{2,1,0:T(8,128)} %broadcast_in_dim.10), calls=%async_computation.1 | async-start | bytes 524288 | tf_op jit(solution)/shard_map/all_to_all | solution.py:691
  69.1 2.0 %collective-permute-start.13 = (f32[480,128]{1,0:T(8,128)}, f32[480,128]{1,0:T(8,128)S(1)}, u32[]{:S(2)}, u32[]{:S(2)}) collective-permute-start(f32[480,128]{1,0:T(8,128)} %copy-done.9), channel_id=1, source_target_pairs={{0,2},{1,3},{2,0},{3,1},{4,6},{5,7},{6,4},{7,5},{8,10},{9,11},{10,... | collective-permute-start | bytes 737288 | tf_op jit(solution)/shard_map/ppermute | solution.py:658
  71.3 1.9 %collective-permute-start.11 = (f32[16,8,128]{2,1,0:T(8,128)S(1)}, f32[16,8,128]{2,1,0:T(8,128)S(1)}, u32[]{:S(2)}, u32[]{:S(2)}) collective-permute-start(f32[16,8,128]{2,1,0:T(8,128)S(1)} %get-tuple-element.65), channel_id=1, source_target_pairs={{0,2},{1,3},{2,0},{3,1},{4,6},{5,7},{6,4},{7,5},{8,10},{9,11},{10,... | collective-permute-start | bytes 196616 | tf_op jit(solution)/shard_map/ppermute | solution.py:658
  73.2 4.7 %shard_map.128.base_ref = f32[64,128,128]{2,1,0:T(8,128)} custom-call(f32[4,960,128]{2,1,0:T(8,128)} %collective-permute-done.16.pay_ref, bf16[64,192]{1,0:T(8,128)(2,1)S(1)} %copy-done.5, bf16[1152,512]{1,0:T(8,128)(2,1)S(1)} %copy-done, f32[64,128,128]{2,1,0:T(8,128)} %get-tuple-element.71.base_ref), custom_call_target="tpu_custom_call", output_to_operand_aliasing={{}: (3, {})} | custom-call | tf_op jit(solution)/shard_map/pallas_call | solution.py:450
  77.9 3.5 %shard_map.129 = f32[64,128,128]{2,1,0:T(8,128)} custom-call(s32[8,128]{1,0:T(8,128)S(1)} %broadcast_in_dim.4.place, f32[16,32,128]{2,1,0:T(8,128)S(1)} %all-to-all-done.1.band_ref, bf16[64,48]{1,0:T(8,128)(2,1)S(1)} %copy-done.7, bf16[384,512]{1,0:T(8,128)(2,1)S(1)} %copy-done.2), custom_call_target="tpu_custom_call" | custom-call | tf_op jit(solution)/shard_map/pallas_call | solution.py:450
  82.3 3.3 %shard_map.130.base_ref = f32[64,128,128]{2,1,0:T(8,128)} custom-call(f32[2,960,128]{2,1,0:T(8,128)} %collective-permute-done.14.pay_ref, bf16[64,192]{1,0:T(8,128)(2,1)S(1)} %copy-done.5, bf16[1152,512]{1,0:T(8,128)(2,1)S(1)} %copy-done, f32[64,128,128]{2,1,0:T(8,128)} %shard_map.128.base_ref), custom_call_target="tpu_custom_call", output_to_operand_aliasing={{}: (3, {})} | custom-call | tf_op jit(solution)/shard_map/pallas_call | solution.py:450
  85.6 1.9 %collective-permute-done.13.half_ref = f32[480,128]{1,0:T(8,128)S(1)} collective-permute-done((f32[480,128]{1,0:T(8,128)}, f32[480,128]{1,0:T(8,128)S(1)}, u32[]{:S(2)}, u32[]{:S(2)}) %collective-permute-start.13) | collective-permute-done | bytes 245792 | tf_op jit(solution)/shard_map/ppermute | solution.py:658
  88.7 3.0 %collective-permute-done.12.there_ref = f32[48,8,128]{2,1,0:T(8,128)S(1)} collective-permute-done((f32[48,8,128]{2,1,0:T(8,128)}, f32[48,8,128]{2,1,0:T(8,128)S(1)}, u32[]{:S(2)}, u32[]{:S(2)}) %collective-permute-start.12) | collective-permute-done | bytes 196640 | tf_op jit(solution)/shard_map/ppermute | solution.py:658
  (55 shorter events, 14.4 us)
Async XLA Ops:
  1.7 2.0 %collective-permute-start = (f32[64,16,128]{2,1,0:T(8,128)S(1)}, f32[64,16,128]{2,1,0:T(8,128)S(1)}, u32[]{:S(2)}, u32[]{:S(2)}) collective-permute-start(f32[64,16,128]{2,1,0:T(8,128)S(1)} %dynamic-slice_convert_fusion), channel_id=1, source_target_pairs={{0,1},{1,0},{2,3},{3,2},{4,5},{5,4},{6,7},{7,6},{8,9},{9,8},{10,11... | collective-permute-start | bytes 1572872 | tf_op jit(solution)/shard_map/ppermute | solution.py:655
  3.7 4.2 %collective-permute-start.2 = (f32[64,64,128]{2,1,0:T(8,128)S(1)}, f32[64,64,128]{2,1,0:T(8,128)S(1)}, u32[]{:S(2)}, u32[]{:S(2)}) collective-permute-start(f32[64,64,128]{2,1,0:T(8,128)S(1)} %get-tuple-element.48), channel_id=1, source_target_pairs={{0,1},{1,0},{2,3},{3,2},{4,5},{5,4},{6,7},{7,6},{8,9},{9,8},{10,11... | collective-permute-start | bytes 6291464 | tf_op jit(solution)/shard_map/ppermute | solution.py:655
  3.9 14.8 %collective-permute-start.1 = (f32[64,16,128]{2,1,0:T(8,128)S(1)}, f32[64,16,128]{2,1,0:T(8,128)S(1)}, u32[]{:S(2)}, u32[]{:S(2)}) collective-permute-start(f32[64,16,128]{2,1,0:T(8,128)S(1)} %add.13), channel_id=1, source_target_pairs={{0,2},{1,3},{2,0},{3,1},{4,6},{5,7},{6,4},{7,5},{8,10},{9,11},{10,... | collective-permute-start | bytes 1572872 | tf_op jit(solution)/shard_map/ppermute | solution.py:658
  13.7 4.9 %collective-permute-start.7 = (f32[64,16,128]{2,1,0:T(8,128)S(1)}, f32[64,16,128]{2,1,0:T(8,128)S(1)}, u32[]{:S(2)}, u32[]{:S(2)}) collective-permute-start(f32[64,16,128]{2,1,0:T(8,128)S(1)} %get-tuple-element.58), channel_id=1, source_target_pairs={{0,1},{1,0},{2,3},{3,2},{4,5},{5,4},{6,7},{7,6},{8,9},{9,8},{10,11... | collective-permute-start | bytes 1572872 | tf_op jit(solution)/shard_map/ppermute | solution.py:655
  13.9 47.3 %collective-permute-start.16 = (f32[4,960,128]{2,1,0:T(8,128)}, f32[4,960,128]{2,1,0:T(8,128)}, u32[]{:S(2)}, u32[]{:S(2)}) collective-permute-start(f32[4,960,128]{2,1,0:T(8,128)} %get-tuple-element.49), channel_id=1, source_target_pairs={{0,2},{1,3},{2,0},{3,1},{4,6},{5,7},{6,4},{7,5},{8,10},{9,11},{10,... | collective-permute-start | bytes 5898248 | tf_op jit(solution)/shard_map/ppermute | solution.py:658
  16.0 3.2 %collective-permute-start.8 = (f32[64,16,128]{2,1,0:T(8,128)S(1)}, f32[64,16,128]{2,1,0:T(8,128)S(1)}, u32[]{:S(2)}, u32[]{:S(2)}) collective-permute-start(f32[64,16,128]{2,1,0:T(8,128)S(1)} %get-tuple-element.59), channel_id=1, source_target_pairs={{0,1},{1,0},{2,3},{3,2},{4,5},{5,4},{6,7},{7,6},{8,9},{9,8},{10,11... | collective-permute-start | bytes 1572872 | tf_op jit(solution)/shard_map/ppermute | solution.py:655
  16.0 3.2 %collective-permute-start.9 = (f32[64,16,128]{2,1,0:T(8,128)S(1)}, f32[64,16,128]{2,1,0:T(8,128)S(1)}, u32[]{:S(2)}, u32[]{:S(2)}) collective-permute-start(f32[64,16,128]{2,1,0:T(8,128)S(1)} %get-tuple-element.60), channel_id=1, source_target_pairs={{0,1},{1,0},{2,3},{3,2},{4,5},{5,4},{6,7},{7,6},{8,9},{9,8},{10,11... | collective-permute-start | bytes 1572872 | tf_op jit(solution)/shard_map/ppermute | solution.py:655
  18.7 4.4 %collective-permute-start.6 = (f32[64,32,128]{2,1,0:T(8,128)S(1)}, f32[64,32,128]{2,1,0:T(8,128)S(1)}, u32[]{:S(2)}, u32[]{:S(2)}) collective-permute-start(f32[64,32,128]{2,1,0:T(8,128)S(1)} %get-tuple-element.56), channel_id=1, source_target_pairs={{0,1},{1,0},{2,3},{3,2},{4,5},{5,4},{6,7},{7,6},{8,9},{9,8},{10,11... | collective-permute-start | bytes 3145736 | tf_op jit(solution)/shard_map/ppermute | solution.py:655
  18.7 6.5 %collective-permute-start.3 = (f32[64,32,128]{2,1,0:T(8,128)S(1)}, f32[64,32,128]{2,1,0:T(8,128)S(1)}, u32[]{:S(2)}, u32[]{:S(2)}) collective-permute-start(f32[64,32,128]{2,1,0:T(8,128)S(1)} %get-tuple-element.53), channel_id=1, source_target_pairs={{0,1},{1,0},{2,3},{3,2},{4,5},{5,4},{6,7},{7,6},{8,9},{9,8},{10,11... | collective-permute-start | bytes 3145736 | tf_op jit(solution)/shard_map/ppermute | solution.py:655
  19.2 8.6 %collective-permute-start.4 = (f32[64,32,128]{2,1,0:T(8,128)S(1)}, f32[64,32,128]{2,1,0:T(8,128)S(1)}, u32[]{:S(2)}, u32[]{:S(2)}) collective-permute-start(f32[64,32,128]{2,1,0:T(8,128)S(1)} %get-tuple-element.54), channel_id=1, source_target_pairs={{0,1},{1,0},{2,3},{3,2},{4,5},{5,4},{6,7},{7,6},{8,9},{9,8},{10,11... | collective-permute-start | bytes 3145736 | tf_op jit(solution)/shard_map/ppermute | solution.py:655
  19.3 8.5 %collective-permute-start.5 = (f32[64,32,128]{2,1,0:T(8,128)S(1)}, f32[64,32,128]{2,1,0:T(8,128)S(1)}, u32[]{:S(2)}, u32[]{:S(2)}) collective-permute-start(f32[64,32,128]{2,1,0:T(8,128)S(1)} %get-tuple-element.55), channel_id=1, source_target_pairs={{0,1},{1,0},{2,3},{3,2},{4,5},{5,4},{6,7},{7,6},{8,9},{9,8},{10,11... | collective-permute-start | bytes 3145736 | tf_op jit(solution)/shard_map/ppermute | solution.py:655
  19.7 8.1 %copy-start.8 = (bf16[16,192]{1,0:T(8,128)(2,1)S(1)}, bf16[16,192]{1,0:T(8,128)(2,1)}, u32[]{:S(2)}) copy-start(bf16[16,192]{1,0:T(8,128)(2,1)} %constant.34.clone.refs_4_) | copy-start | bytes 18436
  23.1 59.2 %collective-permute-start.14 = (f32[2,960,128]{2,1,0:T(8,128)}, f32[2,960,128]{2,1,0:T(8,128)}, u32[]{:S(2)}, u32[]{:S(2)}) collective-permute-start(f32[2,960,128]{2,1,0:T(8,128)} %get-tuple-element.68), channel_id=1, source_target_pairs={{0,2},{1,3},{2,0},{3,1},{4,6},{5,7},{6,4},{7,5},{8,10},{9,11},{10,... | collective-permute-start | bytes 2949128 | tf_op jit(solution)/shard_map/ppermute | solution.py:658
  25.2 9.2 %collective-permute-start.10 = (f32[16,32,128]{2,1,0:T(8,128)S(1)}, f32[16,32,128]{2,1,0:T(8,128)S(1)}, u32[]{:S(2)}, u32[]{:S(2)}) collective-permute-start(f32[16,32,128]{2,1,0:T(8,128)S(1)} %get-tuple-element.62), channel_id=1, source_target_pairs={{0,66},{1,67},{2,64},{3,65},{4,70},{5,71},{6,68},{7,69},{8,74},{9,... | collective-permute-start | bytes 786440 | tf_op jit(solution)/shard_map/ppermute | solution.py:679
  27.8 14.5 %copy-start.2 = (bf16[384,512]{1,0:T(8,128)(2,1)S(1)}, bf16[384,512]{1,0:T(8,128)(2,1)}, u32[]{:S(2)}) copy-start(bf16[384,512]{1,0:T(8,128)(2,1)} %constant.40.clone.refs_4_.band_back) | copy-start | bytes 1179652
  27.8 14.5 %copy-start.7 = (bf16[64,48]{1,0:T(8,128)(2,1)S(1)}, bf16[64,48]{1,0:T(8,128)(2,1)}, u32[]{:S(2)}) copy-start(bf16[64,48]{1,0:T(8,128)(2,1)} %constant.35.clone.refs_2_.low_back) | copy-start | bytes 18436
  35.2 15.6 %all-to-all-start = ((f32[16,32,128]{2,1,0:T(8,128)}), f32[16,32,128]{2,1,0:T(8,128)}, u32[]{:S(2)}, u32[]{:S(2)}) async-start(f32[16,32,128]{2,1,0:T(8,128)} %add.14), calls=%async_computation | async-start | bytes 524288 | tf_op jit(solution)/shard_map/all_to_all | solution.py:684
  43.6 29.6 %copy-start = (bf16[1152,512]{1,0:T(8,128)(2,1)S(1)}, bf16[1152,512]{1,0:T(8,128)(2,1)}, u32[]{:S(2)}) copy-start(bf16[1152,512]{1,0:T(8,128)(2,1)} %constant.38.clone.kept_back) | copy-start | bytes 3538948
  43.6 29.6 %copy-start.5 = (bf16[64,192]{1,0:T(8,128)(2,1)S(1)}, bf16[64,192]{1,0:T(8,128)(2,1)}, u32[]{:S(2)}) copy-start(bf16[64,192]{1,0:T(8,128)(2,1)} %constant.33.clone.rows_back) | copy-start | bytes 73732
  51.8 7.5 %collective-permute-start.15 = (f32[32,128]{1,0:T(8,128)S(1)}, f32[32,128]{1,0:T(8,128)S(1)}, u32[]{:S(2)}, u32[]{:S(2)}) collective-permute-start(f32[32,128]{1,0:T(8,128)S(1)} %reduce_sum.9), channel_id=1, source_target_pairs={{0,112},{1,113},{2,114},{3,115},{4,116},{5,117},{6,118},{7,119},{8... | collective-permute-start | bytes 49160 | tf_op jit(solution)/shard_map/ppermute | solution.py:688
  62.0 15.9 %all-to-all-start.1 = ((f32[16,32,128]{2,1,0:T(8,128)}), f32[16,32,128]{2,1,0:T(8,128)S(1)}, u32[]{:S(2)}, u32[]{:S(2)}) async-start(f32[16,32,128]{2,1,0:T(8,128)} %broadcast_in_dim.10), calls=%async_computation.1 | async-start | bytes 524288 | tf_op jit(solution)/shard_map/all_to_all | solution.py:691
  69.1 18.4 %collective-permute-start.13 = (f32[480,128]{1,0:T(8,128)}, f32[480,128]{1,0:T(8,128)S(1)}, u32[]{:S(2)}, u32[]{:S(2)}) collective-permute-start(f32[480,128]{1,0:T(8,128)} %copy-done.9), channel_id=1, source_target_pairs={{0,2},{1,3},{2,0},{3,1},{4,6},{5,7},{6,4},{7,5},{8,10},{9,11},{10,... | collective-permute-start | bytes 737288 | tf_op jit(solution)/shard_map/ppermute | solution.py:658
  71.2 20.5 %collective-permute-start.12 = (f32[48,8,128]{2,1,0:T(8,128)}, f32[48,8,128]{2,1,0:T(8,128)S(1)}, u32[]{:S(2)}, u32[]{:S(2)}) collective-permute-start(f32[48,8,128]{2,1,0:T(8,128)} %copy-done.10), channel_id=1, source_target_pairs={{0,2},{1,3},{2,0},{3,1},{4,6},{5,7},{6,4},{7,5},{8,10},{9,11},{10,... | collective-permute-start | bytes 589832 | tf_op jit(solution)/shard_map/ppermute | solution.py:658
  71.3 21.6 %collective-permute-start.11 = (f32[16,8,128]{2,1,0:T(8,128)S(1)}, f32[16,8,128]{2,1,0:T(8,128)S(1)}, u32[]{:S(2)}, u32[]{:S(2)}) collective-permute-start(f32[16,8,128]{2,1,0:T(8,128)S(1)} %get-tuple-element.65), channel_id=1, source_target_pairs={{0,2},{1,3},{2,0},{3,1},{4,6},{5,7},{6,4},{7,5},{8,10},{9,11},{10,... | collective-permute-start | bytes 196616 | tf_op jit(solution)/shard_map/ppermute | solution.py:658
  (6 other events, 23.0 us)
